TPU v7x, 32 devices: a whole 2x2x4 slice. The times are simulated.
32 devices in a mesh: seq: 16 (over z, y, x), grp: 2 (over core).
Axes of the slice: x: 2, y: 2, z: 4, core: 2. Of those that a mesh axis runs over, the one named last changes fastest.
Arguments:
- tokens: bfloat16 [2, 2048, 768], P('grp', 'seq'), may hold values from -6 to 6
- cotangent: bfloat16 [2, 2048, 768], P('grp', 'seq'), may hold values from -6 to 6
- holes: int32 [2, 2048], P('grp', 'seq'), may hold values 0 or 1
- slide_lengths: int32 [2, 8], P('grp'), may hold values from 1 to 1984, 2048 in all within a row
- master: float32 [2, 3542400], P('grp', 'seq'), may hold values from -2 to 2
- first_moment: float32 [2, 3542400], P('grp', 'seq'), may hold values from -32 to 32
- second_moment: float32 [2, 3542400], P('grp', 'seq'), may hold values from 2.048 to 2048
Outputs:
- output: bfloat16 [2, 2048, 768], P('grp', 'seq')
- input_grad: float32 [2, 2048, 768], P('grp', 'seq')
- new_moment: float32 [2, 3542400], P('grp', 'seq')
- new_second: float32 [2, 3542400], P('grp', 'seq')
- new_master: float32 [2, 3542400], P('grp', 'seq')
All inputs are finite; a program needn't handle non-finite values. No bound on the sum of `holes` on one device may be relied on, other than what follows from the above.
Results may differ from a plain program's by a relative error of at most 0.018.
Values may be sent and summed in bfloat16 or wider, within the bound.
A program may use at most 128 MiB of HBM per device.

v0:
```python
from functools import partial

import jax
import jax.numpy as jnp
from jax import lax
from jax.sharding import PartitionSpec as P

D = 768
FF = 3072
HEADS = 16
HEAD = 48
STEP = 10


EPS_NORM = 1e-05
EPS_ADAM = 1e-08
BETA_ONE = 0.9
BETA_TWO = 0.95


def as_sent(array):
    return jax.tree.map(lambda a: a.astype(jnp.bfloat16) if a.dtype == jnp.float32 else a, array)


def bounds():
    qkv_edge = 3 * D * D // 2
    out_edge = qkv_edge + D * D // 2
    up_edge = out_edge + D * FF // 2
    down_edge = up_edge + FF * D // 2
    gain_edge = down_edge + D
    return (qkv_edge, out_edge, up_edge, down_edge, gain_edge)


def per_segment(flat_index, values):
    edge_list = bounds()
    result = jnp.full(flat_index.shape, values[5], jnp.float32)
    for position in range(4, -1, -1):
        result = jnp.where(flat_index < edge_list[position], jnp.float32(values[position]), result)
    return result


def unpack(flat):
    edge_list = bounds()
    total = flat.shape[1]

    def joined(start, stop, shape):
        return jnp.concatenate(
            [flat[0, start:stop].reshape(shape), flat[1, start:stop].reshape(shape)], axis=-1
        )

    w_qkv = joined(0, edge_list[0], (D, 3 * D // 2))
    w_out = joined(edge_list[0], edge_list[1], (D, D // 2))
    w_up = joined(edge_list[1], edge_list[2], (D, FF // 2))
    w_down = joined(edge_list[2], edge_list[3], (FF, D // 2))
    gain_rows = joined(edge_list[3], edge_list[4], (2, D // 2))
    shift_rows = joined(edge_list[4], edge_list[4] + 3 * D // 2, (3, D // 2))
    bias_up = joined(edge_list[4] + 3 * D // 2, total, (FF // 2,))
    return (w_qkv, w_out, w_up, w_down, gain_rows, shift_rows, bias_up)


def normalize(values):
    centered = values - jnp.mean(values, axis=-1, keepdims=True)
    inverse = lax.rsqrt(jnp.mean(centered * centered, axis=-1, keepdims=True) + EPS_NORM)
    return (centered * inverse, inverse)


def norm_back(grad_hat, normed_hat, inverse):
    return inverse * (
        grad_hat
        - jnp.mean(grad_hat, axis=-1, keepdims=True)
        - normed_hat * jnp.mean(grad_hat * normed_hat, axis=-1, keepdims=True)
    )


def contract_rows(left, right):
    return lax.dot_general(
        left, right, (((0,), (0,)), ((), ())), preferred_element_type=jnp.float32
    )


def contract_cols(left, right):
    return lax.dot_general(
        left, right, (((1,), (1,)), ((), ())), preferred_element_type=jnp.float32
    )


def slide_index(positions, slide_ends):
    return jnp.sum((positions[:, None] >= slide_ends[None, :]).astype(jnp.int32), axis=1)


def split_heads(block_rows):
    return block_rows.reshape(block_rows.shape[0], HEADS, HEAD).transpose(1, 0, 2)


def join_heads(stacked):
    return stacked.transpose(1, 0, 2).reshape(stacked.shape[1], HEADS * HEAD)


def allowance(slides, present):
    token_count = slides.shape[0]
    same_slide = (slides[:, None] == slides[None, :]) & (present[None, :] > 0)
    return same_slide | jnp.eye(token_count, dtype=bool)


def attend(packed, slides, present):
    allowed = allowance(slides, present)
    scale = HEAD ** (-0.5)

    def one_head(pieces):
        query_head, key_head, value_head = pieces
        scores = contract_cols(query_head, key_head) * scale
        scores = jnp.where(allowed, scores, -1000000000.0)
        row_max = jnp.max(scores, axis=-1, keepdims=True)
        exponent = jnp.exp(scores - row_max)
        denominator = jnp.sum(exponent, axis=-1, keepdims=True)
        attention = (exponent / denominator).astype(jnp.bfloat16)
        result = jnp.dot(attention, value_head, preferred_element_type=jnp.float32)
        return (result, (row_max + jnp.log(denominator))[:, 0])

    outs, lses = lax.map(
        one_head,
        (
            split_heads(packed[:, :D]),
            split_heads(packed[:, D : 2 * D]),
            split_heads(packed[:, 2 * D :]),
        ),
    )
    return (join_heads(outs), lses.T)


def attend_back(packed, slides, present, lse_rows, out_grad, lse_grad):
    allowed = allowance(slides, present)
    scale = HEAD ** (-0.5)

    def one_head(pieces):
        query_head, key_head, value_head, lse_head, grad_head, extra_lse = pieces
        scores = contract_cols(query_head, key_head) * scale
        scores = jnp.where(allowed, scores, -1000000000.0)
        attention = jnp.exp(scores - lse_head[:, None])
        prob_grad = contract_cols(grad_head, value_head)
        inner_sum = jnp.sum(attention * prob_grad, axis=-1, keepdims=True)
        score_grad = (attention * (prob_grad - inner_sum + extra_lse[:, None])).astype(jnp.bfloat16)
        query_grad = jnp.dot(score_grad, key_head, preferred_element_type=jnp.float32) * scale
        key_grad = contract_rows(score_grad, query_head) * scale
        value_grad = contract_rows(attention.astype(jnp.bfloat16), grad_head)
        return (query_grad, key_grad, value_grad)

    query_grad, key_grad, value_grad = lax.map(
        one_head,
        (
            split_heads(packed[:, :D]),
            split_heads(packed[:, D : 2 * D]),
            split_heads(packed[:, 2 * D :]),
            lse_rows.T,
            split_heads(out_grad),
            lse_grad.T,
        ),
    )
    return jnp.concatenate(
        [join_heads(query_grad), join_heads(key_grad), join_heads(value_grad)], axis=1
    )


def adam_update(weights, moment, second, gradient, flat_index):
    step_rates = per_segment(
        flat_index,
        (
            0.7 * (2.0 / D) ** 0.5,
            0.7 * (24.0 / D) ** 0.5,
            0.7 * (1.0 / D) ** 0.5,
            0.7 * (1.0 / FF) ** 0.5,
            0.15,
            0.2,
        ),
    )
    decays = per_segment(flat_index, (0.1, 0.1, 0.1, 0.1, 0.0, 0.0))
    new_moment = BETA_ONE * moment + (1.0 - BETA_ONE) * gradient
    new_second = BETA_TWO * second + (1.0 - BETA_TWO) * gradient * gradient
    fix_one = 1.0 - BETA_ONE**STEP
    fix_two = 1.0 - BETA_TWO**STEP
    update = new_moment / fix_one / (jnp.sqrt(new_second / fix_two) + EPS_ADAM)
    return (new_moment, new_second, weights - step_rates * (update + decays * weights))


def column_halves(values):
    return values.reshape(values.shape[0], 2, values.shape[1] // 2)


def on_device(tokens, cotangent, holes, slide_lengths, master, first_moment, second_moment):
    own_half = lax.all_gather(master.astype(jnp.bfloat16), "seq", axis=1, tiled=True)
    whole_flat = lax.all_gather(own_half, "grp", axis=0, tiled=True)
    w_qkv, w_out, w_up, w_down, gain_rows, shift_rows, bias_up = unpack(whole_flat)
    gain_rows = gain_rows.astype(jnp.float32)
    shift_rows = shift_rows.astype(jnp.float32)
    bias_up = bias_up.astype(jnp.float32)
    inputs = tokens[0].astype(jnp.float32)
    row_count = inputs.shape[0]
    seq_ways = lax.axis_size("seq")
    seq_place = lax.axis_index("seq")
    row_steps = jnp.arange(row_count, dtype=jnp.int32)
    slide_ends = jnp.cumsum(slide_lengths[0])
    near_slides = slide_index(seq_place * row_count + row_steps, slide_ends)
    far_slides = slide_index(seq_place + seq_ways * row_steps, slide_ends)
    near_present = holes[0]
    strided_shape = (row_count // seq_ways, seq_ways)

    def to_strided(packed):
        moved, moved_mask = (
            lax.all_to_all(
                packed.reshape(strided_shape + (3 * D,)),
                "seq",
                split_axis=1,
                concat_axis=0,
                tiled=True,
            ),
            lax.all_to_all(
                near_present.astype(jnp.bfloat16).reshape(strided_shape + (1,)),
                "seq",
                split_axis=1,
                concat_axis=0,
                tiled=True,
            ),
        )
        return (moved.reshape(row_count, 3 * D), moved_mask.reshape(row_count).astype(jnp.int32))

    normed_one, inverse_one = normalize(inputs)
    normed = (normed_one * gain_rows[0] + shift_rows[0]).astype(jnp.bfloat16)
    projected = jnp.dot(normed, w_qkv, preferred_element_type=jnp.float32).astype(jnp.bfloat16)
    near_out, near_lse = attend(projected, near_slides, near_present)
    far_proj, far_present = to_strided(projected)
    far_local, far_local_lse = attend(far_proj, far_slides, far_present)
    returned = (
        lax.all_to_all(
            far_local.reshape(row_count, 1, D).astype(jnp.bfloat16),
            "seq",
            split_axis=0,
            concat_axis=1,
            tiled=True,
        ).astype(jnp.float32),
        lax.all_to_all(
            far_local_lse.reshape(row_count, 1, HEADS).astype(jnp.bfloat16),
            "seq",
            split_axis=0,
            concat_axis=1,
            tiled=True,
        ).astype(jnp.float32),
    )
    far_out = returned[0].reshape(row_count, D)
    far_lse = returned[1].reshape(row_count, HEADS)
    near_share = jax.nn.sigmoid(near_lse - far_lse)
    near_heads = near_out.reshape(row_count, HEADS, HEAD)
    far_heads = far_out.reshape(row_count, HEADS, HEAD)
    mixture = (
        (near_share[:, :, None] * near_heads + (1.0 - near_share[:, :, None]) * far_heads)
        .reshape(row_count, D)
        .astype(jnp.bfloat16)
    )
    middle = inputs + jnp.dot(mixture, w_out, preferred_element_type=jnp.float32)
    normed_two, inverse_two = normalize(middle)
    second_in = (normed_two * gain_rows[1] + shift_rows[1]).astype(jnp.bfloat16)
    hidden = jnp.dot(second_in, w_up, preferred_element_type=jnp.float32) + bias_up
    activated = jax.nn.gelu(hidden, approximate=True).astype(jnp.bfloat16)
    output = middle + jnp.dot(activated, w_down, preferred_element_type=jnp.float32) + shift_rows[2]
    upstream = cotangent[0].astype(jnp.float32)
    down_grad = upstream.astype(jnp.bfloat16)
    grad_act = contract_cols(down_grad, w_down)
    gelu_pull = jax.vjp(partial(jax.nn.gelu, approximate=True), hidden)[1]
    hidden_grad = gelu_pull(grad_act)[0].astype(jnp.bfloat16)
    second_grad = contract_cols(hidden_grad, w_up)
    grad_gain_two = jnp.sum(second_grad * normed_two, axis=0)
    grad_shift_two = jnp.sum(second_grad, axis=0)
    middle_grad = upstream + norm_back(second_grad * gain_rows[1], normed_two, inverse_two)
    attend_grad = middle_grad.astype(jnp.bfloat16)
    mix_grad = contract_cols(attend_grad, w_out).reshape(row_count, HEADS, HEAD)
    near_lse_grad = (
        near_share * (1.0 - near_share) * jnp.sum((near_heads - far_heads) * mix_grad, axis=-1)
    )
    near_grad = (near_share[:, :, None] * mix_grad).reshape(row_count, D).astype(jnp.bfloat16)
    far_grad = ((1.0 - near_share[:, :, None]) * mix_grad).reshape(row_count, D)
    sent = (
        lax.all_to_all(
            as_sent(far_grad.reshape(strided_shape + (D,))),
            "seq",
            split_axis=1,
            concat_axis=0,
            tiled=True,
        ),
        lax.all_to_all(
            as_sent((-near_lse_grad).reshape(strided_shape + (HEADS,))),
            "seq",
            split_axis=1,
            concat_axis=0,
            tiled=True,
        ),
    )
    far_back = sent[0].reshape(row_count, D).astype(jnp.bfloat16)
    far_lse_grad = sent[1].reshape(row_count, HEADS)
    again_proj, again_present = to_strided(projected)
    again_lse = attend(again_proj, far_slides, again_present)[1]
    far_proj_grad = attend_back(
        again_proj, far_slides, again_present, again_lse, far_back, far_lse_grad
    ).astype(jnp.bfloat16)
    far_home = lax.all_to_all(
        far_proj_grad.reshape(row_count, 1, 3 * D), "seq", split_axis=0, concat_axis=1, tiled=True
    ).reshape(row_count, 3 * D)
    near_proj_grad = attend_back(
        projected, near_slides, near_present, near_lse, near_grad, near_lse_grad
    )
    proj_grad = (near_proj_grad + far_home.astype(jnp.float32)).astype(jnp.bfloat16)
    first_grad = contract_cols(proj_grad, w_qkv)
    grad_gain_one = jnp.sum(first_grad * normed_one, axis=0)
    grad_shift_one = jnp.sum(first_grad, axis=0)
    input_grad = middle_grad + norm_back(first_grad * gain_rows[0], normed_one, inverse_one)
    both_rows = (
        lax.all_gather(normed, "grp", axis=0, tiled=True),
        lax.all_gather(mixture, "grp", axis=0, tiled=True),
        lax.all_gather(second_in, "grp", axis=0, tiled=True),
        lax.all_gather(activated, "grp", axis=0, tiled=True),
    )
    moved = (
        lax.all_to_all(column_halves(proj_grad), "grp", split_axis=1, concat_axis=0, tiled=True),
        lax.all_to_all(column_halves(attend_grad), "grp", split_axis=1, concat_axis=0, tiled=True),
        lax.all_to_all(column_halves(hidden_grad), "grp", split_axis=1, concat_axis=0, tiled=True),
        lax.all_to_all(column_halves(down_grad), "grp", split_axis=1, concat_axis=0, tiled=True),
    )
    proj_mine = moved[0].reshape(2 * row_count, 3 * D // 2)
    attend_mine = moved[1].reshape(2 * row_count, D // 2)
    hidden_mine = moved[2].reshape(2 * row_count, FF // 2)
    down_mine = moved[3].reshape(2 * row_count, D // 2)
    norm_sums = lax.psum(
        jnp.stack([grad_gain_one, grad_gain_two, grad_shift_one, grad_shift_two]), "grp"
    )
    half_width = D // 2
    norm_half = lax.dynamic_slice_in_dim(
        norm_sums, lax.axis_index("grp") * half_width, half_width, 1
    )
    grad_w_qkv = contract_rows(both_rows[0], proj_mine)
    grad_w_out = contract_rows(both_rows[1], attend_mine)
    grad_w_up = contract_rows(both_rows[2], hidden_mine)
    grad_w_down = contract_rows(both_rows[3], down_mine)
    grad_bias_down = jnp.sum(down_mine.astype(jnp.float32), axis=0)
    grad_bias_up = jnp.sum(hidden_mine.astype(jnp.float32), axis=0)
    gradient = jnp.concatenate(
        [
            grad_w_qkv.reshape(-1),
            grad_w_out.reshape(-1),
            grad_w_up.reshape(-1),
            grad_w_down.reshape(-1),
            norm_half[0],
            norm_half[1],
            norm_half[2],
            norm_half[3],
            grad_bias_down,
            grad_bias_up,
        ]
    )
    reduced = lax.psum_scatter(gradient, "seq", scatter_dimension=0, tiled=True)
    shard_size = master.shape[1]
    flat_index = lax.axis_index("seq") * shard_size + jnp.arange(shard_size, dtype=jnp.int32)
    new_moment, new_second, new_master = adam_update(
        master[0], first_moment[0], second_moment[0], reduced, flat_index
    )
    return (
        output[None].astype(jnp.bfloat16),
        input_grad[None],
        new_moment[None],
        new_second[None],
        new_master[None],
    )


def solution(mesh):
    return jax.shard_map(
        on_device,
        mesh=mesh,
        in_specs=(
            P("grp", "seq", None),
            P("grp", "seq", None),
            P("grp", "seq"),
            P("grp", None),
            P("grp", "seq"),
            P("grp", "seq"),
            P("grp", "seq"),
        ),
        out_specs=(
            P("grp", "seq", None),
            P("grp", "seq", None),
            P("grp", "seq"),
            P("grp", "seq"),
            P("grp", "seq"),
        ),
        check_vma=False,
    )
```

profile of v0, /device:TPU:0, one launch (start us, length us, event | category | flops | bytes accessed | tf_op | source)
XLA Modules:
  0.0 1661.4 jit_solution(5358271662675954129)
XLA Ops:
  7.2 7.5 convert_reduce_fusion.1
  20.2 7.6 dynamic-update-slice
  27.8 232.0 %all-reduce.5.cloned.1.call-done = bf16[3542400]{0:T(1024)(128)(2,1)} async-done(((bf16[3542400]{0:T(1024)(128)(2,1)}), bf16[3542400]{0:T(1024)(128)(2,1)}) %all-reduce.5.cloned.1.call-update) | async-done | bytes 7084816
  259.8 68.6 %reshape.460 = bf16[1,1,3542400]{2,1,0:T(2,128)(2,1)} reshape(bf16[3542400]{0:T(1024)(128)(2,1)} %all-reduce.5.cloned.1.call-done) | data formatting | bytes 14169600
  351.0 22.5 %all-gather.6.cloned.1.call-done = bf16[2,1,3542400]{2,1,0:T(2,128)(2,1)} async-done(((bf16[1,1,3542400]{2,1,0:T(2,128)(2,1)}), bf16[2,1,3542400]{2,1,0:T(2,128)(2,1)}) %all-gather.6.cloned.1.call-update) | async-done | bytes 14169616 | tf_op jit(solution)/shard_map/all_gather | solution.py:191
  373.6 39.2 %copy.425 = bf16[2,1,3542400]{2,0,1:T(2,128)(2,1)S(1)} copy(bf16[2,1,3542400]{2,1,0:T(2,128)(2,1)} %all-gather.6.cloned.1.call-done) | data formatting | bytes 28339200
  412.9 38.4 %slice_reduce_fusion.4 = (bf16[884736]{0:T(1024)(128)(2,1)}, bf16[884736]{0:T(1024)(128)(2,1)S(1)}) fusion(bf16[2,3542400]{1,0:T(2,128)(2,1)S(1)} %bitcast.462), kind=kLoop, calls=%fused_computation.147 | loop fusion | bytes 7077888 | tf_op jit(solution)/shard_map/slice | solution.py:48
  451.2 13.6 slice_reduce_fusion.6
  464.8 56.5 %slice_reduce_fusion = (bf16[1179648]{0:T(1024)(128)(2,1)}, bf16[1179648]{0:T(1024)(128)(2,1)}, bf16[1179648]{0:T(1024)(128)(2,1)}, bf16[1179648]{0:T(1024)(128)(2,1)}) fusion(bf16[2,3542400]{1,0:T(2,128)(2,1)} %bitcast.464), kind=kLoop, calls=%fused_computation.140 | loop fusion | bytes 18874368 | tf_op jit(solution)/shard_map/slice | solution.py:48
  538.3 6.8 all-to-all-start
  557.0 60.1 %while.67 = (s32[]{:T(128)}, f32[16,128,48]{1,2,0:T(8,128)}, f32[16,128]{1,0:T(8,128)S(1)}, bf16[16,128,48]{2,1,0:T(8,128)(2,1)}, bf16[16,128,48]{2,1,0:T(8,128)...) while((s32[]{:T(128)}, f32[16,128,48]{1,2,0:T(8,128)}, ...), condition=%wide.region_7.8_spmd.clone, body=%wide.region_4.0_spmd.clone.sunk | while | flops 3342210 | bytes 328297 | solution.py:120
  623.3 5.6 reshape_squeeze.44
  638.5 5.6 reshape_squeeze.45
  644.1 5.0 reshape_squeeze.46
  649.1 5.0 reshape_squeeze.47
  674.8 60.0 %while.68 = (s32[]{:T(128)}, bf16[16,128,48]{1,2,0:T(8,128)(2,1)}, bf16[16,128]{1,0:T(8,128)(2,1)S(1)}, bf16[16,128,48]{2,1,0:T(8,128)(2,1)}, bf16[16,128,48]{2,...) while((s32[]{:T(128)}, bf16[16,128,48]{1,2,0:T(8,128)(2,1)}, ...), condition=%wide.region_12.13_spmd.clone, body=%wide.region_9.12_spmd.clone.sunk | while | flops 3342338 | bytes 327529 | solution.py:120
  735.5 7.1 all-to-all-start.2
  743.2 44.9 %while.70 = (s32[]{:T(128)}, f32[16,128]{1,0:T(8,128)}, bf16[16,128,48]{2,1,0:T(8,128)(2,1)}, bf16[16,128,48]{2,1,0:T(8,128)(2,1)}, s32[128]{0:T(128)}, /*index=5*/pred[128]{0:T(512)(128)(4,1)}, s32[]{:T(128)}, s32[]{:T(128)}) while((s32[]{:T(128)}, f32[16,128]{1,0:T(8,128)}, bf16[16,128,48]{2,1,0:T(8,128)(2,1)}, ...), condition=%wide.region_24.25_spmd.clone, body=%wide.region_21.24_spmd.clone.sunk | while | flops 1720194 | bytes 203353 | solution.py:120
  794.4 7.0 all-to-all-start.3
  858.4 6.9 all-to-all-start.5
  879.8 114.4 %while.69 = (s32[]{:T(128)}, f32[16,128,48]{1,2,0:T(8,128)}, f32[16,128,48]{1,2,0:T(8,128)}, f32[16,128,48]{1,2,0:T(8,128)}, bf16[16,128,48]{2,1,0:T(8,128)(2,1)...) while((s32[]{:T(128)}, f32[16,128,48]{1,2,0:T(8,128)}, ...), condition=%wide.region_20.21_spmd.clone, body=%wide.region_18.20_spmd.clone.sunk | while | flops 8105858 | bytes 764545 | solution.py:148
  1012.4 116.4 %while.71 = (s32[]{:T(128)}, bf16[16,128,48]{1,2,0:T(8,128)(2,1)}, bf16[16,128,48]{1,2,0:T(8,128)(2,1)}, bf16[16,128,48]{1,2,0:T(8,128)(2,1)}, bf16[16,128,48]{2...) while((s32[]{:T(128)}, bf16[16,128,48]{1,2,0:T(8,128)(2,1)}, ...), condition=%wide.region_27.28_spmd.clone, body=%wide.region_25.27_spmd.clone.sunk | while | flops 8105986 | bytes 805253 | solution.py:148
  1138.2 5.7 all_to_all.151
  1143.9 6.9 all-to-all-start.6
  1155.1 5.6 reshape.444
  1220.6 6.2 reshape.447
  1239.8 9.1 reduce.30
  1249.6 10.4 multiply_reduce_fusion.2
  1265.2 372.3 %all-reduce.7.cloned.1.call-done = f32[3542400]{0:T(1024)} async-done(((f32[3542400]{0:T(1024)}), f32[3542400]{0:T(1024)}) %all-reduce.7.cloned.1.call-update) | async-done | bytes 14169616
  1639.8 5.1 broadcast_in_dim.128
  1644.9 4.9 broadcast_in_dim.129
  1649.8 4.9 broadcast_in_dim.137
  (748 shorter events, 679.1 us)
Async XLA Ops:
  7.2 252.7 %all-reduce.5.cloned.1.call-start = ((), (), s32[]{:S(2)}) async-start(), calls=%async_computation.12 | async-start | bytes 14172160
  27.8 345.8 %all-gather.6.cloned.1.call-start = ((), (), s32[]{:S(2)}) async-start(), calls=%async_computation.13 | async-start | bytes 42508800 | tf_op jit(solution)/shard_map/all_gather | solution.py:191
  328.5 7.3 copy-start.44
  328.5 7.5 copy-start.45
  329.4 8.7 copy-start.5
  330.2 8.0 all-to-all-start.10
  338.2 12.1 all-to-all-start.1
  412.8 38.4 %copy-start = (bf16[2,1,3542400]{2,0,1:T(2,128)(2,1)}, bf16[2,1,3542400]{2,0,1:T(2,128)(2,1)S(1)}, u32[]{:S(2)}) copy-start(bf16[2,1,3542400]{2,0,1:T(2,128)(2,1)S(1)} %copy.425) | copy-start | bytes 42508804
  538.3 123.6 %all-to-all-start = ((bf16[8,16,2304]{2,0,1:T(8,128)(2,1)}), bf16[8,16,2304]{2,0,1:T(8,128)(2,1)}, u32[]{:S(2)}, u32[]{:S(2)}) async-start(bf16[8,16,2304]{2,0,1:T(8,128)(2,1)} %copy.359), calls=%async_computation | async-start | bytes 1179648 | tf_op jit(solution)/shard_map/all_to_all | solution.py:209
  617.1 11.8 copy-start.23
  628.9 4.3 copy-start.27
  628.9 4.9 copy-start.14
  661.8 13.0 copy-start.29
  735.5 58.9 %all-to-all-start.2 = ((bf16[128,1,16]{2,1,0:T(2,128)(2,1)}), bf16[128,1,16]{2,1,0:T(2,128)(2,1)}, u32[]{:S(2)}, u32[]{:S(2)}) async-start(bf16[128,1,16]{2,1,0:T(2,128)(2,1)} %copy.369), calls=%async_computation.2 | async-start | bytes 131072 | tf_op jit(solution)/shard_map/all_to_all | solution.py:240
  794.4 22.3 %all-to-all-start.3 = ((bf16[16,2,3072]{2,1,0:T(2,128)(2,1)}), bf16[16,2,3072]{2,1,0:T(2,128)(2,1)}, u32[]{:S(2)}, u32[]{:S(2)}) async-start(bf16[16,2,3072]{2,1,0:T(2,128)(2,1)} %reshape.501), calls=%async_computation.3 | async-start | bytes 393216 | tf_op jit(solution)/shard_map/all_to_all | solution.py:233
  830.3 11.8 copy-start.1
  830.7 4.7 copy-start.22
  830.7 4.7 copy-start.21
  830.7 9.0 slice-start
  835.3 4.4 slice-start.1
  858.4 14.4 all-to-all-start.5
  872.8 130.7 %all-to-all-start.4 = ((bf16[8,16,768]{2,0,1:T(8,128)(2,1)}), bf16[8,16,768]{2,0,1:T(8,128)(2,1)}, u32[]{:S(2)}, u32[]{:S(2)}) async-start(bf16[8,16,768]{2,0,1:T(8,128)(2,1)} %copy.392), calls=%async_computation.4 | async-start | bytes 393216 | tf_op jit(solution)/shard_map/all_to_all | solution.py:281
  879.0 115.2 %copy-start.25 = (f32[768]{0:T(1024)S(1)}, f32[768]{0:T(1024)}, u32[]{:S(2)}) copy-start(f32[768]{0:T(1024)} %get-tuple-element.685) | copy-start | bytes 9220
  879.0 115.7 %copy-start.24 = (f32[768]{0:T(1024)S(1)}, f32[768]{0:T(1024)}, u32[]{:S(2)}) copy-start(f32[768]{0:T(1024)} %get-tuple-element.692) | copy-start | bytes 9220
  1003.5 134.7 %all-to-all-start.9 = ((bf16[128,2,1536]{2,0,1:T(8,128)(2,1)}), bf16[128,2,1536]{2,0,1:T(8,128)(2,1)}, u32[]{:S(2)}, u32[]{:S(2)}) async-start(bf16[128,2,1536]{2,0,1:T(8,128)(2,1)} %bitcast.480), calls=%async_computation.9 | async-start | bytes 1572864 | tf_op jit(solution)/shard_map/all_to_all | solution.py:323
  1143.9 30.2 %all-to-all-start.6 = ((bf16[16,2,9216]{2,1,0:T(2,128)(2,1)}), bf16[16,2,9216]{2,1,0:T(2,128)(2,1)}, u32[]{:S(2)}, u32[]{:S(2)}) async-start(bf16[16,2,9216]{2,1,0:T(2,128)(2,1)} %reshape.503), calls=%async_computation.6 | async-start | bytes 1179648 | tf_op jit(solution)/shard_map/all_to_all | solution.py:303
  1150.8 65.3 %all-gather.4.cloned.1.call-start = ((), (), s32[]{:S(2)}) async-start(), calls=%async_computation.11 | async-start | bytes 2359296 | tf_op jit(solution)/shard_map/all_gather | solution.py:318
  1172.7 464.7 %all-reduce.7.cloned.1.call-start = ((), (), s32[]{:S(2)}) async-start(), calls=%async_computation.14 | async-start | bytes 28344320
  1183.3 6.0 copy-start.16
  1226.8 9.3 copy-start.36
  1239.8 20.1 %copy-start.2 = (f32[128,768]{1,0:T(8,128)S(1)}, f32[128,768]{1,0:T(8,128)}, u32[]{:S(2)}) copy-start(f32[128,768]{1,0:T(8,128)} %copy-done.1) | copy-start | bytes 1179652
  1239.8 20.1 %copy-start.30 = (f32[768]{0:T(1024)S(1)}, f32[768]{0:T(1024)}, u32[]{:S(2)}) copy-start(f32[768]{0:T(1024)} %get-tuple-element.697) | copy-start | bytes 9220
  (29 other events, 84.0 us)
Sparse Core Ops, SparseCore 0:
  27.9 231.8 all-reduce.4
  328.6 44.8 all-gather.5
  1172.8 11.0 all-gather.3
  1238.8 398.5 all-reduce.6
where the time goes:
time: 1690 us; the launch traced here: 1660 us
  waiting for transfers between devices  633 us (37%)
  local copies, waits for them, and re-layouts  505 us (30%)
  matrix products  342 us (20%)
  other arithmetic  90.9 us (5%)
  starting transfers between devices  52.5 us (3%)
  blocking collectives  21.4 us (1%)
    unnamed x6, waiting for transfers between devices  604 us
    unnamed x132, local copies, waits for them, and re-layouts  184 us
    dot_general x116, matrix products, contract_cols(): lax.dot_general(left, right, (((1,), (1,)), ((), ())), preferred_element_...  119 us
    dot_general x68, matrix products, contract_rows(): lax.dot_general(left, right, (((0,), (0,)), ((), ())), preferred_element_...  112 us
    slice x3, local copies, waits for them, and re-layouts, joined(): flat[1, start:stop].reshape(shape)  108 us
    dot_general x32, matrix products, one_head(): result = jnp.dot(attention, value_head, preferred_element_type=jnp.float32)  49.8 us
    dot_general x32, matrix products, one_head(): jnp.dot(score_grad, key_head, preferred_element_type=jnp.float32) * scale  49.7 us
    dynamic_update_slice x48, local copies, waits for them, and re-layouts, attend(): lax.map(one_head, (split_heads(packed[:, :D]), split_heads(packed[:, D:2...  41.8 us
  transfers between devices with their start and end apart: 13, of which 5 were waited for; matrix products, arithmetic and copies ran while one was open for 32% of the time, Pallas kernels for 0%

commit v1 on v0

--- a/solution.py
+++ b/solution.py
@@ -3,6 +3,8 @@
 import jax
 import jax.numpy as jnp
 from jax import lax
+from jax.experimental import pallas as pl
+from jax.experimental.pallas import tpu as pltpu
 from jax.sharding import PartitionSpec as P
 
 D = 768
@@ -186,7 +188,7 @@
     return values.reshape(values.shape[0], 2, values.shape[1] // 2)
 
 
-def on_device(tokens, cotangent, holes, slide_lengths, master, first_moment, second_moment):
+def plain_on_device(tokens, cotangent, holes, slide_lengths, master, first_moment, second_moment):
     own_half = lax.all_gather(master.astype(jnp.bfloat16), "seq", axis=1, tiled=True)
     whole_flat = lax.all_gather(own_half, "grp", axis=0, tiled=True)
     w_qkv, w_out, w_up, w_down, gain_rows, shift_rows, bias_up = unpack(whole_flat)
@@ -369,9 +371,1008 @@
     )
 
 
+LANES = 128
+BF16 = jnp.bfloat16
+F32 = jnp.float32
+MAT_ROWS = (3 * D * D + D * D + D * FF + FF * D) // 2 // LANES
+SMALL_ROWS = 32
+UNIT = 576
+PAIR = 2
+TILES = (3 * D // 2 // LANES, D // 2 // LANES, FF // 2 // LANES, D // 2 // LANES)
+DEPTHS = (D, D, D, FF)
+MESH = pl.DeviceIdType.MESH
+VMEM_BYTES = 60 * 2**20
+NEG = -1000000000.0
+
+
+def matrix_starts():
+    starts = [0]
+    for tiles, depth in zip(TILES, DEPTHS):
+        starts.append(starts[-1] + tiles * depth)
+    return starts
+
+
+def place():
+    return lax.axis_index("seq"), lax.axis_index("grp")
+
+
+def enter(ways):
+    s, g = place()
+    barrier = pltpu.get_barrier_semaphore()
+
+    def greet(step, carry):
+        pl.semaphore_signal(
+            barrier, inc=1, device_id=(lax.rem(s + step, ways), g), device_id_type=MESH
+        )
+        return carry
+
+    lax.fori_loop(1, ways, greet, 0)
+    pl.semaphore_signal(barrier, inc=1, device_id=(s, 1 - g), device_id_type=MESH)
+    pl.semaphore_wait(barrier, ways)
+
+
+def remote(src, dst, send_sem, recv_sem, to):
+    return pltpu.make_async_remote_copy(
+        src_ref=src,
+        dst_ref=dst,
+        send_sem=send_sem,
+        recv_sem=recv_sem,
+        device_id=to,
+        device_id_type=MESH,
+    )
+
+
+def unit_tiles(unit, body):
+    edges = [start // UNIT for start in matrix_starts()]
+    kinds = {}
+    for index, tiles in enumerate(TILES):
+        inside = (unit >= edges[index]) & (unit < edges[index + 1])
+        kinds[tiles] = kinds[tiles] | inside if tiles in kinds else inside
+    for tiles, inside in kinds.items():
+        pl.when(inside)(lambda tiles=tiles: body(tiles))
+
+
+def gather_kernel(
+    ways, flat, whole, small, extended, aligned, tail,
+    tail_send, tail_recv, slot_send, slot_recv, pair_send, pair_recv, small_send, small_recv,
+):
+    s, g = place()
+    planes = ways // 4
+    z, y, x = s // 4, lax.rem(s // 2, 2), lax.rem(s, 2)
+    own = MAT_ROWS // ways
+    half = own // 2
+    flat_rows = flat.shape[0]
+    entries = (MAT_ROWS * LANES + bounds_total()) // ways - own * LANES
+    last_row, last_lane = divmod(own * LANES + entries, LANES)
+    lanes = lax.broadcasted_iota(jnp.int32, (SMALL_ROWS, LANES), 1)
+    gap = LANES - last_lane
+    older = pltpu.roll(flat[last_row - SMALL_ROWS : last_row, :], gap, 1)
+    newer = pltpu.roll(flat[last_row - SMALL_ROWS + 1 : last_row + 1, :], gap, 1)
+    tail[...] = jnp.where(lanes < gap, older, newer)
+    enter(ways)
+    follow = remote(
+        tail, extended.at[pl.ds(0, SMALL_ROWS)], tail_send, tail_recv, (lax.rem(s + 1, ways), g)
+    )
+    follow.start()
+    extended[SMALL_ROWS : SMALL_ROWS + flat_rows, :] = flat[...]
+    extended[SMALL_ROWS + flat_rows :, :] = jnp.zeros(
+        (extended.shape[0] - SMALL_ROWS - flat_rows, LANES), F32
+    )
+    follow.wait()
+    shift = entries * s
+    row_shift, lane_shift = shift // LANES, lax.rem(shift, LANES)
+    step_rows = 176
+    step_lanes = lax.broadcasted_iota(jnp.int32, (step_rows, LANES), 1)
+
+    def align(step, carry):
+        start = step * step_rows
+        here = extended[pl.ds(SMALL_ROWS + start - row_shift, step_rows), :]
+        before = extended[pl.ds(SMALL_ROWS - 1 + start - row_shift, step_rows), :]
+        aligned[pl.ds(pl.multiple_of(start, 8), step_rows), :] = jnp.where(
+            step_lanes >= lane_shift,
+            pltpu.roll(here, lane_shift, 1),
+            pltpu.roll(before, lane_shift, 1),
+        )
+        return carry
+
+    lax.fori_loop(0, (own + SMALL_ROWS) // step_rows, align, 0)
+    base = s * own
+
+    def fill(unit, carry):
+        first = unit * UNIT
+
+        def tiled(tiles):
+            for group in range(UNIT // (16 * tiles)):
+                for tile in range(tiles):
+                    rows = aligned[pl.ds(first + group * 16 * tiles + tile, 16, stride=tiles), :]
+                    at = base + first + 16 * (group * tiles + tile)
+                    whole[g, pl.ds(pl.multiple_of(at, 16), 16), :] = rows.astype(BF16)
+
+        unit_tiles(s * (own // UNIT) + unit, tiled)
+        return carry
+
+    lax.fori_loop(0, own // UNIT, fill, 0)
+
+    def slot(plane, row, column, part):
+        at = ((plane * 2 + row) * 2 + column) * own + part * half
+        return whole.at[g, pl.ds(pl.multiple_of(at, 16), half)]
+
+    def copy(plane, row, column, part, kind, to):
+        where = slot(plane, row, column, part)
+        return remote(
+            where,
+            where,
+            slot_send.at[part, plane, kind],
+            slot_recv.at[part, (plane * 2 + row) * 2 + column],
+            to,
+        )
+
+    def chip(plane, row, column):
+        return ((plane * 2 + row) * 2 + column, g)
+
+    def spread(plane, act):
+        for part in range(2):
+            if act == "start":
+                pl.when(z != plane)(copy(plane, y, x, part, 0, chip(z, y, x)).wait_recv)
+            up = copy(plane, y, x, part, 0, chip(z + 1, y, x))
+            down = copy(plane, y, x, part, 1, chip(z - 1, y, x))
+            to_x = copy(plane, y, x, part, 2, chip(z, y, 1 - x))
+            to_y = copy(plane, y, x, part, 3, chip(z, 1 - y, x))
+            act_on = (lambda c: c.start) if act == "start" else (lambda c: c.wait_send)
+            pl.when((z >= plane) & (z < planes - 1))(act_on(up))
+            pl.when((z <= plane) & (z > 0))(act_on(down))
+            act_on(to_y if part == 0 else to_x)()
+            act_on(to_x if part == 0 else to_y)()
+
+    def turn(plane, act):
+        first = copy(plane, 1 - y, x, 0, 4, chip(z, y, 1 - x))
+        second = copy(plane, y, 1 - x, 1, 4, chip(z, 1 - y, x))
+        for onward in (first, second):
+            if act == "start":
+                onward.wait_recv()
+                onward.start()
+            else:
+                onward.wait_send()
+
+    def across(plane):
+        block = whole.at[g, pl.ds(plane * 4 * own, 4 * own)]
+        return remote(block, block, pair_send.at[plane], pair_recv.at[plane], (s, 1 - g))
+
+    def finish(plane):
+        copy(plane, y, 1 - x, 0, 0, chip(z, y, x)).wait_recv()
+        copy(plane, 1 - y, 1 - x, 0, 0, chip(z, y, x)).wait_recv()
+        copy(plane, 1 - y, x, 1, 0, chip(z, y, x)).wait_recv()
+        copy(plane, 1 - y, 1 - x, 1, 0, chip(z, y, x)).wait_recv()
+        across(plane).start()
+
+    def small_to(index):
+        return remote(small.at[g], small.at[g], small_send.at[index], small_recv.at[0], (index, g))
+
+    small_pair = remote(
+        small.at[g], small.at[g], small_send.at[ways - 1], small_recv.at[1], (s, 1 - g)
+    )
+
+    @pl.when(s == ways - 1)
+    def _():
+        small[g] = aligned[own : own + SMALL_ROWS, :].astype(BF16)
+
+    def tell(index, carry):
+        small_to(index).start()
+        return carry
+
+    def told(index, carry):
+        small_to(index).wait_send()
+        return carry
+
+    spread(0, "start")
+
+    @pl.when(s == ways - 1)
+    def _():
+        lax.fori_loop(0, ways - 1, tell, 0)
+
+    turn(0, "start")
+    for plane in range(1, planes):
+        spread(plane, "start")
+        turn(plane, "start")
+        if plane == 1:
+            pl.when(s != ways - 1)(small_to(s).wait_recv)
+            small_pair.start()
+        finish(plane - 1)
+    finish(planes - 1)
+    for plane in range(planes):
+        across(plane).wait()
+    for plane in range(planes):
+        spread(plane, "wait")
+        turn(plane, "wait")
+    small_pair.wait()
+
+    @pl.when(s == ways - 1)
+    def _():
+        lax.fori_loop(0, ways - 1, told, 0)
+
+
+def bounds_total():
+    return 5 * D // 2 + FF // 2
+
+
+def gather_params(flat, ways):
+    own = MAT_ROWS // ways
+    planes = ways // 4
+    dma = pltpu.SemaphoreType.DMA
+    return pl.pallas_call(
+        partial(gather_kernel, ways),
+        out_shape=(
+            jax.ShapeDtypeStruct((2, MAT_ROWS, LANES), BF16),
+            jax.ShapeDtypeStruct((2, SMALL_ROWS, LANES), BF16),
+        ),
+        in_specs=[pl.BlockSpec(memory_space=pltpu.VMEM)],
+        out_specs=(
+            pl.BlockSpec(memory_space=pltpu.VMEM),
+            pl.BlockSpec(memory_space=pltpu.VMEM),
+        ),
+        scratch_shapes=[
+            pltpu.VMEM((own + 2 * SMALL_ROWS, LANES), F32),
+            pltpu.VMEM((own + SMALL_ROWS, LANES), F32),
+            pltpu.VMEM((SMALL_ROWS, LANES), F32),
+            dma, dma,
+            dma((2, planes, 5)),
+            dma((2, ways)),
+            dma((planes,)), dma((planes,)),
+            dma((ways,)), dma((2,)),
+        ],
+        compiler_params=pltpu.CompilerParams(
+            collective_id=1, has_side_effects=True, vmem_limit_bytes=VMEM_BYTES
+        ),
+        name="gather_params",
+    )(flat)
+
+
+def dot(left, right):
+    return jnp.dot(left, right, preferred_element_type=F32)
+
+
+def dot_cols(left, right):
+    return contract_cols(left, right)
+
+
+def dot_rows(left, right):
+    return contract_rows(left, right)
+
+
+def tile_view(ref, index):
+    rows = 16 * TILES[index]
+    start = matrix_starts()[index]
+    return ref.reshape(ref.shape[:-2] + (MAT_ROWS // rows, rows, LANES)), start // rows
+
+
+def tile_groups(index):
+    tiles = TILES[index]
+    groups, at = [], 0
+    while at < tiles:
+        width = 3 if tiles - at == 3 else 2
+        groups.append((at, width))
+        at += width
+    return groups
+
+
+def weight(ref, index, half, row, rows, tile, width):
+    view, base = tile_view(ref, index)
+    first = base + row // 16
+    pieces = [
+        view[half, first : first + rows // 16, 16 * t : 16 * t + 16, :].reshape(rows, LANES)
+        for t in range(tile, tile + width)
+    ]
+    return jnp.concatenate(pieces, axis=1)
+
+
+def heads_of(rows):
+    row = lax.broadcasted_iota(jnp.int32, (rows, D), 0) * HEAD
+    column = lax.broadcasted_iota(jnp.int32, (rows, D), 1)
+    return ((column >= row) & (column < row + HEAD)).astype(F32)
+
+
+def to_columns(per_head):
+    return jnp.dot(
+        per_head, heads_of(HEADS), precision=lax.Precision.HIGHEST, preferred_element_type=F32
+    )
+
+
+def to_heads(columns):
+    return lax.dot_general(
+        columns,
+        heads_of(HEADS),
+        (((1,), (1,)), ((), ())),
+        precision=lax.Precision.HIGHEST,
+        preferred_element_type=F32,
+    )
+
+
+def pack_blocks(ref, values, extra):
+    blocks = values.shape[0] // 8
+    split = values.reshape(blocks, 8, D)
+    ref[:, :, : D // 2] = jnp.concatenate(
+        [split[:, :, : D // 2], split[:, :, D // 2 :]], axis=1
+    ).astype(BF16)
+    if extra is not None:
+        high = extra.astype(BF16).astype(F32)
+        low = extra - high
+        pieces = jnp.concatenate(
+            [high.reshape(blocks, 8, HEADS), low.reshape(blocks, 8, HEADS)], axis=1
+        )
+        ref[:, :, D // 2 : D // 2 + HEADS] = pieces.astype(BF16)
+
+
+def unpack_values(ref):
+    blocks = ref.shape[0]
+    values = ref[:, :, : D // 2].astype(F32)
+    return jnp.concatenate(
+        [values[:, :8, :].reshape(blocks * 8, D // 2), values[:, 8:, :].reshape(blocks * 8, D // 2)],
+        axis=1,
+    )
+
+
+def unpack_extra(ref):
+    blocks = ref.shape[0]
+    pieces = ref[:, :, D // 2 :].astype(F32)
+    both = pieces[:, :8, :] + pieces[:, 8:, :]
+    return both.reshape(blocks * 8, LANES)[:, :HEADS]
+
+
+def slide_masks(ends_ref, s, ways, near_keys, far_keys):
+    rows = near_keys.shape[1]
+    ends, end = [], 0
+    for index in range(ends_ref.shape[1]):
+        end = end + ends_ref[0, index]
+        ends.append(end)
+
+    def slides(positions):
+        total = jnp.zeros(positions.shape, jnp.int32)
+        for end in ends:
+            total = total + (positions >= end).astype(jnp.int32)
+        return total
+
+    across = rows // ways
+    result = []
+    for far, keys in ((False, near_keys), (True, far_keys)):
+        found = []
+        for dim in (0, 1):
+            at = lax.broadcasted_iota(jnp.int32, (rows, rows), dim)
+            if far:
+                position = s + ways * at
+            else:
+                position = rows * s + ways * lax.rem(at, across) + at // across
+            found.append(slides(position))
+        query = lax.broadcasted_iota(jnp.int32, (rows, rows), 0)
+        key = lax.broadcasted_iota(jnp.int32, (rows, rows), 1)
+        allowed = ((found[0] == found[1]) & (keys > 0.5)) | (query == key)
+        result.append(allowed.astype(F32))
+    return result
+
+
+def layer_kernel(
+    ways, tokens, cotangent, holes, lengths, whole, small,
+    output, input_grad, grads, small_grads,
+    turning, send_blocks, recv_blocks, masks, normed, normed_hat, inverse, projected, attended, lses,
+    mixture, second_in, activated, slope, second_hat, second_inverse, middle_grad,
+    qkv_grad, out_grad, up_grad, down_grad, near_grad, far_grad, lse_grads,
+    their_normed, their_mixture, their_second, their_activated,
+    their_qkv, their_out, their_up, their_down, small_parts, their_small,
+    block_send, block_recv, pair_send, pair_recv,
+):
+    s, g = place()
+    rows = tokens.shape[0]
+    across = rows // ways
+    tiles = D // LANES
+
+    def exchange(index):
+        def start(step, carry):
+            to = lax.rem(s + step, ways)
+            remote(
+                send_blocks.at[index, to],
+                recv_blocks.at[index, s],
+                block_send.at[index],
+                block_recv.at[index],
+                (to, g),
+            ).start()
+            return carry
+
+        recv_blocks[index, s] = send_blocks[index, s]
+        lax.fori_loop(1, ways, start, 0)
+
+    def exchanged(index):
+        remote(
+            send_blocks.at[index, pl.ds(0, ways - 1)],
+            recv_blocks.at[index, pl.ds(0, ways - 1)],
+            block_send.at[index],
+            block_recv.at[index],
+            (s, 1 - g),
+        ).wait()
+
+    pairs = []
+
+    def hand_over(src, dst):
+        index = len(pairs)
+        copy = remote(src, dst, pair_send.at[index], pair_recv.at[index], (s, 1 - g))
+        copy.start()
+        pairs.append(copy)
+
+    def by_residue(value):
+        for tile in range(tiles):
+            turning[tile] = value[:, tile * LANES : (tile + 1) * LANES]
+        return jnp.concatenate(
+            [
+                jnp.concatenate(
+                    [turning[tile, pl.ds(i, across, stride=ways), :] for i in range(ways)], axis=0
+                )
+                for tile in range(tiles)
+            ],
+            axis=1,
+        )
+
+    def in_order(value):
+        for tile in range(tiles):
+            for i in range(ways):
+                turning[tile, pl.ds(i, across, stride=ways), :] = value[
+                    across * i : across * (i + 1), tile * LANES : (tile + 1) * LANES
+                ]
+        return jnp.concatenate([turning[tile] for tile in range(tiles)], axis=1)
+
+    def small_row(first, count):
+        return jnp.concatenate(
+            [small[half, first + r : first + r + 1, :] for half in range(2) for r in range(count)],
+            axis=1,
+        ).astype(F32)
+
+    third = D // 2 // LANES
+    gain_one, gain_two = small_row(0, third), small_row(third, third)
+    shift_one, shift_two = small_row(2 * third, third), small_row(3 * third, third)
+    shift_down = small_row(4 * third, third)
+    bias_up = small_row(5 * third, FF // 2 // LANES)
+
+    inputs = by_residue(tokens[...].astype(F32))
+    lane = lax.broadcasted_iota(jnp.int32, (rows, rows), 1)
+    row = lax.broadcasted_iota(jnp.int32, (rows, rows), 0)
+    flags = holes[...].astype(F32)
+    to_column = (row == lane).astype(F32)
+    own_column = jnp.sum(to_column * flags, axis=1, keepdims=True)
+    turned_at = ways * lax.rem(row, across) + row // across
+    turned_column = jnp.sum((turned_at == lane).astype(F32) * flags, axis=1, keepdims=True)
+    turned_row_at = ways * lax.rem(lane, across) + lane // across
+    turned_row = jnp.sum((turned_row_at == row).astype(F32) * own_column, axis=0, keepdims=True)
+    enter(ways)
+    pack_blocks(send_blocks.at[0], inputs, jnp.broadcast_to(turned_column, (rows, HEADS)) * 1.0)
+    exchange(0)
+    upstream = by_residue(cotangent[...].astype(F32))
+    half_width = D // 2
+    for half in range(2):
+        down_grad[half] = upstream[:, half * half_width : (half + 1) * half_width].astype(BF16)
+    hand_over(down_grad.at[1 - g], their_down)
+
+    exchanged(0)
+    far_inputs = unpack_values(recv_blocks.at[0])
+    far_column = unpack_extra(recv_blocks.at[0])[:, :1]
+    far_row = jnp.sum(to_column * far_column, axis=0, keepdims=True)
+    near_mask, far_mask = slide_masks(lengths, s, ways, turned_row, far_row)
+    masks[0] = near_mask
+    masks[1] = far_mask
+    hat, scale = normalize(jnp.concatenate([inputs, far_inputs], axis=0))
+    normed[...] = (hat * gain_one + shift_one).astype(BF16)
+    normed_hat[...] = hat[:rows]
+    inverse[...] = scale[:rows]
+    hand_over(normed, their_normed)
+    for half in range(2):
+        for tile, width in tile_groups(0):
+            at = half * 3 * half_width + tile * LANES
+            projected[:, at : at + width * LANES] = dot(
+                normed[...], weight(whole, 0, half, 0, D, tile, width)
+            ).astype(BF16)
+
+    temper = HEAD ** (-0.5)
+
+    def scores(which, head):
+        at = slice(which * rows, (which + 1) * rows)
+        query = projected[at, head * HEAD : (head + 1) * HEAD]
+        key = projected[at, D + head * HEAD : D + (head + 1) * HEAD]
+        value = projected[at, 2 * D + head * HEAD : 2 * D + (head + 1) * HEAD]
+        found = jnp.where(masks[which] > 0.5, dot_cols(query, key) * temper, NEG)
+        return query, key, value, found
+
+    def attend_set(which):
+        results, totals = [], []
+        for head in range(HEADS):
+            _, _, value, found = scores(which, head)
+            top = jnp.max(found, axis=1, keepdims=True)
+            weights = jnp.exp(found - top)
+            total = jnp.sum(weights, axis=1, keepdims=True)
+            results.append(dot(weights.astype(BF16), value) * (1.0 / total))
+            totals.append(top + jnp.log(total))
+        attended[which] = jnp.concatenate(results, axis=1)
+        lses[which] = jnp.concatenate(totals, axis=1)
+
+    attend_set(1)
+    pack_blocks(send_blocks.at[1], attended[1], lses[1])
+    exchange(1)
+    attend_set(0)
+    exchanged(1)
+    far_out = unpack_values(recv_blocks.at[1])
+    near_out = attended[0]
+    share = jax.nn.sigmoid(lses[0] - unpack_extra(recv_blocks.at[1]))
+    shares = to_columns(share)
+    difference = near_out - far_out
+    mixture[...] = (shares * near_out + (1.0 - shares) * far_out).astype(BF16)
+    hand_over(mixture, their_mixture)
+    middle = inputs + jnp.concatenate(
+        [dot(mixture[...], weight(whole, 1, half, 0, D, 0, third)) for half in range(2)], axis=1
+    )
+    hat, scale = normalize(middle)
+    second_hat[...] = hat
+    second_inverse[...] = scale
+    second_in[...] = (hat * gain_two + shift_two).astype(BF16)
+    hand_over(second_in, their_second)
+    root = (2.0 / 3.141592653589793) ** 0.5
+    for half in range(2):
+        for tile, width in tile_groups(2):
+            at = half * FF // 2 + tile * LANES
+            to = slice(at, at + width * LANES)
+            v = dot(second_in[...], weight(whole, 2, half, 0, D, tile, width)) + bias_up[:, to]
+            square = v * v
+            t = jnp.tanh(root * (v + 0.044715 * v * square))
+            activated[:, to] = (0.5 * v * (1.0 + t)).astype(BF16)
+            slope[:, to] = 0.5 * (1.0 + t) + 0.5 * v * (1.0 - t * t) * (
+                root * (1.0 + 3 * 0.044715 * square)
+            )
+    hand_over(activated, their_activated)
+    result = middle + shift_down + jnp.concatenate(
+        [dot(activated[...], weight(whole, 3, half, 0, FF, 0, third)) for half in range(2)], axis=1
+    )
+    output[...] = in_order(result).astype(BF16)
+
+    block = 256
+    up_sums = []
+    for start in range(0, FF, block):
+        to = slice(start, start + block)
+        pulled = sum(
+            dot_cols(down_grad[half], weight(whole, 3, half, start, block, 0, third))
+            for half in range(2)
+        )
+        grad = (pulled * slope[:, to]).astype(BF16)
+        half, at = divmod(start, FF // 2)
+        up_grad[half, :, at : at + block] = grad
+        up_sums.append(jnp.sum(grad.astype(F32), axis=0, keepdims=True))
+    hand_over(up_grad.at[1 - g], their_up)
+    second_grad = jnp.concatenate(
+        [
+            sum(
+                dot_cols(up_grad[half], weight(whole, 2, half, start, block, 0, TILES[2]))
+                for half in range(2)
+            )
+            for start in range(0, D, block)
+        ],
+        axis=1,
+    )
+    hat = second_hat[...]
+    gain_two_sum = jnp.sum(second_grad * hat, axis=0, keepdims=True)
+    shift_two_sum = jnp.sum(second_grad, axis=0, keepdims=True)
+    gained = upstream + norm_back(second_grad * gain_two, hat, second_inverse[...])
+    middle_grad[...] = gained
+    for half in range(2):
+        out_grad[half] = gained[:, half * half_width : (half + 1) * half_width].astype(BF16)
+    hand_over(out_grad.at[1 - g], their_out)
+    mix_grad = jnp.concatenate(
+        [
+            sum(
+                dot_cols(out_grad[half], weight(whole, 1, half, start, block, 0, third))
+                for half in range(2)
+            )
+            for start in range(0, D, block)
+        ],
+        axis=1,
+    )
+    near_lse_grad = share * (1.0 - share) * to_heads(difference * mix_grad)
+    lse_grads[0] = near_lse_grad
+    near_grad[...] = (shares * mix_grad).astype(BF16)
+    pack_blocks(send_blocks.at[2], (1.0 - shares) * mix_grad, -near_lse_grad)
+    exchange(2)
+
+    def attend_set_back(which, out_grads):
+        lists = ([], [], [])
+        for head in range(HEADS):
+            query, key, value, found = scores(which, head)
+            weights = jnp.exp(found - lses[which, :, head : head + 1])
+            pulled = out_grads[:, head * HEAD : (head + 1) * HEAD]
+            weight_grad = dot_cols(pulled, value)
+            inner = jnp.sum(weights * weight_grad, axis=1, keepdims=True)
+            extra = lse_grads[which, :, head : head + 1] - inner
+            score_grad = (weights * (weight_grad + extra)).astype(BF16)
+            lists[0].append(dot(score_grad, key) * temper)
+            lists[1].append(dot_rows(score_grad, query) * temper)
+            lists[2].append(dot_rows(weights.astype(BF16), pulled))
+        at = slice(which * rows, (which + 1) * rows)
+        query_grad, key_grad, value_grad = (jnp.concatenate(one, axis=1).astype(BF16) for one in lists)
+        qkv_grad[0, at, :D] = query_grad
+        qkv_grad[0, at, D:] = key_grad[:, :half_width]
+        qkv_grad[1, at, :half_width] = key_grad[:, half_width:]
+        qkv_grad[1, at, half_width:] = value_grad
+
+    attend_set_back(0, near_grad)
+    exchanged(2)
+    far_grad[...] = unpack_values(recv_blocks.at[2]).astype(BF16)
+    lse_grads[1] = unpack_extra(recv_blocks.at[2])
+    attend_set_back(1, far_grad)
+    hand_over(qkv_grad.at[1 - g], their_qkv)
+    first_grad = jnp.concatenate(
+        [
+            sum(
+                dot_cols(qkv_grad[half], weight(whole, 0, half, start, block, 0, TILES[0]))
+                for half in range(2)
+            )
+            for start in range(0, D, block)
+        ],
+        axis=1,
+    )
+    pack_blocks(send_blocks.at[3], first_grad[rows:], None)
+    exchange(3)
+
+    def weight_grad(index, mine, theirs, grad, their_grad, first, count):
+        left = jnp.concatenate(
+            [mine[:, first : first + count], theirs[:, first : first + count]], axis=0
+        )
+        view, base = tile_view(grads, index)
+        at = base + first // 16
+        for tile, width in tile_groups(index):
+            to = slice(tile * LANES, (tile + width) * LANES)
+            right = jnp.concatenate([grad[g, :, to], their_grad[:, to]], axis=0)
+            found = dot_rows(left, right).astype(BF16)
+            for t in range(width):
+                view[at : at + count // 16, 16 * (tile + t) : 16 * (tile + t) + 16, :] = found[
+                    :, t * LANES : (t + 1) * LANES
+                ].reshape(count // 16, 16, LANES)
+
+    for copy in pairs:
+        copy.wait()
+    for first in range(0, FF, D):
+        weight_grad(3, activated, their_activated, down_grad, their_down, first, D)
+    weight_grad(2, second_in, their_second, up_grad, their_up, 0, D)
+    weight_grad(1, mixture, their_mixture, out_grad, their_out, 0, D)
+    weight_grad(0, normed, their_normed, qkv_grad, their_qkv, 0, D)
+
+    exchanged(3)
+    first_grad = first_grad[:rows] + unpack_values(recv_blocks.at[3])
+    hat = normed_hat[...]
+    gain_one_sum = jnp.sum(first_grad * hat, axis=0, keepdims=True)
+    shift_one_sum = jnp.sum(first_grad, axis=0, keepdims=True)
+    input_grad[...] = in_order(
+        middle_grad[...] + norm_back(first_grad * gain_one, hat, inverse[...])
+    )
+    down_sums = [
+        jnp.sum(down_grad[half].astype(F32), axis=0, keepdims=True) for half in range(2)
+    ]
+    up_sum = jnp.concatenate(up_sums, axis=1)
+    for half in range(2):
+        to = slice(half * half_width, (half + 1) * half_width)
+        listed = (
+            gain_one_sum[:, to], gain_two_sum[:, to], shift_one_sum[:, to], shift_two_sum[:, to],
+            down_sums[half], up_sum[:, half * FF // 2 : (half + 1) * FF // 2],
+        )
+        at = 0
+        for vector in listed:
+            count = vector.shape[1] // LANES
+            small_parts[half, at : at + count, :] = vector.reshape(count, LANES)
+            at += count
+        small_parts[half, at:, :] = jnp.zeros((SMALL_ROWS - at, LANES), F32)
+    hand_over(small_parts.at[1 - g], their_small)
+    pairs[-1].wait()
+    small_grads[...] = small_parts[g] + their_small[...]
+
+
+def run_layer(tokens, cotangent, holes, lengths, whole, small, ways):
+    rows = tokens.shape[0]
+    vmem = pl.BlockSpec(memory_space=pltpu.VMEM)
+    dma = pltpu.SemaphoreType.DMA
+    half = D // 2
+    shapes = [
+        ((D // LANES, rows, LANES), F32),
+        ((4, ways, 16, half + LANES), BF16),
+        ((4, ways, 16, half + LANES), BF16),
+        ((2, rows, rows), F32),
+        ((2 * rows, D), BF16),
+        ((rows, D), F32),
+        ((rows, 1), F32),
+        ((2 * rows, 3 * D), BF16),
+        ((2, rows, D), F32),
+        ((2, rows, HEADS), F32),
+        ((rows, D), BF16),
+        ((rows, D), BF16),
+        ((rows, FF), BF16),
+        ((rows, FF), F32),
+        ((rows, D), F32),
+        ((rows, 1), F32),
+        ((rows, D), F32),
+        ((2, 2 * rows, 3 * half), BF16),
+        ((2, rows, half), BF16),
+        ((2, rows, FF // 2), BF16),
+        ((2, rows, half), BF16),
+        ((rows, D), BF16),
+        ((rows, D), BF16),
+        ((2, rows, HEADS), F32),
+        ((2 * rows, D), BF16),
+        ((rows, D), BF16),
+        ((rows, D), BF16),
+        ((rows, FF), BF16),
+        ((2 * rows, 3 * half), BF16),
+        ((rows, half), BF16),
+        ((rows, FF // 2), BF16),
+        ((rows, half), BF16),
+        ((2, SMALL_ROWS, LANES), F32),
+        ((SMALL_ROWS, LANES), F32),
+    ]
+    return pl.pallas_call(
+        partial(layer_kernel, ways),
+        out_shape=(
+            jax.ShapeDtypeStruct((rows, D), BF16),
+            jax.ShapeDtypeStruct((rows, D), F32),
+            jax.ShapeDtypeStruct((MAT_ROWS, LANES), BF16),
+            jax.ShapeDtypeStruct((SMALL_ROWS, LANES), F32),
+        ),
+        in_specs=[vmem, vmem, vmem, pl.BlockSpec(memory_space=pltpu.SMEM), vmem, vmem],
+        out_specs=(vmem,) * 4,
+        scratch_shapes=[pltpu.VMEM(*shape) for shape in shapes]
+        + [dma((4,)), dma((4,)), dma((9,)), dma((9,))],
+        compiler_params=pltpu.CompilerParams(
+            collective_id=2, has_side_effects=True, vmem_limit_bytes=VMEM_BYTES
+        ),
+        name="run_layer",
+    )(tokens, cotangent, holes, lengths, whole, small)
+
+
+def reduce_kernel(
+    ways, grads_in, small_in, flat, grads, by_x, by_y, up_blocks, down_blocks, total, laid, follow_rows,
+    small_all, x_send, x_recv, y_send, y_recv, z_send, up_recv, down_recv, tail_sem, small_sem,
+    load_sem,
+):
+    s, g = place()
+    planes = ways // 4
+    z, y, x = s // 4, lax.rem(s // 2, 2), lax.rem(s, 2)
+    own = MAT_ROWS // ways
+    half = own // 2
+    load = pltpu.make_async_copy(grads_in, grads, load_sem)
+    load.start()
+    enter(ways)
+    load.wait()
+
+    def at(plane, row, column, part):
+        first = ((plane * 2 + row) * 2 + column) * own + part * half
+        return pl.ds(pl.multiple_of(first, 16), half)
+
+    def chip(plane, row, column):
+        return ((plane * 2 + row) * 2 + column, g)
+
+    def first_copies(plane):
+        for k in range(2):
+            yield remote(
+                grads.at[at(plane, k, 1 - x, 0)], by_x.at[plane, 0, k],
+                x_send.at[plane, 0, k], x_recv.at[plane, 0, k], chip(z, y, 1 - x),
+            )
+            yield remote(
+                grads.at[at(plane, 1 - y, k, 1)], by_x.at[plane, 1, k],
+                x_send.at[plane, 1, k], x_recv.at[plane, 1, k], chip(z, 1 - y, x),
+            )
+
+    def first_wait(plane, part, k):
+        remote(
+            by_x.at[plane, part, k], by_x.at[plane, part, k],
+            x_send.at[plane, part, k], x_recv.at[plane, part, k], chip(z, y, x),
+        ).wait_recv()
+
+    def second_copies(plane):
+        yield remote(
+            grads.at[at(plane, 1 - y, x, 0)], by_y.at[plane, 0],
+            y_send.at[plane, 0], y_recv.at[plane, 0], chip(z, 1 - y, x),
+        )
+        yield remote(
+            grads.at[at(plane, y, 1 - x, 1)], by_y.at[plane, 1],
+            y_send.at[plane, 1], y_recv.at[plane, 1], chip(z, y, 1 - x),
+        )
+
+    def add(where, block):
+        grads[where, :] = (grads[where, :].astype(F32) + block[...].astype(F32)).astype(BF16)
+
+    def second(plane):
+        for part, other in ((0, 1 - y), (1, 1 - x)):
+            first_wait(plane, part, other)
+            where = at(plane, other, x, 0) if part == 0 else at(plane, y, other, 1)
+            add(where, by_x.at[plane, part, other])
+        for copy in second_copies(plane):
+            copy.start()
+        for part, mine in ((0, y), (1, x)):
+            first_wait(plane, part, mine)
+            add(at(plane, y, x, part), by_x.at[plane, part, mine])
+
+    def line_copies(plane, part):
+        where = grads.at[at(plane, y, x, part)]
+        up = remote(
+            where, up_blocks.at[plane, part], z_send.at[plane, part], up_recv.at[plane, part],
+            chip(z + 1, y, x),
+        )
+        down = remote(
+            where, down_blocks.at[plane, part], z_send.at[plane, part], down_recv.at[plane, part],
+            chip(z - 1, y, x),
+        )
+        return up, down
+
+    def line(plane):
+        for part, copy in enumerate(second_copies(plane)):
+            copy.wait_recv()
+            where = at(plane, y, x, part)
+            add(where, by_y.at[plane, part])
+            up, down = line_copies(plane, part)
+
+            def take_up(where=where, up=up, part=part):
+                up.wait_recv()
+                add(where, up_blocks.at[plane, part])
+
+            def take_down(where=where, down=down, part=part):
+                down.wait_recv()
+                add(where, down_blocks.at[plane, part])
+
+            pl.when((z < plane) & (z > 0))(take_up)
+            pl.when((z > plane) & (z < planes - 1))(take_down)
+            pl.when(z < plane)(up.start)
+            pl.when(z > plane)(down.start)
+
+    def settle(plane):
+        def at_home():
+            for part in range(2):
+                up, down = line_copies(plane, part)
+                to = slice(part * half, (part + 1) * half)
+                total[to, :] = grads[at(plane, y, x, part), :].astype(F32)
+                if plane > 0:
+                    up.wait_recv()
+                    total[to, :] += up_blocks[plane, part].astype(F32)
+                if plane < planes - 1:
+                    down.wait_recv()
+                    total[to, :] += down_blocks[plane, part].astype(F32)
+
+        pl.when(z == plane)(at_home)
+
+    small_copy = remote(
+        small_in, small_all.at[s], small_sem.at[0], small_sem.at[1], (ways - 1, g)
+    )
+    pl.when(s != ways - 1)(small_copy.start)
+    order = list(range(planes - 1, -1, -1))
+    for plane in order:
+        for copy in first_copies(plane):
+            copy.start()
+    for plane in order:
+        second(plane)
+    for plane in order:
+        line(plane)
+    for plane in order:
+        settle(plane)
+
+    def lay(unit, carry):
+        first = unit * UNIT
+
+        def tiled(tiles):
+            for group in range(UNIT // (16 * tiles)):
+                for tile in range(tiles):
+                    rows = total[pl.ds(first + 16 * (group * tiles + tile), 16), :]
+                    laid[pl.ds(first + group * 16 * tiles + tile, 16, stride=tiles), :] = rows
+
+        unit_tiles(s * (own // UNIT) + unit, tiled)
+        return carry
+
+    lax.fori_loop(0, own // UNIT, lay, 0)
+
+    @pl.when(s == ways - 1)
+    def _():
+        remote(
+            small_all.at[pl.ds(0, ways - 1)], small_all.at[pl.ds(0, ways - 1)],
+            small_sem.at[0], small_sem.at[1], (0, g),
+        ).wait_recv()
+        small_all[ways - 1] = small_in[...]
+        laid[own : own + SMALL_ROWS, :] = jnp.sum(small_all[...], axis=0)
+
+    pl.when(s != ways - 1)(small_copy.wait_send)
+    follow = remote(
+        laid.at[pl.ds(0, SMALL_ROWS)], follow_rows, tail_sem.at[0], tail_sem.at[1],
+        (lax.rem(s + ways - 1, ways), g),
+    )
+    follow.start()
+    follow.wait()
+
+    @pl.when(s != ways - 1)
+    def _():
+        laid[own : own + SMALL_ROWS, :] = follow_rows[...]
+
+    flat_rows = flat.shape[0]
+    laid[own + SMALL_ROWS :, :] = jnp.zeros(
+        (laid.shape[0] - own - SMALL_ROWS, LANES), F32
+    )
+    entries = (MAT_ROWS * LANES + bounds_total()) // ways - own * LANES
+    shift = entries * s
+    row_shift, lane_shift = shift // LANES, lax.rem(shift, LANES)
+    back = lax.rem(LANES - lane_shift, LANES)
+    step_rows = 56
+    lanes = lax.broadcasted_iota(jnp.int32, (step_rows, LANES), 1)
+
+    def align(step, carry):
+        start = step * step_rows
+        here = laid[pl.ds(start + row_shift, step_rows), :]
+        after = laid[pl.ds(start + row_shift + 1, step_rows), :]
+        flat[pl.ds(pl.multiple_of(start, 8), step_rows), :] = jnp.where(
+            lanes < LANES - lane_shift, pltpu.roll(here, back, 1), pltpu.roll(after, back, 1)
+        )
+        return carry
+
+    lax.fori_loop(0, flat_rows // step_rows, align, 0)
+    for plane in order:
+        for copy in first_copies(plane):
+            copy.wait_send()
+        for copy in second_copies(plane):
+            copy.wait_send()
+        for part in range(2):
+            pl.when(z != plane)(line_copies(plane, part)[0].wait_send)
+
+
+def reduce_grads(grads, small, flat_rows, ways):
+    own = MAT_ROWS // ways
+    half = own // 2
+    planes = ways // 4
+    dma = pltpu.SemaphoreType.DMA
+    vmem = pl.BlockSpec(memory_space=pltpu.VMEM)
+    return pl.pallas_call(
+        partial(reduce_kernel, ways),
+        out_shape=jax.ShapeDtypeStruct((flat_rows, LANES), F32),
+        in_specs=[pl.BlockSpec(memory_space=pl.ANY), vmem],
+        out_specs=vmem,
+        scratch_shapes=[
+            pltpu.VMEM((MAT_ROWS, LANES), BF16),
+            pltpu.VMEM((planes, 2, 2, half, LANES), BF16),
+            pltpu.VMEM((planes, 2, half, LANES), BF16),
+            pltpu.VMEM((planes, 2, half, LANES), BF16),
+            pltpu.VMEM((planes, 2, half, LANES), BF16),
+            pltpu.VMEM((own, LANES), F32),
+            pltpu.VMEM((own + 2 * SMALL_ROWS, LANES), F32),
+            pltpu.VMEM((SMALL_ROWS, LANES), F32),
+            pltpu.VMEM((ways, SMALL_ROWS, LANES), F32),
+            dma((planes, 2, 2)), dma((planes, 2, 2)),
+            dma((planes, 2)), dma((planes, 2)),
+            dma((planes, 2)), dma((planes, 2)), dma((planes, 2)),
+            dma((2,)), dma((2,)), dma,
+        ],
+        compiler_params=pltpu.CompilerParams(
+            collective_id=3, has_side_effects=True, vmem_limit_bytes=VMEM_BYTES
+        ),
+        name="reduce_grads",
+    )(grads, small)
+
+
+def on_device(tokens, cotangent, holes, slide_lengths, master, first_moment, second_moment):
+    ways = lax.axis_size("seq")
+    shard_size = master.shape[1]
+    flat_rows = -(-shard_size // (8 * LANES)) * 8
+    flat = jnp.pad(master[0], (0, flat_rows * LANES - shard_size)).reshape(flat_rows, LANES)
+    whole, small = gather_params(flat, ways)
+    output, input_grad, grads, small_grads = run_layer(
+        tokens[0], cotangent[0], holes, slide_lengths, whole, small, ways
+    )
+    reduced = reduce_grads(grads, small_grads, flat_rows, ways).reshape(-1)[:shard_size]
+    flat_index = lax.axis_index("seq") * shard_size + jnp.arange(shard_size, dtype=jnp.int32)
+    new_moment, new_second, new_master = adam_update(
+        master[0], first_moment[0], second_moment[0], reduced, flat_index
+    )
+    return (output[None], input_grad[None], new_moment[None], new_second[None], new_master[None])
+
+
+def even(mesh):
+    ways = mesh.shape["seq"]
+    return ways % 4 == 0 and MAT_ROWS % (ways * UNIT) == 0 and ways * 8 == LANES
+
+
 def solution(mesh):
     return jax.shard_map(
-        on_device,
+        on_device if even(mesh) else plain_on_device,
         mesh=mesh,
         in_specs=(
             P("grp", "seq", None),

time: 1690 us -> 323 us (0.19); the launches traced: 1660 us -> 318 us
  waiting for transfers between devices: 633 us -> 0 us
  local copies, waits for them, and re-layouts: 505 us -> 19 us
  matrix products: 342 us -> 0 us
  Pallas kernels: 0 us -> 275 us
  other arithmetic: 90.9 us -> 22.7 us
  starting transfers between devices: 52.5 us -> 0 us
  blocking collectives: 21.4 us -> 0 us
    unnamed x6 -> x0, waiting for transfers between devices: 604 us -> none
    dot_general x252 -> x0, matrix products: 342 us -> none  [the longest x116 119 us: contract_cols(): lax.dot_general(left, right, (((1,), (1,)), ((), ())), preferred_element_...]
    pallas_call x0 -> x3, Pallas kernels: none -> 275 us  [the longest x1 110 us: gather_params(): pl.pallas_call(partial(gather_kernel, ways), out_shape=(jax.ShapeDtypeStr...]
    unnamed x132 -> x4, local copies, waits for them, and re-layouts: 184 us -> 3.39 us
    slice x15 -> x0, local copies, waits for them, and re-layouts: 123 us -> none  [the longest x3 108 us: joined(): flat[1, start:stop].reshape(shape)]
    all_to_all x9 -> x0, starting transfers between devices: 52.3 us -> none  [the longest x1 7.1 us: on_device(): lax.all_to_all(far_local_lse.reshape(row_count, 1, HEADS).astype(jnp.bflo...]
    dynamic_update_slice x48 -> x0, local copies, waits for them, and re-layouts: 41.8 us -> none  [attend(): lax.map(one_head, (split_heads(packed[:, :D]), split_heads(packed[:, D:2...]
    another operation x23 -> x0, local copies, waits for them, and re-layouts: 41.3 us -> none  [the longest x6 17.7 us: joined(): flat[1, start:stop].reshape(shape)]
  transfers between devices with their start and end apart: 13 -> 0, of which waited for: 5 -> 0; matrix products, arithmetic and copies ran while one was open for 32% -> 0% of each run, Pallas kernels for 0% -> 0%
where the time goes in v1:
time: 323 us; the launch traced here: 318 us
  Pallas kernels  275 us (85%)
  other arithmetic  22.7 us (7%)
  local copies, waits for them, and re-layouts  19 us (6%)
    pallas_call x1, Pallas kernels, gather_params(): pl.pallas_call(partial(gather_kernel, ways), out_shape=(jax.ShapeDtypeStr...  110 us
    pallas_call x1, Pallas kernels, reduce_grads(): pl.pallas_call(partial(reduce_kernel, ways), out_shape=jax.ShapeDtypeStru...  104 us
    pallas_call x1, Pallas kernels, run_layer(): pl.pallas_call(partial(layer_kernel, ways), out_shape=(jax.ShapeDtypeStru...  60.6 us
    mul x1, other arithmetic, adam_update(): new_second = BETA_TWO * second + (1.0 - BETA_TWO) * gradient * gradient  10.3 us
    unnamed x1, other arithmetic  10.2 us

profile of v1, /device:TPU:0, one launch (start us, length us, event | category | flops | bytes accessed | tf_op | source)
XLA Modules:
  0.0 318.1 jit_solution(1318731999784874934)
XLA Ops:
  0.6 0.0 copy-start
  0.6 10.2 %reduce = f32[221400]{0:T(1024)S(1)} reduce(f32[1,221400]{1,0:T(1,128)} %param.11, f32[]{:T(128)} %constant.61), dimensions={0}, to_apply=%param.11.reduce_sub_computation | reduce | bytes 1771204 | tf_op args[4]
  10.9 1.0 pad_bitcast_fusion.flat
  11.9 110.4 %gather_params.1 = (bf16[2,27648,128]{2,1,0:T(8,128)(2,1)}, bf16[2,32,128]{2,1,0:T(8,128)(2,1)}) custom-call(f32[1736,128]{1,0:T(8,128)} %pad_bitcast_fusion.flat), custom_call_target="tpu_custom_call" | custom-call | tf_op jit(solution)/shard_map/gather_params/pallas_call | solution.py:602
  122.2 60.6 %run_layer.1 = (bf16[128,768]{1,0:T(8,128)(2,1)}, f32[128,768]{1,0:T(8,128)}, bf16[27648,128]{1,0:T(8,128)(2,1)}, f32[32,128]{1,0:T(8,128)}) custom-call(bf16[128,768]{1,0:T(8,128)(2,1)} %bitcast.9, bf16[128,768]{1,0:T(8,128)(2,1)} %bitcast.10, s32[1,128]{1,0:T(1,128)} %holes.1, s32[1,8]{1,0:T(1,128)} %lengths.1, ...), custom_call_target="tpu_custom_call" | custom-call | tf_op jit(solution)/shard_map/run_layer/pallas_call | solution.py:1109
  182.9 104.5 %reduce_grads.1 = f32[1736,128]{1,0:T(8,128)} custom-call(bf16[27648,128]{1,0:T(8,128)(2,1)} %get-tuple-element.15.grads_in, f32[32,128]{1,0:T(8,128)} %get-tuple-element.16.small_in), custom_call_target="tpu_custom_call" | custom-call | tf_op jit(solution)/shard_map/reduce_grads/pallas_call | solution.py:1324
  287.4 0.0 copy-done
  287.4 10.3 %multiply_reduce_fusion = (f32[221400]{0:T(1024)S(1)}, f32[221400]{0:T(1024)S(1)}) fusion(f32[1,221400]{1,0:T(1,128)S(1)} %copy-done, f32[1,221400]{1,0:T(1,128)} %param.12), kind=kLoop, calls=%fused_computation.11 | loop fusion | flops 442800 | bytes 3542400 | tf_op jit(solution)/shard_map/mul | solution.py:180
  297.6 2.3 multiply_subtract_fusion
  299.9 4.9 %broadcast_in_dim.44 = f32[1,221400]{1,0:T(1,128)} reshape(f32[221400]{0:T(1024)S(1)} %get-tuple-element.19) | data formatting | bytes 1771200 | tf_op jit(solution)/shard_map/broadcast_in_dim | solution.py:1365
  304.8 4.9 %broadcast_in_dim.45 = f32[1,221400]{1,0:T(1,128)} reshape(f32[221400]{0:T(1024)S(1)} %get-tuple-element.18) | data formatting | bytes 1771200 | tf_op jit(solution)/shard_map/broadcast_in_dim | solution.py:1365
  309.7 4.9 %broadcast_in_dim.53 = f32[1,221400]{1,0:T(1,128)} reshape(f32[221400]{0:T(1024)S(1)} %get-tuple-element.17) | data formatting | bytes 1771200 | tf_op jit(solution)/shard_map/broadcast_in_dim | solution.py:1365
  314.5 1.6 copy.14
  316.1 1.8 copy.15
Async XLA Ops:
  0.6 286.7 %copy-start = (f32[1,221400]{1,0:T(1,128)S(1)}, f32[1,221400]{1,0:T(1,128)}, u32[]{:S(2)}) copy-start(f32[1,221400]{1,0:T(1,128)} %param.13) | copy-start | bytes 2656804

commit v2 on v0

--- a/solution.py
+++ b/solution.py
@@ -3,6 +3,8 @@
 import jax
 import jax.numpy as jnp
 from jax import lax
+from jax.experimental import pallas as pl
+from jax.experimental.pallas import tpu as pltpu
 from jax.sharding import PartitionSpec as P
 
 D = 768
@@ -186,7 +188,7 @@
     return values.reshape(values.shape[0], 2, values.shape[1] // 2)
 
 
-def on_device(tokens, cotangent, holes, slide_lengths, master, first_moment, second_moment):
+def plain_on_device(tokens, cotangent, holes, slide_lengths, master, first_moment, second_moment):
     own_half = lax.all_gather(master.astype(jnp.bfloat16), "seq", axis=1, tiled=True)
     whole_flat = lax.all_gather(own_half, "grp", axis=0, tiled=True)
     w_qkv, w_out, w_up, w_down, gain_rows, shift_rows, bias_up = unpack(whole_flat)
@@ -369,9 +371,1133 @@
     )
 
 
+LANES = 128
+BF16 = jnp.bfloat16
+F32 = jnp.float32
+MAT_ROWS = (3 * D * D + D * D + D * FF + FF * D) // 2 // LANES
+SMALL_ROWS = 32
+UNIT = 576
+PAIR = 2
+TILES = (3 * D // 2 // LANES, D // 2 // LANES, FF // 2 // LANES, D // 2 // LANES)
+DEPTHS = (D, D, D, FF)
+MESH = pl.DeviceIdType.MESH
+VMEM_BYTES = 60 * 2**20
+NEG = -1000000000.0
+
+
+def matrix_starts():
+    starts = [0]
+    for tiles, depth in zip(TILES, DEPTHS):
+        starts.append(starts[-1] + tiles * depth)
+    return starts
+
+
+def place():
+    return lax.axis_index("seq"), lax.axis_index("grp")
+
+
+def greet_all(ways):
+    s, g = place()
+    barrier = pltpu.get_barrier_semaphore()
+
+    def greet(step, carry):
+        pl.semaphore_signal(
+            barrier, inc=1, device_id=(lax.rem(s + step, ways), g), device_id_type=MESH
+        )
+        return carry
+
+    lax.fori_loop(1, ways, greet, 0)
+    pl.semaphore_signal(barrier, inc=1, device_id=(s, 1 - g), device_id_type=MESH)
+    return barrier
+
+
+def remote(src, dst, send_sem, recv_sem, to):
+    return pltpu.make_async_remote_copy(
+        src_ref=src,
+        dst_ref=dst,
+        send_sem=send_sem,
+        recv_sem=recv_sem,
+        device_id=to,
+        device_id_type=MESH,
+    )
+
+
+def unit_tiles(unit, body):
+    edges = [start // UNIT for start in matrix_starts()]
+    kinds = {}
+    for index, tiles in enumerate(TILES):
+        inside = (unit >= edges[index]) & (unit < edges[index + 1])
+        kinds[tiles] = kinds[tiles] | inside if tiles in kinds else inside
+    for tiles, inside in kinds.items():
+        pl.when(inside)(lambda tiles=tiles: body(tiles))
+
+
+def dot(left, right):
+    return jnp.dot(left, right, preferred_element_type=F32)
+
+
+def dot_cols(left, right):
+    return contract_cols(left, right)
+
+
+def dot_rows(left, right):
+    return contract_rows(left, right)
+
+
+def tile_view(ref, index):
+    rows = 16 * TILES[index]
+    start = matrix_starts()[index]
+    return ref.reshape(ref.shape[:-2] + (MAT_ROWS // rows, rows, LANES)), start // rows
+
+
+def tile_groups(index):
+    tiles = TILES[index]
+    groups, at = [], 0
+    while at < tiles:
+        width = 3 if tiles - at == 3 else 2
+        groups.append((at, width))
+        at += width
+    return groups
+
+
+def weight(ref, index, half, row, rows, tile, width):
+    view, base = tile_view(ref, index)
+    first = base + row // 16
+    pieces = [
+        view[half, first : first + rows // 16, 16 * t : 16 * t + 16, :].reshape(rows, LANES)
+        for t in range(tile, tile + width)
+    ]
+    return jnp.concatenate(pieces, axis=1)
+
+
+def heads_of(rows):
+    row = lax.broadcasted_iota(jnp.int32, (rows, D), 0) * HEAD
+    column = lax.broadcasted_iota(jnp.int32, (rows, D), 1)
+    return ((column >= row) & (column < row + HEAD)).astype(F32)
+
+
+def to_columns(per_head):
+    return jnp.dot(
+        per_head, heads_of(HEADS), precision=lax.Precision.HIGHEST, preferred_element_type=F32
+    )
+
+
+def to_heads(columns):
+    return lax.dot_general(
+        columns,
+        heads_of(HEADS),
+        (((1,), (1,)), ((), ())),
+        precision=lax.Precision.HIGHEST,
+        preferred_element_type=F32,
+    )
+
+
+def pack_blocks(ref, values, extra):
+    blocks = values.shape[0] // 8
+    split = values.reshape(blocks, 8, D)
+    ref[:, :, : D // 2] = jnp.concatenate(
+        [split[:, :, : D // 2], split[:, :, D // 2 :]], axis=1
+    ).astype(BF16)
+    if extra is not None:
+        high = extra.astype(BF16).astype(F32)
+        low = extra - high
+        pieces = jnp.concatenate(
+            [high.reshape(blocks, 8, HEADS), low.reshape(blocks, 8, HEADS)], axis=1
+        )
+        ref[:, :, D // 2 : D // 2 + HEADS] = pieces.astype(BF16)
+
+
+def unpack_values(ref):
+    blocks = ref.shape[0]
+    values = ref[:, :, : D // 2].astype(F32)
+    return jnp.concatenate(
+        [values[:, :8, :].reshape(blocks * 8, D // 2), values[:, 8:, :].reshape(blocks * 8, D // 2)],
+        axis=1,
+    )
+
+
+def unpack_extra(ref):
+    blocks = ref.shape[0]
+    pieces = ref[:, :, D // 2 :].astype(F32)
+    both = pieces[:, :8, :] + pieces[:, 8:, :]
+    return both.reshape(blocks * 8, LANES)[:, :HEADS]
+
+
+def slide_masks(ends_ref, s, ways, near_keys, far_keys):
+    rows = near_keys.shape[1]
+    ends, end = [], 0
+    for index in range(ends_ref.shape[1]):
+        end = end + ends_ref[0, index]
+        ends.append(end)
+
+    def slides(positions):
+        total = jnp.zeros(positions.shape, jnp.int32)
+        for end in ends:
+            total = total + (positions >= end).astype(jnp.int32)
+        return total
+
+    across = rows // ways
+    result = []
+    for far, keys in ((False, near_keys), (True, far_keys)):
+        found = []
+        for dim in (0, 1):
+            at = lax.broadcasted_iota(jnp.int32, (rows, rows), dim)
+            if far:
+                position = s + ways * at
+            else:
+                position = rows * s + ways * lax.rem(at, across) + at // across
+            found.append(slides(position))
+        query = lax.broadcasted_iota(jnp.int32, (rows, rows), 0)
+        key = lax.broadcasted_iota(jnp.int32, (rows, rows), 1)
+        allowed = ((found[0] == found[1]) & (keys > 0.5)) | (query == key)
+        result.append(allowed.astype(F32))
+    return result
+
+
+def step_kernel(
+    ways, tokens, cotangent, holes, lengths, flat,
+    output, input_grad, flat_grad,
+    whole, grads, small, extended, aligned, tail,
+    turning, send_blocks, recv_blocks, masks, normed, normed_hat, inverse, projected, attended, lses,
+    mixture, second_in, activated, slope, second_hat, second_inverse, middle_grad,
+    qkv_grad, out_grad, up_grad, down_grad, near_grad, far_grad, lse_grads,
+    their_normed, their_mixture, their_second, their_activated,
+    their_qkv, their_out, their_up, their_down, small_parts, their_small,
+    by_x, by_y, by_z, total, laid, follow_rows, small_all,
+    tail_sem, slot_send, slot_recv, core_send, core_recv, small_send, small_recv,
+    block_send, block_recv, pair_send, pair_recv,
+    x_send, x_recv, y_send, y_recv, z_send, z_recv, end_sem, sum_sem,
+):
+    s, g = place()
+    planes = ways // 4
+    z, y, x = s // 4, lax.rem(s // 2, 2), lax.rem(s, 2)
+    own = MAT_ROWS // ways
+    half_own = own // 2
+    rows = tokens.shape[0]
+    across = rows // ways
+    tiles = D // LANES
+    half_width = D // 2
+    third = half_width // LANES
+    entries = (MAT_ROWS * LANES + bounds_total()) // ways - own * LANES
+    shift = entries * s
+    row_shift, lane_shift = shift // LANES, lax.rem(shift, LANES)
+
+    def chip(plane, row, column):
+        return ((plane * 2 + row) * 2 + column, g)
+
+    def part_at(plane, row, column, part):
+        first = ((plane * 2 + row) * 2 + column) * own + part * half_own
+        return pl.ds(pl.multiple_of(first, 16), half_own)
+
+
+    last_row, last_lanes = divmod(own * LANES + entries, LANES)
+
+    def take_flat():
+        end = SMALL_ROWS + flat.shape[0]
+        extended[SMALL_ROWS:end, :] = flat[...]
+        extended[end:, :] = jnp.zeros((extended.shape[0] - end, LANES), F32)
+
+    def follow_copy():
+        return remote(
+            tail, extended.at[pl.ds(0, SMALL_ROWS)], tail_sem.at[0], tail_sem.at[1],
+            (lax.rem(s + 1, ways), g),
+        )
+
+    def send_tail():
+        lanes = lax.broadcasted_iota(jnp.int32, (SMALL_ROWS, LANES), 1)
+        gap = LANES - last_lanes
+        older = pltpu.roll(flat[last_row - SMALL_ROWS : last_row, :], gap, 1)
+        newer = pltpu.roll(flat[last_row - SMALL_ROWS + 1 : last_row + 1, :], gap, 1)
+        tail[...] = jnp.where(lanes < gap, older, newer)
+        follow_copy().start()
+
+    def align_own():
+        follow_copy().wait()
+        step_rows = 176
+        step_lanes = lax.broadcasted_iota(jnp.int32, (step_rows, LANES), 1)
+
+        def align(step, carry):
+            start = step * step_rows
+            here = extended[pl.ds(SMALL_ROWS + start - row_shift, step_rows), :]
+            before = extended[pl.ds(SMALL_ROWS - 1 + start - row_shift, step_rows), :]
+            aligned[pl.ds(pl.multiple_of(start, 8), step_rows), :] = jnp.where(
+                step_lanes >= lane_shift,
+                pltpu.roll(here, lane_shift, 1),
+                pltpu.roll(before, lane_shift, 1),
+            )
+            return carry
+
+        lax.fori_loop(0, (own + SMALL_ROWS) // step_rows, align, 0)
+
+        def fill(unit, carry):
+            first = unit * UNIT
+
+            def tiled(count):
+                for group in range(UNIT // (16 * count)):
+                    for tile in range(count):
+                        block = aligned[pl.ds(first + group * 16 * count + tile, 16, stride=count), :]
+                        at = s * own + first + 16 * (group * count + tile)
+                        whole[g, pl.ds(pl.multiple_of(at, 16), 16), :] = block.astype(BF16)
+
+            unit_tiles(s * (own // UNIT) + unit, tiled)
+            return carry
+
+        lax.fori_loop(0, own // UNIT, fill, 0)
+
+    order = [z]
+    for step in range(1, planes):
+        listed = [[p for p in ([0] + [q for q in range(at + 1, planes)] + [q for q in range(at - 1, 0, -1)]) if p != at]
+                  for at in range(planes)]
+        plane = jnp.int32(listed[0][step - 1])
+        for at in range(1, planes):
+            plane = jnp.where(z == at, listed[at][step - 1], plane)
+        order.append(plane)
+
+    def slot_copy(plane, row, column, part, kind, to):
+        where = whole.at[g, part_at(plane, row, column, part)]
+        return remote(
+            where,
+            where,
+            slot_send.at[part, plane, kind],
+            slot_recv.at[part, (plane * 2 + row) * 2 + column],
+            to,
+        )
+
+    def line_up(plane, part):
+        return slot_copy(plane, y, x, part, 0, chip(z + 1, y, x))
+
+    def line_down(plane, part):
+        return slot_copy(plane, y, x, part, 1, chip(z - 1, y, x))
+
+    def in_plane(plane, part):
+        to_x = slot_copy(plane, y, x, part, 2, chip(z, y, 1 - x))
+        to_y = slot_copy(plane, y, x, part, 3, chip(z, 1 - y, x))
+        return (to_y, to_x) if part == 0 else (to_x, to_y)
+
+    def turned(plane):
+        return (
+            slot_copy(plane, 1 - y, x, 0, 4, chip(z, y, 1 - x)),
+            slot_copy(plane, y, 1 - x, 1, 4, chip(z, 1 - y, x)),
+        )
+
+    def spread_own():
+        for part in range(2):
+            pl.when(z > 0)(lambda part=part: line_down(z, part).start())
+            pl.when(z == 0)(lambda part=part: line_up(z, part).start())
+            for copy in in_plane(z, part):
+                copy.start()
+
+    def spread_own_up():
+        for part in range(2):
+            pl.when((z > 0) & (z < planes - 1))(lambda part=part: line_up(z, part).start())
+
+    def spread(step):
+        plane = order[step]
+        for part in range(2):
+            slot_copy(plane, y, x, part, 0, chip(z, y, x)).wait_recv()
+            pl.when((z > plane) & (z < planes - 1))(lambda part=part: line_up(plane, part).start())
+            pl.when((z < plane) & (z > 0))(lambda part=part: line_down(plane, part).start())
+            for copy in in_plane(plane, part):
+                copy.start()
+
+    def turn(step):
+        for copy in turned(order[step]):
+            copy.wait_recv()
+            copy.start()
+
+    def across_copy(plane):
+        block = whole.at[g, pl.ds(pl.multiple_of(plane * 4 * own, 16), 4 * own)]
+        return remote(block, block, core_send.at[plane], core_recv.at[plane], (s, 1 - g))
+
+    def across_recv(plane):
+        block = whole.at[1 - g, pl.ds(pl.multiple_of(plane * 4 * own, 16), 4 * own)]
+        return remote(block, block, core_send.at[plane], core_recv.at[plane], (s, 1 - g))
+
+    def finish(step):
+        plane = order[step]
+        slot_copy(plane, y, 1 - x, 0, 0, chip(z, y, x)).wait_recv()
+        slot_copy(plane, 1 - y, 1 - x, 0, 0, chip(z, y, x)).wait_recv()
+        slot_copy(plane, 1 - y, x, 1, 0, chip(z, y, x)).wait_recv()
+        slot_copy(plane, 1 - y, 1 - x, 1, 0, chip(z, y, x)).wait_recv()
+        across_copy(plane).start()
+
+    def arrived(step):
+        across_recv(order[step]).wait_recv()
+
+    def gather_sent():
+        for plane in range(planes):
+            for part in range(2):
+                pl.when((z >= plane) & (z < planes - 1))(
+                    lambda part=part, plane=plane: line_up(plane, part).wait_send()
+                )
+                pl.when((z <= plane) & (z > 0))(
+                    lambda part=part, plane=plane: line_down(plane, part).wait_send()
+                )
+                for copy in in_plane(plane, part):
+                    copy.wait_send()
+            for copy in turned(plane):
+                copy.wait_send()
+            across_copy(plane).wait_send()
+
+    def small_to(index):
+        return remote(small.at[g], small.at[g], small_send.at[index], small_recv.at[0], (index, g))
+
+    def small_across():
+        return remote(
+            small.at[g], small.at[g], small_send.at[ways - 1], small_recv.at[1], (s, 1 - g)
+        )
+
+    def small_out():
+        def tell(index, carry):
+            small_to(index).start()
+            return carry
+
+        @pl.when(s == ways - 1)
+        def _():
+            small[g] = aligned[own : own + SMALL_ROWS, :].astype(BF16)
+            lax.fori_loop(0, ways - 1, tell, 0)
+
+    def small_in():
+        pl.when(s != ways - 1)(lambda: small_to(s).wait_recv())
+        small_across().start()
+        remote(
+            small.at[1 - g], small.at[1 - g], small_send.at[ways - 1], small_recv.at[1], (s, 1 - g)
+        ).wait_recv()
+
+    def small_sent():
+        def told(index, carry):
+            small_to(index).wait_send()
+            return carry
+
+        @pl.when(s == ways - 1)
+        def _():
+            lax.fori_loop(0, ways - 1, told, 0)
+
+        small_across().wait_send()
+
+
+    def first_copies(plane):
+        for k in range(2):
+            yield remote(
+                grads.at[part_at(plane, k, 1 - x, 0)], by_x.at[plane, 0, k],
+                x_send.at[plane, 0, k], x_recv.at[plane, 0, k], chip(z, y, 1 - x),
+            )
+            yield remote(
+                grads.at[part_at(plane, 1 - y, k, 1)], by_x.at[plane, 1, k],
+                x_send.at[plane, 1, k], x_recv.at[plane, 1, k], chip(z, 1 - y, x),
+            )
+
+    def first_wait(plane, part, k):
+        remote(
+            by_x.at[plane, part, k], by_x.at[plane, part, k],
+            x_send.at[plane, part, k], x_recv.at[plane, part, k], chip(z, y, x),
+        ).wait_recv()
+
+    def second_copies(plane):
+        yield remote(
+            grads.at[part_at(plane, 1 - y, x, 0)], by_y.at[plane, 0],
+            y_send.at[plane, 0], y_recv.at[plane, 0], chip(z, 1 - y, x),
+        )
+        yield remote(
+            grads.at[part_at(plane, y, 1 - x, 1)], by_y.at[plane, 1],
+            y_send.at[plane, 1], y_recv.at[plane, 1], chip(z, y, 1 - x),
+        )
+
+    def add(where, block):
+        grads[where, :] = (grads[where, :].astype(F32) + block[...].astype(F32)).astype(BF16)
+
+    def reduce_first(plane):
+        for copy in first_copies(plane):
+            copy.start()
+
+    def reduce_second(plane):
+        copies = list(second_copies(plane))
+        for part, other in ((0, 1 - y), (1, 1 - x)):
+            first_wait(plane, part, other)
+            where = part_at(plane, other, x, 0) if part == 0 else part_at(plane, y, other, 1)
+            add(where, by_x.at[plane, part, other])
+            copies[part].start()
+        for part, mine in ((0, y), (1, x)):
+            first_wait(plane, part, mine)
+            add(part_at(plane, y, x, part), by_x.at[plane, part, mine])
+
+    def home_copy(plane, part, step):
+        return remote(
+            grads.at[part_at(plane, y, x, part)], by_z.at[step - 1, part],
+            z_send.at[plane, part], z_recv.at[step - 1, part], chip(plane, y, x),
+        )
+
+    def reduce_third(plane):
+        for part, copy in enumerate(second_copies(plane)):
+            copy.wait_recv()
+            add(part_at(plane, y, x, part), by_y.at[plane, part])
+
+            @pl.when(z != plane)
+            def _(part=part):
+                home_copy(plane, part, lax.rem(planes + plane - z, planes)).start()
+
+    def reduce_sent():
+        for plane in range(planes):
+            for copy in first_copies(plane):
+                copy.wait_send()
+            for copy in second_copies(plane):
+                copy.wait_send()
+            for part in range(2):
+
+                @pl.when(z != plane)
+                def _(part=part, plane=plane):
+                    home_copy(plane, part, lax.rem(planes + plane - z, planes)).wait_send()
+
+    def reduce_last():
+        for part in range(2):
+            to = slice(part * half_own, (part + 1) * half_own)
+            total[to, :] = grads[part_at(z, y, x, part), :].astype(F32)
+            for step in range(1, planes):
+                home_copy(z, part, step).wait_recv()
+                total[to, :] += by_z[step - 1, part].astype(F32)
+
+    def small_home():
+        return remote(
+            small_parts.at[g], small_all.at[s], sum_sem.at[0], sum_sem.at[1], (ways - 1, g)
+        )
+
+    def settle():
+        def lay(unit, carry):
+            first = unit * UNIT
+
+            def tiled(count):
+                for group in range(UNIT // (16 * count)):
+                    for tile in range(count):
+                        block = total[
+                            pl.ds(pl.multiple_of(first + 16 * (group * count + tile), 16), 16), :
+                        ]
+                        laid[pl.ds(first + group * 16 * count + tile, 16, stride=count), :] = block
+
+            unit_tiles(s * (own // UNIT) + unit, tiled)
+            return carry
+
+        lax.fori_loop(0, own // UNIT, lay, 0)
+        follow = remote(
+            laid.at[pl.ds(0, SMALL_ROWS)], follow_rows, end_sem.at[0], end_sem.at[1],
+            (lax.rem(s + ways - 1, ways), g),
+        )
+        follow.start()
+
+        @pl.when(s == ways - 1)
+        def _():
+            remote(
+                small_all.at[pl.ds(0, ways - 1)], small_all.at[pl.ds(0, ways - 1)],
+                sum_sem.at[0], sum_sem.at[1], (0, g),
+            ).wait_recv()
+            small_all[ways - 1] = small_parts[g]
+            laid[own : own + SMALL_ROWS, :] = jnp.sum(small_all[...], axis=0)
+
+        laid[own + SMALL_ROWS :, :] = jnp.zeros((laid.shape[0] - own - SMALL_ROWS, LANES), F32)
+        follow.wait()
+
+        @pl.when(s != ways - 1)
+        def _():
+            laid[own : own + SMALL_ROWS, :] = follow_rows[...]
+
+        back = lax.rem(LANES - lane_shift, LANES)
+        step_rows = 56
+        lanes = lax.broadcasted_iota(jnp.int32, (step_rows, LANES), 1)
+
+        def align(step, carry):
+            start = step * step_rows
+            here = laid[pl.ds(start + row_shift, step_rows), :]
+            after = laid[pl.ds(start + row_shift + 1, step_rows), :]
+            flat_grad[pl.ds(pl.multiple_of(start, 8), step_rows), :] = jnp.where(
+                lanes < LANES - lane_shift, pltpu.roll(here, back, 1), pltpu.roll(after, back, 1)
+            )
+            return carry
+
+        lax.fori_loop(0, flat_grad.shape[0] // step_rows, align, 0)
+
+
+    def exchange(index):
+        def start(step, carry):
+            to = lax.rem(s + step, ways)
+            remote(
+                send_blocks.at[index, to],
+                recv_blocks.at[index, s],
+                block_send.at[index],
+                block_recv.at[index],
+                (to, g),
+            ).start()
+            return carry
+
+        recv_blocks[index, s] = send_blocks[index, s]
+        lax.fori_loop(1, ways, start, 0)
+
+    def exchanged(index):
+        remote(
+            send_blocks.at[index, pl.ds(0, ways - 1)],
+            recv_blocks.at[index, pl.ds(0, ways - 1)],
+            block_send.at[index],
+            block_recv.at[index],
+            (s, 1 - g),
+        ).wait()
+
+    pairs = {}
+
+    def hand_over(name, src, dst):
+        index = len(pairs)
+        pairs[name] = remote(src, dst, pair_send.at[index], pair_recv.at[index], (s, 1 - g))
+        pairs[name].start()
+
+    def by_residue(value):
+        for tile in range(tiles):
+            turning[tile] = value[:, tile * LANES : (tile + 1) * LANES]
+        return jnp.concatenate(
+            [
+                jnp.concatenate(
+                    [turning[tile, pl.ds(i, across, stride=ways), :] for i in range(ways)], axis=0
+                )
+                for tile in range(tiles)
+            ],
+            axis=1,
+        )
+
+    def in_order(value):
+        for tile in range(tiles):
+            for i in range(ways):
+                turning[tile, pl.ds(i, across, stride=ways), :] = value[
+                    across * i : across * (i + 1), tile * LANES : (tile + 1) * LANES
+                ]
+        return jnp.concatenate([turning[tile] for tile in range(tiles)], axis=1)
+
+    def small_row(first, count):
+        return jnp.concatenate(
+            [small[half, first + r : first + r + 1, :] for half in range(2) for r in range(count)],
+            axis=1,
+        ).astype(F32)
+
+    temper = HEAD ** (-0.5)
+
+    def scores(which, head):
+        at = slice(which * rows, (which + 1) * rows)
+        query = projected[at, head * HEAD : (head + 1) * HEAD]
+        key = projected[at, D + head * HEAD : D + (head + 1) * HEAD]
+        value = projected[at, 2 * D + head * HEAD : 2 * D + (head + 1) * HEAD]
+        found = jnp.where(masks[which] > 0.5, dot_cols(query, key) * temper, NEG)
+        return query, key, value, found
+
+    def attend_set(which, between):
+        results, totals = [], []
+        for head in range(HEADS):
+            _, _, value, found = scores(which, head)
+            top = jnp.max(found, axis=1, keepdims=True)
+            weights = jnp.exp(found - top)
+            summed = jnp.sum(weights, axis=1, keepdims=True)
+            results.append(dot(weights.astype(BF16), value) * (1.0 / summed))
+            totals.append(top + jnp.log(summed))
+            if head in between:
+                between[head]()
+        attended[which] = jnp.concatenate(results, axis=1)
+        lses[which] = jnp.concatenate(totals, axis=1)
+
+    def attend_set_back(which, out_grads, between):
+        lists = ([], [], [])
+        for head in range(HEADS):
+            query, key, value, found = scores(which, head)
+            weights = jnp.exp(found - lses[which, :, head : head + 1])
+            pulled = out_grads[:, head * HEAD : (head + 1) * HEAD]
+            weight_grad = dot_cols(pulled, value)
+            inner = jnp.sum(weights * weight_grad, axis=1, keepdims=True)
+            extra = lse_grads[which, :, head : head + 1] - inner
+            score_grad = (weights * (weight_grad + extra)).astype(BF16)
+            lists[0].append(dot(score_grad, key) * temper)
+            lists[1].append(dot_rows(score_grad, query) * temper)
+            lists[2].append(dot_rows(weights.astype(BF16), pulled))
+            if head in between:
+                between[head]()
+        at = slice(which * rows, (which + 1) * rows)
+        query_grad, key_grad, value_grad = (jnp.concatenate(one, axis=1).astype(BF16) for one in lists)
+        qkv_grad[0, at, :D] = query_grad
+        qkv_grad[0, at, D:] = key_grad[:, :half_width]
+        qkv_grad[1, at, :half_width] = key_grad[:, half_width:]
+        qkv_grad[1, at, half_width:] = value_grad
+
+    def weight_grad(index, mine, theirs, grad, their_grad, first, count):
+        left = jnp.concatenate(
+            [mine[:, first : first + count], theirs[:, first : first + count]], axis=0
+        )
+        view, base = tile_view(grads, index)
+        at = base + first // 16
+        for tile, width in tile_groups(index):
+            to = slice(tile * LANES, (tile + width) * LANES)
+            right = jnp.concatenate([grad[g, :, to], their_grad[:, to]], axis=0)
+            found = dot_rows(left, right).astype(BF16)
+            for t in range(width):
+                view[at : at + count // 16, 16 * (tile + t) : 16 * (tile + t) + 16, :] = found[
+                    :, t * LANES : (t + 1) * LANES
+                ].reshape(count // 16, 16, LANES)
+
+
+    barrier = greet_all(ways)
+    inputs = by_residue(tokens[...].astype(F32))
+    lane = lax.broadcasted_iota(jnp.int32, (rows, rows), 1)
+    row = lax.broadcasted_iota(jnp.int32, (rows, rows), 0)
+    flags = holes[...].astype(F32)
+    to_column = (row == lane).astype(F32)
+    own_column = jnp.sum(to_column * flags, axis=1, keepdims=True)
+    turned_at = ways * lax.rem(row, across) + row // across
+    turned_column = jnp.sum((turned_at == lane).astype(F32) * flags, axis=1, keepdims=True)
+    turned_row_at = ways * lax.rem(lane, across) + lane // across
+    turned_row = jnp.sum((turned_row_at == row).astype(F32) * own_column, axis=0, keepdims=True)
+    pack_blocks(send_blocks.at[0], inputs, jnp.broadcast_to(turned_column, (rows, HEADS)) * 1.0)
+    take_flat()
+    pl.semaphore_wait(barrier, ways)
+    send_tail()
+    exchange(0)
+    align_own()
+    spread_own()
+    small_out()
+
+    upstream = by_residue(cotangent[...].astype(F32))
+    for half in range(2):
+        down_grad[half] = upstream[:, half * half_width : (half + 1) * half_width].astype(BF16)
+    hand_over("down_grad", down_grad.at[1 - g], their_down)
+    exchanged(0)
+    spread(1)
+    spread_own_up()
+    far_inputs = unpack_values(recv_blocks.at[0])
+    far_column = unpack_extra(recv_blocks.at[0])[:, :1]
+    far_row = jnp.sum(to_column * far_column, axis=0, keepdims=True)
+    near_mask, far_mask = slide_masks(lengths, s, ways, turned_row, far_row)
+    masks[0] = near_mask
+    masks[1] = far_mask
+    turn(0)
+    hat, scale = normalize(jnp.concatenate([inputs, far_inputs], axis=0))
+    small_in()
+    gain_one, gain_two = small_row(0, third), small_row(third, third)
+    shift_one, shift_two = small_row(2 * third, third), small_row(3 * third, third)
+    shift_down = small_row(4 * third, third)
+    bias_up = small_row(5 * third, FF // 2 // LANES)
+    normed[...] = (hat * gain_one + shift_one).astype(BF16)
+    normed_hat[...] = hat[:rows]
+    inverse[...] = scale[:rows]
+    hand_over("normed", normed, their_normed)
+    spread(2)
+    turn(1)
+    finish(0)
+    finish(1)
+    spread(3)
+    arrived(0)
+    arrived(1)
+    for half in range(2):
+        for tile, width in tile_groups(0):
+            at = half * 3 * half_width + tile * LANES
+            projected[:, at : at + width * LANES] = dot(
+                normed[...], weight(whole, 0, half, 0, D, tile, width)
+            ).astype(BF16)
+    attend_set(1, {})
+    pack_blocks(send_blocks.at[1], attended[1], lses[1])
+    exchange(1)
+    turn(2)
+    attend_set(0, {HEADS // 2: lambda: finish(2)})
+    turn(3)
+    exchanged(1)
+    far_out = unpack_values(recv_blocks.at[1])
+    near_out = attended[0]
+    share = jax.nn.sigmoid(lses[0] - unpack_extra(recv_blocks.at[1]))
+    shares = to_columns(share)
+    difference = near_out - far_out
+    mixture[...] = (shares * near_out + (1.0 - shares) * far_out).astype(BF16)
+    hand_over("mixture", mixture, their_mixture)
+    finish(3)
+    arrived(2)
+    arrived(3)
+    middle = inputs + jnp.concatenate(
+        [dot(mixture[...], weight(whole, 1, half, 0, D, 0, third)) for half in range(2)], axis=1
+    )
+    hat, scale = normalize(middle)
+    second_hat[...] = hat
+    second_inverse[...] = scale
+    second_in[...] = (hat * gain_two + shift_two).astype(BF16)
+    hand_over("second_in", second_in, their_second)
+    root = (2.0 / 3.141592653589793) ** 0.5
+    for half in range(2):
+        for tile, width in tile_groups(2):
+            at = half * FF // 2 + tile * LANES
+            to = slice(at, at + width * LANES)
+            v = dot(second_in[...], weight(whole, 2, half, 0, D, tile, width)) + bias_up[:, to]
+            square = v * v
+            t = jnp.tanh(root * (v + 0.044715 * v * square))
+            activated[:, to] = (0.5 * v * (1.0 + t)).astype(BF16)
+            slope[:, to] = 0.5 * (1.0 + t) + 0.5 * v * (1.0 - t * t) * (
+                root * (1.0 + 3 * 0.044715 * square)
+            )
+    hand_over("activated", activated, their_activated)
+
+    block = 256
+    up_sums = []
+    for start in range(0, FF, block):
+        to = slice(start, start + block)
+        pulled = sum(
+            dot_cols(down_grad[half], weight(whole, 3, half, start, block, 0, third))
+            for half in range(2)
+        )
+        grad = (pulled * slope[:, to]).astype(BF16)
+        half, at = divmod(start, FF // 2)
+        up_grad[half, :, at : at + block] = grad
+        up_sums.append(jnp.sum(grad.astype(F32), axis=0, keepdims=True))
+    hand_over("up_grad", up_grad.at[1 - g], their_up)
+    pairs["down_grad"].wait()
+    pairs["activated"].wait()
+    for first in range(0, FF, D):
+        weight_grad(3, activated, their_activated, down_grad, their_down, first, D)
+    reduce_first(3)
+    second_grad = jnp.concatenate(
+        [
+            sum(
+                dot_cols(up_grad[half], weight(whole, 2, half, start, block, 0, TILES[2]))
+                for half in range(2)
+            )
+            for start in range(0, D, block)
+        ],
+        axis=1,
+    )
+    hat = second_hat[...]
+    gain_two_sum = jnp.sum(second_grad * hat, axis=0, keepdims=True)
+    shift_two_sum = jnp.sum(second_grad, axis=0, keepdims=True)
+    gained = upstream + norm_back(second_grad * gain_two, hat, second_inverse[...])
+    middle_grad[...] = gained
+    for half in range(2):
+        out_grad[half] = gained[:, half * half_width : (half + 1) * half_width].astype(BF16)
+    hand_over("out_grad", out_grad.at[1 - g], their_out)
+    mix_grad = jnp.concatenate(
+        [
+            sum(
+                dot_cols(out_grad[half], weight(whole, 1, half, start, block, 0, third))
+                for half in range(2)
+            )
+            for start in range(0, D, block)
+        ],
+        axis=1,
+    )
+    near_lse_grad = share * (1.0 - share) * to_heads(difference * mix_grad)
+    lse_grads[0] = near_lse_grad
+    near_grad[...] = (shares * mix_grad).astype(BF16)
+    pack_blocks(send_blocks.at[2], (1.0 - shares) * mix_grad, -near_lse_grad)
+    exchange(2)
+    pairs["second_in"].wait()
+    pairs["up_grad"].wait()
+    weight_grad(2, second_in, their_second, up_grad, their_up, 0, D)
+    reduce_first(2)
+    pairs["mixture"].wait()
+    pairs["out_grad"].wait()
+    weight_grad(1, mixture, their_mixture, out_grad, their_out, 0, D)
+    reduce_first(1)
+    reduce_second(3)
+    result = middle + shift_down + jnp.concatenate(
+        [dot(activated[...], weight(whole, 3, half, 0, FF, 0, third)) for half in range(2)], axis=1
+    )
+    output[...] = in_order(result).astype(BF16)
+
+    attend_set_back(0, near_grad, {HEADS // 2: lambda: reduce_third(3)})
+    reduce_second(2)
+    exchanged(2)
+    far_grad[...] = unpack_values(recv_blocks.at[2]).astype(BF16)
+    lse_grads[1] = unpack_extra(recv_blocks.at[2])
+    attend_set_back(1, far_grad, {HEADS // 2: lambda: reduce_third(2)})
+    hand_over("qkv_grad", qkv_grad.at[1 - g], their_qkv)
+    reduce_second(1)
+    first_grad = jnp.concatenate(
+        [
+            sum(
+                dot_cols(qkv_grad[half], weight(whole, 0, half, start, block, 0, TILES[0]))
+                for half in range(2)
+            )
+            for start in range(0, D, block)
+        ],
+        axis=1,
+    )
+    pack_blocks(send_blocks.at[3], first_grad[rows:], None)
+    exchange(3)
+    pairs["normed"].wait()
+    pairs["qkv_grad"].wait()
+    weight_grad(0, normed, their_normed, qkv_grad, their_qkv, 0, D)
+    reduce_first(0)
+    reduce_third(1)
+
+    exchanged(3)
+    first_grad = first_grad[:rows] + unpack_values(recv_blocks.at[3])
+    hat = normed_hat[...]
+    gain_one_sum = jnp.sum(first_grad * hat, axis=0, keepdims=True)
+    shift_one_sum = jnp.sum(first_grad, axis=0, keepdims=True)
+    input_grad[...] = in_order(
+        middle_grad[...] + norm_back(first_grad * gain_one, hat, inverse[...])
+    )
+    down_sums = [
+        jnp.sum(down_grad[half].astype(F32), axis=0, keepdims=True) for half in range(2)
+    ]
+    up_sum = jnp.concatenate(up_sums, axis=1)
+    for half in range(2):
+        to = slice(half * half_width, (half + 1) * half_width)
+        listed = (
+            gain_one_sum[:, to], gain_two_sum[:, to], shift_one_sum[:, to], shift_two_sum[:, to],
+            down_sums[half], up_sum[:, half * FF // 2 : (half + 1) * FF // 2],
+        )
+        at = 0
+        for vector in listed:
+            count = vector.shape[1] // LANES
+            small_parts[half, at : at + count, :] = vector.reshape(count, LANES)
+            at += count
+        small_parts[half, at:, :] = jnp.zeros((SMALL_ROWS - at, LANES), F32)
+    hand_over("small", small_parts.at[1 - g], their_small)
+    pairs["small"].wait()
+    small_parts[g] = small_parts[g] + their_small[...]
+    pl.when(s != ways - 1)(lambda: small_home().start())
+    reduce_second(0)
+    reduce_third(0)
+    reduce_last()
+    settle()
+    pl.when(s != ways - 1)(lambda: small_home().wait_send())
+    gather_sent()
+    small_sent()
+    reduce_sent()
+
+
+def bounds_total():
+    return 5 * D // 2 + FF // 2
+
+
+def run_step(tokens, cotangent, holes, lengths, flat, ways):
+    rows = tokens.shape[0]
+    flat_rows = flat.shape[0]
+    own = MAT_ROWS // ways
+    half_own = own // 2
+    planes = ways // 4
+    vmem = pl.BlockSpec(memory_space=pltpu.VMEM)
+    dma = pltpu.SemaphoreType.DMA
+    half = D // 2
+    shapes = [
+        ((2, MAT_ROWS, LANES), BF16),
+        ((MAT_ROWS, LANES), BF16),
+        ((2, SMALL_ROWS, LANES), BF16),
+        ((own + 2 * SMALL_ROWS, LANES), F32),
+        ((own + SMALL_ROWS, LANES), F32),
+        ((SMALL_ROWS, LANES), F32),
+        ((D // LANES, rows, LANES), F32),
+        ((4, ways, 16, half + LANES), BF16),
+        ((4, ways, 16, half + LANES), BF16),
+        ((2, rows, rows), F32),
+        ((2 * rows, D), BF16),
+        ((rows, D), F32),
+        ((rows, 1), F32),
+        ((2 * rows, 3 * D), BF16),
+        ((2, rows, D), F32),
+        ((2, rows, HEADS), F32),
+        ((rows, D), BF16),
+        ((rows, D), BF16),
+        ((rows, FF), BF16),
+        ((rows, FF), F32),
+        ((rows, D), F32),
+        ((rows, 1), F32),
+        ((rows, D), F32),
+        ((2, 2 * rows, 3 * half), BF16),
+        ((2, rows, half), BF16),
+        ((2, rows, FF // 2), BF16),
+        ((2, rows, half), BF16),
+        ((rows, D), BF16),
+        ((rows, D), BF16),
+        ((2, rows, HEADS), F32),
+        ((2 * rows, D), BF16),
+        ((rows, D), BF16),
+        ((rows, D), BF16),
+        ((rows, FF), BF16),
+        ((2 * rows, 3 * half), BF16),
+        ((rows, half), BF16),
+        ((rows, FF // 2), BF16),
+        ((rows, half), BF16),
+        ((2, SMALL_ROWS, LANES), F32),
+        ((SMALL_ROWS, LANES), F32),
+        ((planes, 2, 2, half_own, LANES), BF16),
+        ((planes, 2, half_own, LANES), BF16),
+        ((planes - 1, 2, half_own, LANES), BF16),
+        ((own, LANES), F32),
+        ((own + 2 * SMALL_ROWS, LANES), F32),
+        ((SMALL_ROWS, LANES), F32),
+        ((ways, SMALL_ROWS, LANES), F32),
+    ]
+    return pl.pallas_call(
+        partial(step_kernel, ways),
+        out_shape=(
+            jax.ShapeDtypeStruct((rows, D), BF16),
+            jax.ShapeDtypeStruct((rows, D), F32),
+            jax.ShapeDtypeStruct((flat_rows, LANES), F32),
+        ),
+        in_specs=[
+            vmem, vmem, vmem, pl.BlockSpec(memory_space=pltpu.SMEM), vmem,
+        ],
+        out_specs=(vmem,) * 3,
+        scratch_shapes=[pltpu.VMEM(*shape) for shape in shapes]
+        + [
+            dma((2,)),
+            dma((2, planes, 5)), dma((2, ways)),
+            dma((planes,)), dma((planes,)),
+            dma((ways,)), dma((2,)),
+            dma((4,)), dma((4,)), dma((9,)), dma((9,)),
+            dma((planes, 2, 2)), dma((planes, 2, 2)),
+            dma((planes, 2)), dma((planes, 2)),
+            dma((planes, 2)), dma((planes - 1, 2)),
+            dma((2,)), dma((2,)),
+        ],
+        compiler_params=pltpu.CompilerParams(
+            collective_id=1, has_side_effects=True, vmem_limit_bytes=VMEM_BYTES
+        ),
+        name="run_step",
+    )(tokens, cotangent, holes, lengths, flat)
+
+
+def rows_kernel(entries, flat, last, sems):
+    full, rest = divmod(entries.shape[1], LANES)
+    bulk = pltpu.make_async_copy(
+        entries.at[:, pl.ds(0, full * LANES)].reshape(full, LANES), flat.at[pl.ds(0, full)], sems.at[0]
+    )
+    end = pltpu.make_async_copy(entries.at[:, pl.ds(full * LANES, rest)], last, sems.at[1])
+    bulk.start()
+    end.start()
+    bulk.wait()
+    end.wait()
+    flat[full:, :] = jnp.zeros((flat.shape[0] - full, LANES), F32)
+    flat[full : full + 1, :rest] = last[...]
+
+
+def to_rows(entries):
+    size = entries.shape[1]
+    return pl.pallas_call(
+        rows_kernel,
+        out_shape=jax.ShapeDtypeStruct((-(-size // (8 * LANES)) * 8, LANES), F32),
+        in_specs=[pl.BlockSpec(memory_space=pl.ANY)],
+        out_specs=pl.BlockSpec(memory_space=pltpu.VMEM),
+        scratch_shapes=[pltpu.VMEM((1, size % LANES), F32), pltpu.SemaphoreType.DMA((2,))],
+        name="to_rows",
+    )(entries)
+
+
+def adam_kernel(
+    gradient, master, first_moment, second_moment, new_moment, new_second, new_master,
+    kept, last, load_sem, store_sem,
+):
+    size = master.shape[1]
+    full, rest = divmod(size, LANES)
+    chunks = 4
+    chunk = -(-full // (8 * chunks)) * 8
+    spans = [(c * chunk, min(chunk, full - c * chunk)) for c in range(chunks)]
+    sources, targets = (first_moment, second_moment, master), (new_moment, new_second, new_master)
+
+    def piece(array, first, count):
+        return array.at[:, pl.ds(first * LANES, count * LANES)].reshape(count, LANES)
+
+    def load(which, index):
+        first, count = spans[index]
+        return pltpu.make_async_copy(
+            piece(sources[which], first, count), kept.at[which, pl.ds(first, count)],
+            load_sem.at[which, index],
+        )
+
+    def store(which, index):
+        first, count = spans[index]
+        return pltpu.make_async_copy(
+            kept.at[which, pl.ds(first, count)], piece(targets[which], first, count),
+            store_sem.at[which, index],
+        )
+
+    def load_last(which):
+        return pltpu.make_async_copy(
+            sources[which].at[:, pl.ds(full * LANES, rest)], last.at[which], load_sem.at[which, chunks]
+        )
+
+    def store_last(which):
+        return pltpu.make_async_copy(
+            last.at[which], targets[which].at[:, pl.ds(full * LANES, rest)], store_sem.at[which, chunks]
+        )
+
+    for index in range(chunks):
+        for which in range(3):
+            load(which, index).start()
+    for which in range(3):
+        load_last(which).start()
+    origin = lax.axis_index("seq") * size
+
+    def update(first, count, moment, second, weights):
+        at = (
+            origin
+            + (first + lax.broadcasted_iota(jnp.int32, (count, LANES), 0)) * LANES
+            + lax.broadcasted_iota(jnp.int32, (count, LANES), 1)
+        )
+        return adam_update(weights, moment, second, gradient[pl.ds(first, count), :], at)
+
+    step = 8
+
+    for index, (first, count) in enumerate(spans):
+        for which in range(3):
+            load(which, index).wait()
+
+        def run(at, carry, first=first):
+            where = pl.multiple_of(first + at * step, 8)
+            span = pl.ds(where, step)
+            found = update(where, step, kept[0, span, :], kept[1, span, :], kept[2, span, :])
+            for which in range(3):
+                kept[which, span, :] = found[which]
+            return carry
+
+        lax.fori_loop(0, -(-count // step), run, 0, unroll=2)
+        for which in range(3):
+            store(which, index).start()
+    for which in range(3):
+        load_last(which).wait()
+    moment, second, weights = (last[which] for which in range(3))
+    at = origin + full * LANES + lax.broadcasted_iota(jnp.int32, (1, rest), 1)
+    found = adam_update(weights, moment, second, gradient[full : full + 1, :rest], at)
+    for which in range(3):
+        last[which] = found[which]
+        store_last(which).start()
+    for which in range(3):
+        for index in range(chunks):
+            store(which, index).wait()
+        store_last(which).wait()
+
+
+def run_adam(gradient, master, first_moment, second_moment):
+    size = master.shape[1]
+    anywhere = pl.BlockSpec(memory_space=pl.ANY)
+    return pl.pallas_call(
+        adam_kernel,
+        out_shape=(jax.ShapeDtypeStruct((1, size), F32),) * 3,
+        in_specs=[pl.BlockSpec(memory_space=pltpu.VMEM), anywhere, anywhere, anywhere],
+        out_specs=(anywhere,) * 3,
+        scratch_shapes=[
+            pltpu.VMEM((3,) + gradient.shape, F32),
+            pltpu.VMEM((3, 1, size % LANES), F32),
+            pltpu.SemaphoreType.DMA((3, 5)),
+            pltpu.SemaphoreType.DMA((3, 5)),
+        ],
+        compiler_params=pltpu.CompilerParams(vmem_limit_bytes=VMEM_BYTES),
+        name="run_adam",
+    )(gradient, master, first_moment, second_moment)
+
+
+def on_device(tokens, cotangent, holes, slide_lengths, master, first_moment, second_moment):
+    ways = lax.axis_size("seq")
+    output, input_grad, gradient = run_step(
+        tokens[0], cotangent[0], holes, slide_lengths, to_rows(master), ways
+    )
+    new_moment, new_second, new_master = run_adam(gradient, master, first_moment, second_moment)
+    return (output[None], input_grad[None], new_moment, new_second, new_master)
+
+
+def even(mesh):
+    ways = mesh.shape["seq"]
+    return ways % 4 == 0 and MAT_ROWS % (ways * UNIT) == 0 and ways * 8 == LANES
+
+
 def solution(mesh):
     return jax.shard_map(
-        on_device,
+        on_device if even(mesh) else plain_on_device,
         mesh=mesh,
         in_specs=(
             P("grp", "seq", None),

time: 1690 us -> 229 us (0.14); the launches traced: 1660 us -> 229 us
  waiting for transfers between devices: 633 us -> 0 us
  local copies, waits for them, and re-layouts: 505 us -> 1.8 us
  matrix products: 342 us -> 0 us
  Pallas kernels: 0 us -> 227 us
  other arithmetic: 90.9 us -> 0 us
  starting transfers between devices: 52.5 us -> 0 us
  blocking collectives: 21.4 us -> 0 us
    unnamed x6 -> x0, waiting for transfers between devices: 604 us -> none
    dot_general x252 -> x0, matrix products: 342 us -> none  [the longest x116 119 us: contract_cols(): lax.dot_general(left, right, (((1,), (1,)), ((), ())), preferred_element_...]
    pallas_call x0 -> x3, Pallas kernels: none -> 227 us  [the longest x1 218 us: run_step(): pl.pallas_call(partial(step_kernel, ways), out_shape=(jax.ShapeDtypeStruc...]
    unnamed x132 -> x6, local copies, waits for them, and re-layouts: 184 us -> 1.8 us
    slice x15 -> x0, local copies, waits for them, and re-layouts: 123 us -> none  [the longest x3 108 us: joined(): flat[1, start:stop].reshape(shape)]
    all_to_all x9 -> x0, starting transfers between devices: 52.3 us -> none  [the longest x1 7.1 us: on_device(): lax.all_to_all(far_local_lse.reshape(row_count, 1, HEADS).astype(jnp.bflo...]
    dynamic_update_slice x48 -> x0, local copies, waits for them, and re-layouts: 41.8 us -> none  [attend(): lax.map(one_head, (split_heads(packed[:, :D]), split_heads(packed[:, D:2...]
    another operation x23 -> x0, local copies, waits for them, and re-layouts: 41.3 us -> none  [the longest x6 17.7 us: joined(): flat[1, start:stop].reshape(shape)]
  transfers between devices with their start and end apart: 13 -> 0, of which waited for: 5 -> 0; matrix products, arithmetic and copies ran while one was open for 32% -> 0% of each run, Pallas kernels for 0% -> 0%
where the time goes in v2:
time: 229 us
  Pallas kernels  227 us (99%)
    pallas_call x1, Pallas kernels, run_step(): pl.pallas_call(partial(step_kernel, ways), out_shape=(jax.ShapeDtypeStruc...  218 us
    pallas_call x1, Pallas kernels, run_adam(): pl.pallas_call(adam_kernel, out_shape=(jax.ShapeDtypeStruct((1, size), F3...  6.35 us

profile of v2, /device:TPU:0, one launch (start us, length us, event | category | flops | bytes accessed | tf_op | source)
XLA Modules:
  0.0 229.0 jit_solution(10294053172321887114)
XLA Ops:
  0.6 2.1 to_rows.1.flat
  2.7 218.1 %run_step.1 = (bf16[128,768]{1,0:T(8,128)(2,1)}, f32[128,768]{1,0:T(8,128)}, f32[1736,128]{1,0:T(8,128)}) custom-call(bf16[128,768]{1,0:T(8,128)(2,1)} %bitcast.6, bf16[128,768]{1,0:T(8,128)(2,1)} %bitcast.7, s32[1,128]{1,0:T(1,128)} %holes.1, s32[1,8]{1,0:T(1,128)} %lengths.1, f32[1736,128]{1,0:T(8,128)} %to_rows.1.flat), custom_call_target="tpu_custom_call" | custom-call | tf_op jit(solution)/shard_map/run_step/pallas_call | solution.py:1325
  220.8 0.0 copy-start.1
  220.9 6.4 %run_adam.1 = (f32[1,221400]{1,0:T(1,128)}, f32[1,221400]{1,0:T(1,128)}, f32[1,221400]{1,0:T(1,128)}) custom-call(f32[1736,128]{1,0:T(8,128)} %get-tuple-element.13.gradient, f32[1,221400]{1,0:T(1,128)} %master.1, f32[1,221400]{1,0:T(1,128)} %first_moment.1, f32[1,221400]{1,0:T(1,128)} %second_moment.1), custom_call_target="tpu_custom_call" | custom-call | tf_op jit(solution)/shard_map/run_adam/pallas_call | solution.py:1468
  227.2 0.0 copy-start
  227.2 0.0 copy-done.1
  227.2 0.7 copy.14
  227.9 0.4 copy-done
  228.3 0.7 copy.15
Async XLA Ops:
  220.8 6.4 %copy-start.1 = (bf16[128,768]{1,0:T(8,128)(2,1)S(1)}, bf16[128,768]{1,0:T(8,128)(2,1)}, u32[]{:S(2)}) copy-start(bf16[128,768]{1,0:T(8,128)(2,1)} %get-tuple-element.11) | copy-start | bytes 589828
  227.2 1.1 copy-start

commit v3 on v2

--- a/solution.py
+++ b/solution.py
@@ -383,6 +383,8 @@
 MESH = pl.DeviceIdType.MESH
 VMEM_BYTES = 60 * 2**20
 NEG = -1000000000.0
+ORDERS = ((1, 2, 3), (0, 2, 3), (3, 0, 1), (2, 0, 1))
+PIECES = 2
 
 
 def matrix_starts():
@@ -577,7 +579,7 @@
     across = rows // ways
     tiles = D // LANES
     half_width = D // 2
-    third = half_width // LANES
+    third_rows = half_width // LANES
     entries = (MAT_ROWS * LANES + bounds_total()) // ways - own * LANES
     shift = entries * s
     row_shift, lane_shift = shift // LANES, lax.rem(shift, LANES)
@@ -646,11 +648,9 @@
 
     order = [z]
     for step in range(1, planes):
-        listed = [[p for p in ([0] + [q for q in range(at + 1, planes)] + [q for q in range(at - 1, 0, -1)]) if p != at]
-                  for at in range(planes)]
-        plane = jnp.int32(listed[0][step - 1])
+        plane = jnp.int32(ORDERS[0][step - 1])
         for at in range(1, planes):
-            plane = jnp.where(z == at, listed[at][step - 1], plane)
+            plane = jnp.where(z == at, ORDERS[at][step - 1], plane)
         order.append(plane)
 
     def slot_copy(plane, row, column, part, kind, to):
@@ -669,10 +669,11 @@
     def line_down(plane, part):
         return slot_copy(plane, y, x, part, 1, chip(z - 1, y, x))
 
-    def in_plane(plane, part):
-        to_x = slot_copy(plane, y, x, part, 2, chip(z, y, 1 - x))
-        to_y = slot_copy(plane, y, x, part, 3, chip(z, 1 - y, x))
-        return (to_y, to_x) if part == 0 else (to_x, to_y)
+    def to_x(plane, part):
+        return slot_copy(plane, y, x, part, 2, chip(z, y, 1 - x))
+
+    def to_y(plane, part):
+        return slot_copy(plane, y, x, part, 3, chip(z, 1 - y, x))
 
     def turned(plane):
         return (
@@ -681,15 +682,17 @@
         )
 
     def spread_own():
+        to_y(z, 0).start()
+        to_x(z, 1).start()
         for part in range(2):
+            pl.when((z != 1) & (z < planes - 1))(lambda part=part: line_up(z, part).start())
             pl.when(z > 0)(lambda part=part: line_down(z, part).start())
-            pl.when(z == 0)(lambda part=part: line_up(z, part).start())
-            for copy in in_plane(z, part):
-                copy.start()
+        to_x(z, 0).start()
+        to_y(z, 1).start()
 
     def spread_own_up():
         for part in range(2):
-            pl.when((z > 0) & (z < planes - 1))(lambda part=part: line_up(z, part).start())
+            pl.when((z == 1) & (z < planes - 1))(lambda part=part: line_up(z, part).start())
 
     def spread(step):
         plane = order[step]
@@ -697,8 +700,11 @@
             slot_copy(plane, y, x, part, 0, chip(z, y, x)).wait_recv()
             pl.when((z > plane) & (z < planes - 1))(lambda part=part: line_up(plane, part).start())
             pl.when((z < plane) & (z > 0))(lambda part=part: line_down(plane, part).start())
-            for copy in in_plane(plane, part):
-                copy.start()
+            if part == 0:
+                to_y(plane, 0).start()
+        to_x(plane, 1).start()
+        to_x(plane, 0).start()
+        to_y(plane, 1).start()
 
     def turn(step):
         for copy in turned(order[step]):
@@ -733,8 +739,8 @@
                 pl.when((z <= plane) & (z > 0))(
                     lambda part=part, plane=plane: line_down(plane, part).wait_send()
                 )
-                for copy in in_plane(plane, part):
-                    copy.wait_send()
+                to_x(plane, part).wait_send()
+                to_y(plane, part).wait_send()
             for copy in turned(plane):
                 copy.wait_send()
             across_copy(plane).wait_send()
@@ -776,85 +782,117 @@
         small_across().wait_send()
 
 
-    def first_copies(plane):
-        for k in range(2):
-            yield remote(
-                grads.at[part_at(plane, k, 1 - x, 0)], by_x.at[plane, 0, k],
-                x_send.at[plane, 0, k], x_recv.at[plane, 0, k], chip(z, y, 1 - x),
-            )
-            yield remote(
-                grads.at[part_at(plane, 1 - y, k, 1)], by_x.at[plane, 1, k],
-                x_send.at[plane, 1, k], x_recv.at[plane, 1, k], chip(z, 1 - y, x),
-            )
-
-    def first_wait(plane, part, k):
-        remote(
-            by_x.at[plane, part, k], by_x.at[plane, part, k],
-            x_send.at[plane, part, k], x_recv.at[plane, part, k], chip(z, y, x),
-        ).wait_recv()
-
-    def second_copies(plane):
-        yield remote(
-            grads.at[part_at(plane, 1 - y, x, 0)], by_y.at[plane, 0],
-            y_send.at[plane, 0], y_recv.at[plane, 0], chip(z, 1 - y, x),
-        )
-        yield remote(
-            grads.at[part_at(plane, y, 1 - x, 1)], by_y.at[plane, 1],
-            y_send.at[plane, 1], y_recv.at[plane, 1], chip(z, y, 1 - x),
+    piece_rows = half_own // PIECES
+
+    def piece_at(plane, row, column, part, piece):
+        first = ((plane * 2 + row) * 2 + column) * own + part * half_own + piece * piece_rows
+        return pl.ds(pl.multiple_of(first, 16), piece_rows)
+
+    def first_copy(plane, part, k, piece):
+        where = (k, 1 - x) if part == 0 else (1 - y, k)
+        return remote(
+            grads.at[piece_at(plane, *where, part, piece)], by_x.at[plane, part, k, piece],
+            x_send.at[plane, part, k, piece], x_recv.at[plane, part, k, piece],
+            chip(z, y, 1 - x) if part == 0 else chip(z, 1 - y, x),
+        )
+
+    def second_copy(plane, part, piece):
+        where = (1 - y, x) if part == 0 else (y, 1 - x)
+        return remote(
+            grads.at[piece_at(plane, *where, part, piece)], by_y.at[plane, part, piece],
+            y_send.at[plane, part, piece], y_recv.at[plane, part, piece],
+            chip(z, 1 - y, x) if part == 0 else chip(z, y, 1 - x),
+        )
+
+    def line_copy(plane, part, piece, way):
+        return remote(
+            grads.at[piece_at(plane, y, x, part, piece)], by_z.at[way, plane, part, piece],
+            z_send.at[plane, part, piece], z_recv.at[way, plane, part, piece],
+            chip(z + 1 - 2 * way, y, x),
         )
 
     def add(where, block):
         grads[where, :] = (grads[where, :].astype(F32) + block[...].astype(F32)).astype(BF16)
 
+    def each():
+        return [(part, piece) for piece in range(PIECES) for part in range(2)]
+
     def reduce_first(plane):
-        for copy in first_copies(plane):
-            copy.start()
+        for part, piece in each():
+            first_copy(plane, part, (1 - y, 1 - x)[part], piece).start()
+        for part, piece in each():
+            first_copy(plane, part, (y, x)[part], piece).start()
 
     def reduce_second(plane):
-        copies = list(second_copies(plane))
-        for part, other in ((0, 1 - y), (1, 1 - x)):
-            first_wait(plane, part, other)
-            where = part_at(plane, other, x, 0) if part == 0 else part_at(plane, y, other, 1)
-            add(where, by_x.at[plane, part, other])
-            copies[part].start()
-        for part, mine in ((0, y), (1, x)):
-            first_wait(plane, part, mine)
-            add(part_at(plane, y, x, part), by_x.at[plane, part, mine])
-
-    def home_copy(plane, part, step):
-        return remote(
-            grads.at[part_at(plane, y, x, part)], by_z.at[step - 1, part],
-            z_send.at[plane, part], z_recv.at[step - 1, part], chip(plane, y, x),
-        )
+        for part, piece in each():
+            other = (1 - y, 1 - x)[part]
+            first_copy(plane, part, other, piece).wait_recv()
+            where = (other, x) if part == 0 else (y, other)
+            add(piece_at(plane, *where, part, piece), by_x.at[plane, part, other, piece])
+            second_copy(plane, part, piece).start()
+        for part, piece in each():
+            mine = (y, x)[part]
+            first_copy(plane, part, mine, piece).wait_recv()
+            add(piece_at(plane, y, x, part, piece), by_x.at[plane, part, mine, piece])
+
+    def third(plane, part, piece):
+        second_copy(plane, part, piece).wait_recv()
+        add(piece_at(plane, y, x, part, piece), by_y.at[plane, part, piece])
+        if plane > 0:
+            pl.when(z == 0)(lambda: line_copy(plane, part, piece, 0).start())
+        if plane < planes - 1:
+            pl.when(z == planes - 1)(lambda: line_copy(plane, part, piece, 1).start())
+
+    def relay(plane, part, piece):
+        for way in range(2):
+
+            def take(way=way):
+                line_copy(plane, part, piece, way).wait_recv()
+                add(piece_at(plane, y, x, part, piece), by_z.at[way, plane, part, piece])
+                line_copy(plane, part, piece, way).start()
+
+            if way == 0 and plane > 1:
+                pl.when((z > 0) & (z < plane))(take)
+            if way == 1 and plane < planes - 2:
+                pl.when((z > plane) & (z < planes - 1))(take)
 
     def reduce_third(plane):
-        for part, copy in enumerate(second_copies(plane)):
-            copy.wait_recv()
-            add(part_at(plane, y, x, part), by_y.at[plane, part])
-
-            @pl.when(z != plane)
-            def _(part=part):
-                home_copy(plane, part, lax.rem(planes + plane - z, planes)).start()
+        for part, piece in each():
+            third(plane, part, piece)
+
+    def reduce_relay(plane):
+        for part, piece in each():
+            relay(plane, part, piece)
+
+    def reduce_end(plane):
+        for part, piece in each():
+            third(plane, part, piece)
+            relay(plane, part, piece)
 
     def reduce_sent():
         for plane in range(planes):
-            for copy in first_copies(plane):
-                copy.wait_send()
-            for copy in second_copies(plane):
-                copy.wait_send()
-            for part in range(2):
-
-                @pl.when(z != plane)
-                def _(part=part, plane=plane):
-                    home_copy(plane, part, lax.rem(planes + plane - z, planes)).wait_send()
+            for part, piece in each():
+                for k in range(2):
+                    first_copy(plane, part, k, piece).wait_send()
+                second_copy(plane, part, piece).wait_send()
+                pl.when(z != plane)(
+                    lambda plane=plane, part=part, piece=piece: line_copy(
+                        plane, part, piece, 0
+                    ).wait_send()
+                )
 
     def reduce_last():
-        for part in range(2):
-            to = slice(part * half_own, (part + 1) * half_own)
-            total[to, :] = grads[part_at(z, y, x, part), :].astype(F32)
-            for step in range(1, planes):
-                home_copy(z, part, step).wait_recv()
-                total[to, :] += by_z[step - 1, part].astype(F32)
+        for part, piece in each():
+            first = part * half_own + piece * piece_rows
+            to = slice(first, first + piece_rows)
+            total[to, :] = grads[piece_at(z, y, x, part, piece), :].astype(F32)
+            for way in range(2):
+
+                def take(way=way, part=part, piece=piece, to=to):
+                    line_copy(z, part, piece, way).wait_recv()
+                    total[to, :] += by_z[way, z, part, piece].astype(F32)
+
+                pl.when((z > 0) if way == 0 else (z < planes - 1))(take)
 
     def small_home():
         return remote(
@@ -1059,45 +1097,48 @@
     for half in range(2):
         down_grad[half] = upstream[:, half * half_width : (half + 1) * half_width].astype(BF16)
     hand_over("down_grad", down_grad.at[1 - g], their_down)
-    exchanged(0)
+    turn(0)
     spread(1)
     spread_own_up()
+    exchanged(0)
     far_inputs = unpack_values(recv_blocks.at[0])
     far_column = unpack_extra(recv_blocks.at[0])[:, :1]
     far_row = jnp.sum(to_column * far_column, axis=0, keepdims=True)
     near_mask, far_mask = slide_masks(lengths, s, ways, turned_row, far_row)
     masks[0] = near_mask
     masks[1] = far_mask
-    turn(0)
     hat, scale = normalize(jnp.concatenate([inputs, far_inputs], axis=0))
     small_in()
-    gain_one, gain_two = small_row(0, third), small_row(third, third)
-    shift_one, shift_two = small_row(2 * third, third), small_row(3 * third, third)
-    shift_down = small_row(4 * third, third)
-    bias_up = small_row(5 * third, FF // 2 // LANES)
+    gain_one, gain_two = small_row(0, third_rows), small_row(third_rows, third_rows)
+    shift_one, shift_two = small_row(2 * third_rows, third_rows), small_row(3 * third_rows, third_rows)
+    shift_down = small_row(4 * third_rows, third_rows)
+    bias_up = small_row(5 * third_rows, FF // 2 // LANES)
     normed[...] = (hat * gain_one + shift_one).astype(BF16)
     normed_hat[...] = hat[:rows]
     inverse[...] = scale[:rows]
     hand_over("normed", normed, their_normed)
+    finish(0)
+    turn(1)
     spread(2)
-    turn(1)
-    finish(0)
     finish(1)
     spread(3)
+    turn(2)
+    finish(2)
     arrived(0)
     arrived(1)
+    arrived(2)
     for half in range(2):
         for tile, width in tile_groups(0):
             at = half * 3 * half_width + tile * LANES
             projected[:, at : at + width * LANES] = dot(
                 normed[...], weight(whole, 0, half, 0, D, tile, width)
             ).astype(BF16)
+    turn(3)
     attend_set(1, {})
     pack_blocks(send_blocks.at[1], attended[1], lses[1])
     exchange(1)
-    turn(2)
-    attend_set(0, {HEADS // 2: lambda: finish(2)})
-    turn(3)
+    attend_set(0, {})
+    finish(3)
     exchanged(1)
     far_out = unpack_values(recv_blocks.at[1])
     near_out = attended[0]
@@ -1106,11 +1147,9 @@
     difference = near_out - far_out
     mixture[...] = (shares * near_out + (1.0 - shares) * far_out).astype(BF16)
     hand_over("mixture", mixture, their_mixture)
-    finish(3)
-    arrived(2)
     arrived(3)
     middle = inputs + jnp.concatenate(
-        [dot(mixture[...], weight(whole, 1, half, 0, D, 0, third)) for half in range(2)], axis=1
+        [dot(mixture[...], weight(whole, 1, half, 0, D, 0, third_rows)) for half in range(2)], axis=1
     )
     hat, scale = normalize(middle)
     second_hat[...] = hat
@@ -1136,7 +1175,7 @@
     for start in range(0, FF, block):
         to = slice(start, start + block)
         pulled = sum(
-            dot_cols(down_grad[half], weight(whole, 3, half, start, block, 0, third))
+            dot_cols(down_grad[half], weight(whole, 3, half, start, block, 0, third_rows))
             for half in range(2)
         )
         grad = (pulled * slope[:, to]).astype(BF16)
@@ -1170,7 +1209,7 @@
     mix_grad = jnp.concatenate(
         [
             sum(
-                dot_cols(out_grad[half], weight(whole, 1, half, start, block, 0, third))
+                dot_cols(out_grad[half], weight(whole, 1, half, start, block, 0, third_rows))
                 for half in range(2)
             )
             for start in range(0, D, block)
@@ -1189,21 +1228,19 @@
     pairs["mixture"].wait()
     pairs["out_grad"].wait()
     weight_grad(1, mixture, their_mixture, out_grad, their_out, 0, D)
-    reduce_first(1)
+    result = middle + shift_down + jnp.concatenate(
+        [dot(activated[...], weight(whole, 3, half, 0, FF, 0, third_rows)) for half in range(2)], axis=1
+    )
+    output[...] = in_order(result).astype(BF16)
+
+    attend_set_back(0, near_grad, {})
     reduce_second(3)
-    result = middle + shift_down + jnp.concatenate(
-        [dot(activated[...], weight(whole, 3, half, 0, FF, 0, third)) for half in range(2)], axis=1
-    )
-    output[...] = in_order(result).astype(BF16)
-
-    attend_set_back(0, near_grad, {HEADS // 2: lambda: reduce_third(3)})
-    reduce_second(2)
     exchanged(2)
     far_grad[...] = unpack_values(recv_blocks.at[2]).astype(BF16)
     lse_grads[1] = unpack_extra(recv_blocks.at[2])
-    attend_set_back(1, far_grad, {HEADS // 2: lambda: reduce_third(2)})
+    attend_set_back(1, far_grad, {})
     hand_over("qkv_grad", qkv_grad.at[1 - g], their_qkv)
-    reduce_second(1)
+    reduce_second(2)
     first_grad = jnp.concatenate(
         [
             sum(
@@ -1220,8 +1257,10 @@
     pairs["qkv_grad"].wait()
     weight_grad(0, normed, their_normed, qkv_grad, their_qkv, 0, D)
     reduce_first(0)
-    reduce_third(1)
-
+    reduce_third(3)
+    reduce_first(1)
+    reduce_relay(3)
+    reduce_third(2)
     exchanged(3)
     first_grad = first_grad[:rows] + unpack_values(recv_blocks.at[3])
     hat = normed_hat[...]
@@ -1251,7 +1290,11 @@
     small_parts[g] = small_parts[g] + their_small[...]
     pl.when(s != ways - 1)(lambda: small_home().start())
     reduce_second(0)
+    reduce_relay(2)
+    reduce_second(1)
     reduce_third(0)
+    reduce_relay(0)
+    reduce_end(1)
     reduce_last()
     settle()
     pl.when(s != ways - 1)(lambda: small_home().wait_send())
@@ -1314,9 +1357,9 @@
         ((rows, half), BF16),
         ((2, SMALL_ROWS, LANES), F32),
         ((SMALL_ROWS, LANES), F32),
-        ((planes, 2, 2, half_own, LANES), BF16),
-        ((planes, 2, half_own, LANES), BF16),
-        ((planes - 1, 2, half_own, LANES), BF16),
+        ((planes, 2, 2, PIECES, half_own // PIECES, LANES), BF16),
+        ((planes, 2, PIECES, half_own // PIECES, LANES), BF16),
+        ((2, planes, 2, PIECES, half_own // PIECES, LANES), BF16),
         ((own, LANES), F32),
         ((own + 2 * SMALL_ROWS, LANES), F32),
         ((SMALL_ROWS, LANES), F32),
@@ -1340,9 +1383,9 @@
             dma((planes,)), dma((planes,)),
             dma((ways,)), dma((2,)),
             dma((4,)), dma((4,)), dma((9,)), dma((9,)),
-            dma((planes, 2, 2)), dma((planes, 2, 2)),
-            dma((planes, 2)), dma((planes, 2)),
-            dma((planes, 2)), dma((planes - 1, 2)),
+            dma((planes, 2, 2, PIECES)), dma((planes, 2, 2, PIECES)),
+            dma((planes, 2, PIECES)), dma((planes, 2, PIECES)),
+            dma((planes, 2, PIECES)), dma((2, planes, 2, PIECES)),
             dma((2,)), dma((2,)),
         ],
         compiler_params=pltpu.CompilerParams(

time: 229 us -> 191 us (0.83)
  the two profiles are of different devices: /device:TPU:0 before, /device:TPU:12 now
where the time goes in v3:
time: 191 us; the launch traced here: 190 us
  Pallas kernels  188 us (98%)
    pallas_call x1, Pallas kernels, run_step(): pl.pallas_call(partial(step_kernel, ways), out_shape=(jax.ShapeDtypeStruc...  179 us
    pallas_call x1, Pallas kernels, run_adam(): pl.pallas_call(adam_kernel, out_shape=(jax.ShapeDtypeStruct((1, size), F3...  6.35 us

profile of v3, /device:TPU:12, one launch (start us, length us, event | category | flops | bytes accessed | tf_op | source)
XLA Modules:
  0.0 190.3 jit_solution(12883706511198695084)
XLA Ops:
  0.6 2.1 %to_rows.1.flat = f32[1736,128]{1,0:T(8,128)} custom-call(f32[1,221400]{1,0:T(1,128)} %master.1), custom_call_target="tpu_custom_call" | custom-call | tf_op jit(solution)/shard_map/to_rows/pallas_call | solution.py:1414
  2.7 179.3 %run_step.1 = (bf16[128,768]{1,0:T(8,128)(2,1)}, f32[128,768]{1,0:T(8,128)}, f32[1736,128]{1,0:T(8,128)}) custom-call(bf16[128,768]{1,0:T(8,128)(2,1)} %bitcast.6, bf16[128,768]{1,0:T(8,128)(2,1)} %bitcast.7, s32[1,128]{1,0:T(1,128)} %holes.1, s32[1,8]{1,0:T(1,128)} %lengths.1, f32[1736,128]{1,0:T(8,128)} %to_rows.1.flat), custom_call_target="tpu_custom_call" | custom-call | tf_op jit(solution)/shard_map/run_step/pallas_call | solution.py:1368
  182.1 0.0 copy-start.1
  182.1 6.4 %run_adam.1 = (f32[1,221400]{1,0:T(1,128)}, f32[1,221400]{1,0:T(1,128)}, f32[1,221400]{1,0:T(1,128)}) custom-call(f32[1736,128]{1,0:T(8,128)} %get-tuple-element.13.gradient, f32[1,221400]{1,0:T(1,128)} %master.1, f32[1,221400]{1,0:T(1,128)} %first_moment.1, f32[1,221400]{1,0:T(1,128)} %second_moment.1), custom_call_target="tpu_custom_call" | custom-call | tf_op jit(solution)/shard_map/run_adam/pallas_call | solution.py:1511
  188.4 0.0 copy-start
  188.4 0.0 copy-done.1
  188.5 0.7 copy.14
  189.1 0.4 copy-done
  189.5 0.7 copy.15
Async XLA Ops:
  182.1 6.4 %copy-start.1 = (bf16[128,768]{1,0:T(8,128)(2,1)S(1)}, bf16[128,768]{1,0:T(8,128)(2,1)}, u32[]{:S(2)}) copy-start(bf16[128,768]{1,0:T(8,128)(2,1)} %get-tuple-element.11) | copy-start | bytes 589828
  188.4 1.1 copy-start

commit v4 on v3

--- a/solution.py
+++ b/solution.py
@@ -1,4 +1,5 @@
 from functools import partial
+from types import SimpleNamespace
 
 import jax
 import jax.numpy as jnp
@@ -383,8 +384,10 @@
 MESH = pl.DeviceIdType.MESH
 VMEM_BYTES = 60 * 2**20
 NEG = -1000000000.0
-ORDERS = ((1, 2, 3), (0, 2, 3), (3, 0, 1), (2, 0, 1))
+ORDERS = ((1, 2, 3), (0, 2, 3), (0, 3, 1), (0, 2, 1))
 PIECES = 2
+LATE_ROWS = 160
+LATE_OUT = (64, 128, 192, 192)
 
 
 def matrix_starts():
@@ -565,10 +568,10 @@
     qkv_grad, out_grad, up_grad, down_grad, near_grad, far_grad, lse_grads,
     their_normed, their_mixture, their_second, their_activated,
     their_qkv, their_out, their_up, their_down, small_parts, their_small,
-    by_x, by_y, by_z, total, laid, follow_rows, small_all,
-    tail_sem, slot_send, slot_recv, core_send, core_recv, small_send, small_recv,
+    by_x, by_y, by_z, by_late, total, laid, follow_rows, small_all,
+    tail_sem, slot_send, slot_recv, late_send, late_recv, core_send, core_recv, small_send, small_recv,
     block_send, block_recv, pair_send, pair_recv,
-    x_send, x_recv, y_send, y_recv, z_send, z_recv, end_sem, sum_sem,
+    x_send, x_recv, y_send, y_recv, z_send, z_recv, late_out_send, late_out_recv, end_sem, sum_sem,
 ):
     s, g = place()
     planes = ways // 4
@@ -593,11 +596,7 @@
 
 
     last_row, last_lanes = divmod(own * LANES + entries, LANES)
-
-    def take_flat():
-        end = SMALL_ROWS + flat.shape[0]
-        extended[SMALL_ROWS:end, :] = flat[...]
-        extended[end:, :] = jnp.zeros((extended.shape[0] - end, LANES), F32)
+    step_rows = 176
 
     def follow_copy():
         return remote(
@@ -614,22 +613,20 @@
         follow_copy().start()
 
     def align_own():
-        follow_copy().wait()
-        step_rows = 176
-        step_lanes = lax.broadcasted_iota(jnp.int32, (step_rows, LANES), 1)
-
-        def align(step, carry):
-            start = step * step_rows
-            here = extended[pl.ds(SMALL_ROWS + start - row_shift, step_rows), :]
-            before = extended[pl.ds(SMALL_ROWS - 1 + start - row_shift, step_rows), :]
-            aligned[pl.ds(pl.multiple_of(start, 8), step_rows), :] = jnp.where(
-                step_lanes >= lane_shift,
+        lanes = lax.broadcasted_iota(jnp.int32, (step_rows, LANES), 1)
+
+        def align(source, start, to):
+            here = source[pl.ds(start - row_shift, step_rows), :]
+            before = source[pl.ds(start - row_shift - 1, step_rows), :]
+            aligned[pl.ds(pl.multiple_of(to, 8), step_rows), :] = jnp.where(
+                lanes >= lane_shift,
                 pltpu.roll(here, lane_shift, 1),
                 pltpu.roll(before, lane_shift, 1),
             )
+
+        def align_step(step, carry):
+            align(flat, step * step_rows, step * step_rows)
             return carry
-
-        lax.fori_loop(0, (own + SMALL_ROWS) // step_rows, align, 0)
 
         def fill(unit, carry):
             first = unit * UNIT
@@ -644,7 +641,12 @@
             unit_tiles(s * (own // UNIT) + unit, tiled)
             return carry
 
-        lax.fori_loop(0, own // UNIT, fill, 0)
+        extended[SMALL_ROWS:, :] = flat[: extended.shape[0] - SMALL_ROWS, :]
+        lax.fori_loop(1, (own + SMALL_ROWS) // step_rows, align_step, 0)
+        lax.fori_loop(1, own // UNIT, fill, 0)
+        follow_copy().wait()
+        align(extended, SMALL_ROWS, 0)
+        fill(0, 0)
 
     order = [z]
     for step in range(1, planes):
@@ -653,97 +655,164 @@
             plane = jnp.where(z == at, ORDERS[at][step - 1], plane)
         order.append(plane)
 
-    def slot_copy(plane, row, column, part, kind, to):
-        where = whole.at[g, part_at(plane, row, column, part)]
+    part_rows = half_own - LATE_ROWS
+    late = PIECES
+
+    def slot_copy(plane, row, column, part, piece, kind, to):
+        if piece == late:
+            first, count = 2 * part_rows + part * LATE_ROWS, LATE_ROWS
+        else:
+            count = part_rows // PIECES
+            first = part * part_rows + piece * count
+        first = ((plane * 2 + row) * 2 + column) * own + first
+        where = whole.at[g, pl.ds(pl.multiple_of(first, 16), count)]
         return remote(
             where,
             where,
-            slot_send.at[part, plane, kind],
-            slot_recv.at[part, (plane * 2 + row) * 2 + column],
+            slot_send.at[part, plane, kind, piece],
+            slot_recv.at[part, (plane * 2 + row) * 2 + column, piece],
             to,
         )
 
-    def line_up(plane, part):
-        return slot_copy(plane, y, x, part, 0, chip(z + 1, y, x))
-
-    def line_down(plane, part):
-        return slot_copy(plane, y, x, part, 1, chip(z - 1, y, x))
-
-    def to_x(plane, part):
-        return slot_copy(plane, y, x, part, 2, chip(z, y, 1 - x))
-
-    def to_y(plane, part):
-        return slot_copy(plane, y, x, part, 3, chip(z, 1 - y, x))
-
-    def turned(plane):
+    def line_up(plane, part, piece):
+        return slot_copy(plane, y, x, part, piece, 0, chip(z + 1, y, x))
+
+    def line_down(plane, part, piece):
+        return slot_copy(plane, y, x, part, piece, 1, chip(z - 1, y, x))
+
+    def to_x(plane, part, piece):
+        return slot_copy(plane, y, x, part, piece, 2, chip(z, y, 1 - x))
+
+    def to_y(plane, part, piece):
+        return slot_copy(plane, y, x, part, piece, 3, chip(z, 1 - y, x))
+
+    def early(plane, piece):
+        to_y(plane, 0, piece).start()
+        to_x(plane, 1, piece).start()
+
+    def direct(plane, piece):
+        to_x(plane, 0, piece).start()
+        to_y(plane, 1, piece).start()
+
+    def turned(plane, piece):
         return (
-            slot_copy(plane, 1 - y, x, 0, 4, chip(z, y, 1 - x)),
-            slot_copy(plane, y, 1 - x, 1, 4, chip(z, 1 - y, x)),
-        )
-
-    def spread_own():
-        to_y(z, 0).start()
-        to_x(z, 1).start()
-        for part in range(2):
-            pl.when((z != 1) & (z < planes - 1))(lambda part=part: line_up(z, part).start())
-            pl.when(z > 0)(lambda part=part: line_down(z, part).start())
-        to_x(z, 0).start()
-        to_y(z, 1).start()
-
-    def spread_own_up():
-        for part in range(2):
-            pl.when((z == 1) & (z < planes - 1))(lambda part=part: line_up(z, part).start())
-
-    def spread(step):
-        plane = order[step]
-        for part in range(2):
-            slot_copy(plane, y, x, part, 0, chip(z, y, x)).wait_recv()
-            pl.when((z > plane) & (z < planes - 1))(lambda part=part: line_up(plane, part).start())
-            pl.when((z < plane) & (z > 0))(lambda part=part: line_down(plane, part).start())
-            if part == 0:
-                to_y(plane, 0).start()
-        to_x(plane, 1).start()
-        to_x(plane, 0).start()
-        to_y(plane, 1).start()
-
-    def turn(step):
-        for copy in turned(order[step]):
+            slot_copy(plane, 1 - y, x, 0, piece, 4, chip(z, y, 1 - x)),
+            slot_copy(plane, y, 1 - x, 1, piece, 4, chip(z, 1 - y, x)),
+        )
+
+    def turn_piece(plane, piece):
+        for copy in turned(plane, piece):
             copy.wait_recv()
             copy.start()
 
-    def across_copy(plane):
-        block = whole.at[g, pl.ds(pl.multiple_of(plane * 4 * own, 16), 4 * own)]
-        return remote(block, block, core_send.at[plane], core_recv.at[plane], (s, 1 - g))
-
-    def across_recv(plane):
-        block = whole.at[1 - g, pl.ds(pl.multiple_of(plane * 4 * own, 16), 4 * own)]
-        return remote(block, block, core_send.at[plane], core_recv.at[plane], (s, 1 - g))
-
-    def finish(step):
-        plane = order[step]
-        slot_copy(plane, y, 1 - x, 0, 0, chip(z, y, x)).wait_recv()
-        slot_copy(plane, 1 - y, 1 - x, 0, 0, chip(z, y, x)).wait_recv()
-        slot_copy(plane, 1 - y, x, 1, 0, chip(z, y, x)).wait_recv()
-        slot_copy(plane, 1 - y, 1 - x, 1, 0, chip(z, y, x)).wait_recv()
-        across_copy(plane).start()
-
-    def arrived(step):
-        across_recv(order[step]).wait_recv()
+    def come(plane, piece):
+        slot_copy(plane, y, 1 - x, 0, piece, 0, chip(z, y, x)).wait_recv()
+        slot_copy(plane, 1 - y, 1 - x, 0, piece, 0, chip(z, y, x)).wait_recv()
+        slot_copy(plane, 1 - y, x, 1, piece, 0, chip(z, y, x)).wait_recv()
+        slot_copy(plane, 1 - y, 1 - x, 1, piece, 0, chip(z, y, x)).wait_recv()
+
+    def leave(piece, plane_one):
+        for part in range(2):
+
+            def up(part=part):
+                line_up(z, part, piece).start()
+
+            def down(part=part):
+                line_down(z, part, piece).start()
+
+            if plane_one:
+                pl.when((z == 1) & (z < planes - 1))(up)
+            else:
+                pl.when((z != 1) & (z < planes - 1))(up)
+                pl.when(z > 0)(down)
+
+    def enter_plane(plane, piece):
+        for part in range(2):
+            slot_copy(plane, y, x, part, piece, 0, chip(z, y, x)).wait_recv()
+
+            def up(part=part):
+                line_up(plane, part, piece).start()
+
+            def down(part=part):
+                line_down(plane, part, piece).start()
+
+            pl.when((z > plane) & (z < planes - 1))(up)
+            pl.when((z < plane) & (z > 0))(down)
+
+    def late_copy(plane, part, way):
+        view = whole.reshape(2, ways, own, LANES)
+        where = view.at[
+            g, pl.ds(4 * plane, 4), pl.ds(2 * part_rows + part * LATE_ROWS, LATE_ROWS)
+        ]
+        return remote(
+            where, where, late_send.at[way, plane, part], late_recv.at[plane, part],
+            chip(z + 1 - 2 * way, y, x),
+        )
+
+    def late_own():
+        come(z, late)
+        for part in range(2):
+            pl.when(z < planes - 1)(lambda part=part: late_copy(z, part, 0).start())
+            pl.when(z > 0)(lambda part=part: late_copy(z, part, 1).start())
+
+    def late_on(plane):
+        for part in range(2):
+            late_copy(plane, part, 0).wait_recv()
+            pl.when((z > plane) & (z < planes - 1))(
+                lambda part=part: late_copy(plane, part, 0).start()
+            )
+            pl.when((z < plane) & (z > 0))(lambda part=part: late_copy(plane, part, 1).start())
+
+    def to_core(half, plane, part, piece):
+        count = LATE_ROWS if piece == late else part_rows // PIECES
+        first = 2 * part_rows + part * count if piece == late else part * part_rows + piece * count
+        view = whole.reshape(2, ways, own, LANES)
+        where = view.at[half, pl.ds(4 * plane, 4), pl.ds(first, count)]
+        return remote(
+            where, where, core_send.at[plane, part, piece], core_recv.at[plane, part, piece],
+            (s, 1 - g),
+        )
+
+    def finish(plane, piece):
+        if piece != late:
+            come(plane, piece)
+        for part in range(2):
+            to_core(g, plane, part, piece).start()
+
+    def arrived(plane):
+        for part in range(2):
+            for piece in range(PIECES + 1):
+                to_core(1 - g, plane, part, piece).wait_recv()
 
     def gather_sent():
         for plane in range(planes):
             for part in range(2):
+                for piece in range(PIECES):
+
+                    def up(plane=plane, part=part, piece=piece):
+                        line_up(plane, part, piece).wait_send()
+
+                    def down(plane=plane, part=part, piece=piece):
+                        line_down(plane, part, piece).wait_send()
+
+                    pl.when((z >= plane) & (z < planes - 1))(up)
+                    pl.when((z <= plane) & (z > 0))(down)
+                    to_x(plane, part, piece).wait_send()
+                    to_y(plane, part, piece).wait_send()
+                    turned(plane, piece)[part].wait_send()
+                to_own = (to_x(z, part, late), to_y(z, part, late), turned(z, late)[part])
+                if plane == 0:
+                    for copy in to_own:
+                        copy.wait_send()
                 pl.when((z >= plane) & (z < planes - 1))(
-                    lambda part=part, plane=plane: line_up(plane, part).wait_send()
+                    lambda plane=plane, part=part: late_copy(plane, part, 0).wait_send()
                 )
                 pl.when((z <= plane) & (z > 0))(
-                    lambda part=part, plane=plane: line_down(plane, part).wait_send()
+                    lambda plane=plane, part=part: late_copy(plane, part, 1).wait_send()
                 )
-                to_x(plane, part).wait_send()
-                to_y(plane, part).wait_send()
-            for copy in turned(plane):
-                copy.wait_send()
-            across_copy(plane).wait_send()
+            for part in range(2):
+                for piece in range(PIECES + 1):
+                    to_core(g, plane, part, piece).wait_send()
 
     def small_to(index):
         return remote(small.at[g], small.at[g], small_send.at[index], small_recv.at[0], (index, g))
@@ -782,16 +851,25 @@
         small_across().wait_send()
 
 
-    piece_rows = half_own // PIECES
+    def cut(plane, part, piece):
+        if piece == late:
+            return 2 * (half_own - LATE_OUT[plane]) + part * LATE_OUT[plane], LATE_OUT[plane]
+        count = (half_own - LATE_OUT[plane]) // PIECES
+        return part * (half_own - LATE_OUT[plane]) + piece * count, count
 
     def piece_at(plane, row, column, part, piece):
-        first = ((plane * 2 + row) * 2 + column) * own + part * half_own + piece * piece_rows
-        return pl.ds(pl.multiple_of(first, 16), piece_rows)
+        first, count = cut(plane, part, piece)
+        first = ((plane * 2 + row) * 2 + column) * own + first
+        return pl.ds(pl.multiple_of(first, 16), count)
+
+    def held(ref, plane, part, piece):
+        return ref.at[pl.ds(0, cut(plane, part, piece)[1])]
 
     def first_copy(plane, part, k, piece):
         where = (k, 1 - x) if part == 0 else (1 - y, k)
         return remote(
-            grads.at[piece_at(plane, *where, part, piece)], by_x.at[plane, part, k, piece],
+            grads.at[piece_at(plane, *where, part, piece)],
+            held(by_x.at[plane, part, k, piece], plane, part, piece),
             x_send.at[plane, part, k, piece], x_recv.at[plane, part, k, piece],
             chip(z, y, 1 - x) if part == 0 else chip(z, 1 - y, x),
         )
@@ -799,127 +877,218 @@
     def second_copy(plane, part, piece):
         where = (1 - y, x) if part == 0 else (y, 1 - x)
         return remote(
-            grads.at[piece_at(plane, *where, part, piece)], by_y.at[plane, part, piece],
+            grads.at[piece_at(plane, *where, part, piece)],
+            held(by_y.at[plane, part, piece], plane, part, piece),
             y_send.at[plane, part, piece], y_recv.at[plane, part, piece],
             chip(z, 1 - y, x) if part == 0 else chip(z, y, 1 - x),
         )
 
     def line_copy(plane, part, piece, way):
         return remote(
-            grads.at[piece_at(plane, y, x, part, piece)], by_z.at[way, plane, part, piece],
+            grads.at[piece_at(plane, y, x, part, piece)],
+            held(by_z.at[way, plane, part, piece], plane, part, piece),
             z_send.at[plane, part, piece], z_recv.at[way, plane, part, piece],
             chip(z + 1 - 2 * way, y, x),
         )
 
+    def late_out_copy(plane, part, way):
+        first, count = cut(plane, part, late)
+        view = grads.reshape(ways, own, LANES)
+        return remote(
+            view.at[pl.ds(4 * plane, 4), pl.ds(first, count)],
+            by_late.at[way, plane, part, :, pl.ds(0, count)],
+            late_out_send.at[plane, part], late_out_recv.at[way, plane, part],
+            chip(z + 1 - 2 * way, y, x),
+        )
+
     def add(where, block):
         grads[where, :] = (grads[where, :].astype(F32) + block[...].astype(F32)).astype(BF16)
 
-    def each():
-        return [(part, piece) for piece in range(PIECES) for part in range(2)]
-
-    def reduce_first(plane):
-        for part, piece in each():
-            first_copy(plane, part, (1 - y, 1 - x)[part], piece).start()
-        for part, piece in each():
-            first_copy(plane, part, (y, x)[part], piece).start()
-
-    def reduce_second(plane):
-        for part, piece in each():
-            other = (1 - y, 1 - x)[part]
-            first_copy(plane, part, other, piece).wait_recv()
-            where = (other, x) if part == 0 else (y, other)
-            add(piece_at(plane, *where, part, piece), by_x.at[plane, part, other, piece])
-            second_copy(plane, part, piece).start()
-        for part, piece in each():
-            mine = (y, x)[part]
-            first_copy(plane, part, mine, piece).wait_recv()
-            add(piece_at(plane, y, x, part, piece), by_x.at[plane, part, mine, piece])
-
-    def third(plane, part, piece):
-        second_copy(plane, part, piece).wait_recv()
-        add(piece_at(plane, y, x, part, piece), by_y.at[plane, part, piece])
-        if plane > 0:
-            pl.when(z == 0)(lambda: line_copy(plane, part, piece, 0).start())
-        if plane < planes - 1:
-            pl.when(z == planes - 1)(lambda: line_copy(plane, part, piece, 1).start())
-
-    def relay(plane, part, piece):
-        for way in range(2):
-
-            def take(way=way):
+    def at_home(plane, piece, act):
+        if piece == late:
+            pl.when(z == plane)(act)
+        else:
+            act()
+
+    def out_ahead(plane, piece):
+        def act():
+            for part in range(2):
+                first_copy(plane, part, (1 - y, 1 - x)[part], piece).start()
+
+        at_home(plane, piece, act)
+
+    def out_keep(plane, piece):
+        def act():
+            for part in range(2):
+                first_copy(plane, part, (y, x)[part], piece).start()
+
+        at_home(plane, piece, act)
+
+    def out_pass(plane, piece):
+        def act():
+            for part in range(2):
+                other = (1 - y, 1 - x)[part]
+                first_copy(plane, part, other, piece).wait_recv()
+                where = (other, x) if part == 0 else (y, other)
+                add(
+                    piece_at(plane, *where, part, piece),
+                    held(by_x.at[plane, part, other, piece], plane, part, piece),
+                )
+                second_copy(plane, part, piece).start()
+
+        at_home(plane, piece, act)
+
+    def out_take(plane, piece):
+        def act():
+            for part in range(2):
+                mine = (y, x)[part]
+                first_copy(plane, part, mine, piece).wait_recv()
+                add(
+                    piece_at(plane, y, x, part, piece),
+                    held(by_x.at[plane, part, mine, piece], plane, part, piece),
+                )
+
+        at_home(plane, piece, act)
+
+    def out_join(plane, piece):
+        def act():
+            for part in range(2):
+                second_copy(plane, part, piece).wait_recv()
+                add(
+                    piece_at(plane, y, x, part, piece),
+                    held(by_y.at[plane, part, piece], plane, part, piece),
+                )
+                if piece != late and plane > 0:
+                    pl.when(z == 0)(lambda part=part: line_copy(plane, part, piece, 0).start())
+                if piece != late and plane < planes - 1:
+                    pl.when(z == planes - 1)(
+                        lambda part=part: line_copy(plane, part, piece, 1).start()
+                    )
+
+        at_home(plane, piece, act)
+
+    def between(plane, act):
+        if plane > 1:
+            pl.when((z > 0) & (z < plane))(lambda: act(0))
+        if plane < planes - 2:
+            pl.when((z > plane) & (z < planes - 1))(lambda: act(1))
+
+    def out_relay(plane, piece):
+        for part in range(2):
+
+            def act(way, part=part):
                 line_copy(plane, part, piece, way).wait_recv()
-                add(piece_at(plane, y, x, part, piece), by_z.at[way, plane, part, piece])
+                add(
+                    piece_at(plane, y, x, part, piece),
+                    held(by_z.at[way, plane, part, piece], plane, part, piece),
+                )
                 line_copy(plane, part, piece, way).start()
 
-            if way == 0 and plane > 1:
-                pl.when((z > 0) & (z < plane))(take)
-            if way == 1 and plane < planes - 2:
-                pl.when((z > plane) & (z < planes - 1))(take)
-
-    def reduce_third(plane):
-        for part, piece in each():
-            third(plane, part, piece)
-
-    def reduce_relay(plane):
-        for part, piece in each():
-            relay(plane, part, piece)
-
-    def reduce_end(plane):
-        for part, piece in each():
-            third(plane, part, piece)
-            relay(plane, part, piece)
-
-    def reduce_sent():
+            between(plane, act)
+
+    def late_add(plane, part, way):
+        late_out_copy(plane, part, way).wait_recv()
+        for k in range(4):
+            add(
+                piece_at(plane, k // 2, k % 2, part, late),
+                by_late.at[way, plane, part, k, pl.ds(0, LATE_OUT[plane])],
+            )
+
+    def late_start(plane):
+        for part in range(2):
+            if plane > 0:
+                pl.when(z == 0)(lambda part=part: late_out_copy(plane, part, 0).start())
+            if plane < planes - 1:
+                pl.when(z == planes - 1)(lambda part=part: late_out_copy(plane, part, 1).start())
+
+    def late_relay(plane):
+        for part in range(2):
+
+            def act(way, part=part):
+                late_add(plane, part, way)
+                late_out_copy(plane, part, way).start()
+
+            between(plane, act)
+
+    def late_home(plane):
+        @pl.when(z == plane)
+        def _():
+            for part in range(2):
+                if plane > 0:
+                    late_add(plane, part, 0)
+                if plane < planes - 1:
+                    late_add(plane, part, 1)
+
+    def out_sent():
         for plane in range(planes):
-            for part, piece in each():
-                for k in range(2):
-                    first_copy(plane, part, k, piece).wait_send()
-                second_copy(plane, part, piece).wait_send()
-                pl.when(z != plane)(
-                    lambda plane=plane, part=part, piece=piece: line_copy(
-                        plane, part, piece, 0
-                    ).wait_send()
-                )
-
-    def reduce_last():
-        for part, piece in each():
-            first = part * half_own + piece * piece_rows
-            to = slice(first, first + piece_rows)
-            total[to, :] = grads[piece_at(z, y, x, part, piece), :].astype(F32)
-            for way in range(2):
-
-                def take(way=way, part=part, piece=piece, to=to):
-                    line_copy(z, part, piece, way).wait_recv()
-                    total[to, :] += by_z[way, z, part, piece].astype(F32)
-
-                pl.when((z > 0) if way == 0 else (z < planes - 1))(take)
+            for piece in range(PIECES + (1 if LATE_OUT[plane] else 0)):
+
+                def act(plane=plane, piece=piece):
+                    for part in range(2):
+                        for k in range(2):
+                            first_copy(plane, part, k, piece).wait_send()
+                        second_copy(plane, part, piece).wait_send()
+
+                at_home(plane, piece, act)
+
+            @pl.when(z != plane)
+            def _(plane=plane):
+                for part in range(2):
+                    for piece in range(PIECES):
+                        line_copy(plane, part, piece, 0).wait_send()
+                    if LATE_OUT[plane]:
+                        late_out_copy(plane, part, 0).wait_send()
+
+    def out_last(parts):
+        for plane in range(planes):
+
+            @pl.when(z == plane)
+            def _(plane=plane):
+                for part, piece in parts:
+                    first, count = cut(plane, part, piece)
+                    if not count:
+                        continue
+                    found = grads[piece_at(plane, y, x, part, piece), :].astype(F32)
+                    for way in range(2):
+                        if piece != late and (plane > 0 if way == 0 else plane < planes - 1):
+                            line_copy(plane, part, piece, way).wait_recv()
+                            found = found + by_z[way, plane, part, piece, :count].astype(F32)
+                    total[first : first + count, :] = found
 
     def small_home():
         return remote(
             small_parts.at[g], small_all.at[s], sum_sem.at[0], sum_sem.at[1], (ways - 1, g)
         )
 
+    def lay_group(first, group, count):
+        for tile in range(count):
+            block = total[pl.ds(pl.multiple_of(first + 16 * (group * count + tile), 16), 16), :]
+            laid[pl.ds(first + group * 16 * count + tile, 16, stride=count), :] = block
+
+    def follow_back():
+        return remote(
+            laid.at[pl.ds(0, SMALL_ROWS)], follow_rows, end_sem.at[0], end_sem.at[1],
+            (lax.rem(s + ways - 1, ways), g),
+        )
+
+    def settle_first():
+        unit_tiles(s * (own // UNIT), lambda count: lay_group(0, 0, count))
+        follow_back().start()
+
     def settle():
         def lay(unit, carry):
-            first = unit * UNIT
-
             def tiled(count):
-                for group in range(UNIT // (16 * count)):
-                    for tile in range(count):
-                        block = total[
-                            pl.ds(pl.multiple_of(first + 16 * (group * count + tile), 16), 16), :
-                        ]
-                        laid[pl.ds(first + group * 16 * count + tile, 16, stride=count), :] = block
+                for group in range(1, UNIT // (16 * count)):
+                    lay_group(unit * UNIT, group, count)
+
+            def first_group(count):
+                lay_group(unit * UNIT, 0, count)
 
             unit_tiles(s * (own // UNIT) + unit, tiled)
+            pl.when(unit > 0)(lambda: unit_tiles(s * (own // UNIT) + unit, first_group))
             return carry
 
         lax.fori_loop(0, own // UNIT, lay, 0)
-        follow = remote(
-            laid.at[pl.ds(0, SMALL_ROWS)], follow_rows, end_sem.at[0], end_sem.at[1],
-            (lax.rem(s + ways - 1, ways), g),
-        )
-        follow.start()
 
         @pl.when(s == ways - 1)
         def _():
@@ -931,7 +1100,7 @@
             laid[own : own + SMALL_ROWS, :] = jnp.sum(small_all[...], axis=0)
 
         laid[own + SMALL_ROWS :, :] = jnp.zeros((laid.shape[0] - own - SMALL_ROWS, LANES), F32)
-        follow.wait()
+        follow_back().wait()
 
         @pl.when(s != ways - 1)
         def _():
@@ -953,12 +1122,16 @@
         lax.fori_loop(0, flat_grad.shape[0] // step_rows, align, 0)
 
 
+    widths = (half_width + LANES,) * 3 + (half_width,)
+
     def exchange(index):
+        width = widths[index]
+
         def start(step, carry):
             to = lax.rem(s + step, ways)
             remote(
-                send_blocks.at[index, to],
-                recv_blocks.at[index, s],
+                send_blocks.at[index, to, :, pl.ds(0, width)],
+                recv_blocks.at[index, s, :, pl.ds(0, width)],
                 block_send.at[index],
                 block_recv.at[index],
                 (to, g),
@@ -969,20 +1142,22 @@
         lax.fori_loop(1, ways, start, 0)
 
     def exchanged(index):
+        width = widths[index]
         remote(
-            send_blocks.at[index, pl.ds(0, ways - 1)],
-            recv_blocks.at[index, pl.ds(0, ways - 1)],
+            send_blocks.at[index, pl.ds(0, ways - 1), :, pl.ds(0, width)],
+            recv_blocks.at[index, pl.ds(0, ways - 1), :, pl.ds(0, width)],
             block_send.at[index],
             block_recv.at[index],
             (s, 1 - g),
         ).wait()
 
-    pairs = {}
-
-    def hand_over(name, src, dst):
+    pairs = []
+
+    def hand_over(src, dst):
         index = len(pairs)
-        pairs[name] = remote(src, dst, pair_send.at[index], pair_recv.at[index], (s, 1 - g))
-        pairs[name].start()
+        pairs.append(remote(src, dst, pair_send.at[index], pair_recv.at[index], (s, 1 - g)))
+        pairs[index].start()
+        return pairs[index]
 
     def by_residue(value):
         for tile in range(tiles):
@@ -1021,7 +1196,7 @@
         found = jnp.where(masks[which] > 0.5, dot_cols(query, key) * temper, NEG)
         return query, key, value, found
 
-    def attend_set(which, between):
+    def attend_set(which):
         results, totals = [], []
         for head in range(HEADS):
             _, _, value, found = scores(which, head)
@@ -1030,12 +1205,10 @@
             summed = jnp.sum(weights, axis=1, keepdims=True)
             results.append(dot(weights.astype(BF16), value) * (1.0 / summed))
             totals.append(top + jnp.log(summed))
-            if head in between:
-                between[head]()
         attended[which] = jnp.concatenate(results, axis=1)
         lses[which] = jnp.concatenate(totals, axis=1)
 
-    def attend_set_back(which, out_grads, between):
+    def attend_set_back(which, out_grads):
         lists = ([], [], [])
         for head in range(HEADS):
             query, key, value, found = scores(which, head)
@@ -1048,8 +1221,6 @@
             lists[0].append(dot(score_grad, key) * temper)
             lists[1].append(dot_rows(score_grad, query) * temper)
             lists[2].append(dot_rows(weights.astype(BF16), pulled))
-            if head in between:
-                between[head]()
         at = slice(which * rows, (which + 1) * rows)
         query_grad, key_grad, value_grad = (jnp.concatenate(one, axis=1).astype(BF16) for one in lists)
         qkv_grad[0, at, :D] = query_grad
@@ -1073,6 +1244,7 @@
                 ].reshape(count // 16, 16, LANES)
 
 
+    kept = SimpleNamespace()
     barrier = greet_all(ways)
     inputs = by_residue(tokens[...].astype(F32))
     lane = lax.broadcasted_iota(jnp.int32, (rows, rows), 1)
@@ -1085,222 +1257,367 @@
     turned_row_at = ways * lax.rem(lane, across) + lane // across
     turned_row = jnp.sum((turned_row_at == row).astype(F32) * own_column, axis=0, keepdims=True)
     pack_blocks(send_blocks.at[0], inputs, jnp.broadcast_to(turned_column, (rows, HEADS)) * 1.0)
-    take_flat()
     pl.semaphore_wait(barrier, ways)
     send_tail()
     exchange(0)
     align_own()
-    spread_own()
     small_out()
-
     upstream = by_residue(cotangent[...].astype(F32))
     for half in range(2):
         down_grad[half] = upstream[:, half * half_width : (half + 1) * half_width].astype(BF16)
-    hand_over("down_grad", down_grad.at[1 - g], their_down)
-    turn(0)
-    spread(1)
-    spread_own_up()
-    exchanged(0)
-    far_inputs = unpack_values(recv_blocks.at[0])
-    far_column = unpack_extra(recv_blocks.at[0])[:, :1]
-    far_row = jnp.sum(to_column * far_column, axis=0, keepdims=True)
-    near_mask, far_mask = slide_masks(lengths, s, ways, turned_row, far_row)
-    masks[0] = near_mask
-    masks[1] = far_mask
-    hat, scale = normalize(jnp.concatenate([inputs, far_inputs], axis=0))
-    small_in()
-    gain_one, gain_two = small_row(0, third_rows), small_row(third_rows, third_rows)
-    shift_one, shift_two = small_row(2 * third_rows, third_rows), small_row(3 * third_rows, third_rows)
-    shift_down = small_row(4 * third_rows, third_rows)
-    bias_up = small_row(5 * third_rows, FF // 2 // LANES)
-    normed[...] = (hat * gain_one + shift_one).astype(BF16)
-    normed_hat[...] = hat[:rows]
-    inverse[...] = scale[:rows]
-    hand_over("normed", normed, their_normed)
-    finish(0)
-    turn(1)
-    spread(2)
-    finish(1)
-    spread(3)
-    turn(2)
-    finish(2)
-    arrived(0)
-    arrived(1)
-    arrived(2)
-    for half in range(2):
-        for tile, width in tile_groups(0):
-            at = half * 3 * half_width + tile * LANES
-            projected[:, at : at + width * LANES] = dot(
-                normed[...], weight(whole, 0, half, 0, D, tile, width)
-            ).astype(BF16)
-    turn(3)
-    attend_set(1, {})
-    pack_blocks(send_blocks.at[1], attended[1], lses[1])
-    exchange(1)
-    attend_set(0, {})
-    finish(3)
-    exchanged(1)
-    far_out = unpack_values(recv_blocks.at[1])
-    near_out = attended[0]
-    share = jax.nn.sigmoid(lses[0] - unpack_extra(recv_blocks.at[1]))
-    shares = to_columns(share)
-    difference = near_out - far_out
-    mixture[...] = (shares * near_out + (1.0 - shares) * far_out).astype(BF16)
-    hand_over("mixture", mixture, their_mixture)
-    arrived(3)
-    middle = inputs + jnp.concatenate(
-        [dot(mixture[...], weight(whole, 1, half, 0, D, 0, third_rows)) for half in range(2)], axis=1
-    )
-    hat, scale = normalize(middle)
-    second_hat[...] = hat
-    second_inverse[...] = scale
-    second_in[...] = (hat * gain_two + shift_two).astype(BF16)
-    hand_over("second_in", second_in, their_second)
-    root = (2.0 / 3.141592653589793) ** 0.5
-    for half in range(2):
-        for tile, width in tile_groups(2):
-            at = half * FF // 2 + tile * LANES
-            to = slice(at, at + width * LANES)
-            v = dot(second_in[...], weight(whole, 2, half, 0, D, tile, width)) + bias_up[:, to]
-            square = v * v
-            t = jnp.tanh(root * (v + 0.044715 * v * square))
-            activated[:, to] = (0.5 * v * (1.0 + t)).astype(BF16)
-            slope[:, to] = 0.5 * (1.0 + t) + 0.5 * v * (1.0 - t * t) * (
-                root * (1.0 + 3 * 0.044715 * square)
-            )
-    hand_over("activated", activated, their_activated)
+    kept.down_grad_pair = hand_over(down_grad.at[1 - g], their_down)
+
+    def norm():
+        exchanged(0)
+        far_inputs = unpack_values(recv_blocks.at[0])
+        far_column = unpack_extra(recv_blocks.at[0])[:, :1]
+        far_row = jnp.sum(to_column * far_column, axis=0, keepdims=True)
+        near_mask, far_mask = slide_masks(lengths, s, ways, turned_row, far_row)
+        masks[0] = near_mask
+        masks[1] = far_mask
+        hat, scale = normalize(jnp.concatenate([inputs, far_inputs], axis=0))
+        small_in()
+        count = third_rows
+        kept.gain_one, kept.gain_two = small_row(0, count), small_row(count, count)
+        kept.shift_one, kept.shift_two = small_row(2 * count, count), small_row(3 * count, count)
+        kept.shift_down = small_row(4 * count, count)
+        kept.bias_up = small_row(5 * count, FF // 2 // LANES)
+        normed[...] = (hat * kept.gain_one + kept.shift_one).astype(BF16)
+        normed_hat[...] = hat[:rows]
+        inverse[...] = scale[:rows]
+        kept.normed_pair = hand_over(normed, their_normed)
+
+    def project():
+        arrived(0)
+        for half in range(2):
+            for tile, width in tile_groups(0):
+                at = half * 3 * half_width + tile * LANES
+                projected[:, at : at + width * LANES] = dot(
+                    normed[...], weight(whole, 0, half, 0, D, tile, width)
+                ).astype(BF16)
+
+    def attend_far():
+        attend_set(1)
+        pack_blocks(send_blocks.at[1], attended[1], lses[1])
+        exchange(1)
+
+    def mix():
+        exchanged(1)
+        far_out = unpack_values(recv_blocks.at[1])
+        near_out = attended[0]
+        kept.share = jax.nn.sigmoid(lses[0] - unpack_extra(recv_blocks.at[1]))
+        kept.shares = to_columns(kept.share)
+        kept.difference = near_out - far_out
+        mixture[...] = (kept.shares * near_out + (1.0 - kept.shares) * far_out).astype(BF16)
+        kept.mixture_pair = hand_over(mixture, their_mixture)
+
+    def feed():
+        arrived(1)
+        arrived(2)
+        kept.middle = inputs + jnp.concatenate(
+            [dot(mixture[...], weight(whole, 1, half, 0, D, 0, third_rows)) for half in range(2)],
+            axis=1,
+        )
+        hat, scale = normalize(kept.middle)
+        second_hat[...] = hat
+        second_inverse[...] = scale
+        second_in[...] = (hat * kept.gain_two + kept.shift_two).astype(BF16)
+        kept.second_in_pair = hand_over(second_in, their_second)
+        root = (2.0 / 3.141592653589793) ** 0.5
+        for half in range(2):
+            for tile, width in tile_groups(2):
+                at = half * FF // 2 + tile * LANES
+                to = slice(at, at + width * LANES)
+                v = dot(second_in[...], weight(whole, 2, half, 0, D, tile, width))
+                v = v + kept.bias_up[:, to]
+                square = v * v
+                t = jnp.tanh(root * (v + 0.044715 * v * square))
+                activated[:, to] = (0.5 * v * (1.0 + t)).astype(BF16)
+                slope[:, to] = 0.5 * (1.0 + t) + 0.5 * v * (1.0 - t * t) * (
+                    root * (1.0 + 3 * 0.044715 * square)
+                )
+        kept.activated_pair = hand_over(activated, their_activated)
 
     block = 256
-    up_sums = []
-    for start in range(0, FF, block):
-        to = slice(start, start + block)
-        pulled = sum(
-            dot_cols(down_grad[half], weight(whole, 3, half, start, block, 0, third_rows))
-            for half in range(2)
-        )
-        grad = (pulled * slope[:, to]).astype(BF16)
-        half, at = divmod(start, FF // 2)
-        up_grad[half, :, at : at + block] = grad
-        up_sums.append(jnp.sum(grad.astype(F32), axis=0, keepdims=True))
-    hand_over("up_grad", up_grad.at[1 - g], their_up)
-    pairs["down_grad"].wait()
-    pairs["activated"].wait()
-    for first in range(0, FF, D):
-        weight_grad(3, activated, their_activated, down_grad, their_down, first, D)
-    reduce_first(3)
-    second_grad = jnp.concatenate(
-        [
-            sum(
-                dot_cols(up_grad[half], weight(whole, 2, half, start, block, 0, TILES[2]))
+
+    def feed_back():
+        for plane in range(3, planes):
+            arrived(plane)
+        sums = []
+        for start in range(0, FF, block):
+            to = slice(start, start + block)
+            pulled = sum(
+                dot_cols(down_grad[half], weight(whole, 3, half, start, block, 0, third_rows))
                 for half in range(2)
             )
-            for start in range(0, D, block)
-        ],
-        axis=1,
-    )
-    hat = second_hat[...]
-    gain_two_sum = jnp.sum(second_grad * hat, axis=0, keepdims=True)
-    shift_two_sum = jnp.sum(second_grad, axis=0, keepdims=True)
-    gained = upstream + norm_back(second_grad * gain_two, hat, second_inverse[...])
-    middle_grad[...] = gained
-    for half in range(2):
-        out_grad[half] = gained[:, half * half_width : (half + 1) * half_width].astype(BF16)
-    hand_over("out_grad", out_grad.at[1 - g], their_out)
-    mix_grad = jnp.concatenate(
-        [
-            sum(
-                dot_cols(out_grad[half], weight(whole, 1, half, start, block, 0, third_rows))
+            grad = (pulled * slope[:, to]).astype(BF16)
+            half, at = divmod(start, FF // 2)
+            up_grad[half, :, at : at + block] = grad
+            sums.append(jnp.sum(grad.astype(F32), axis=0, keepdims=True))
+        kept.up_sum = jnp.concatenate(sums, axis=1)
+        kept.up_grad_pair = hand_over(up_grad.at[1 - g], their_up)
+
+    def down_weights():
+        kept.down_grad_pair.wait()
+        kept.activated_pair.wait()
+        for first in range(0, FF, D):
+            weight_grad(3, activated, their_activated, down_grad, their_down, first, D)
+
+    def through(left, index, tiles_to):
+        return jnp.concatenate(
+            [
+                sum(
+                    dot_cols(left[half], weight(whole, index, half, start, block, 0, tiles_to))
+                    for half in range(2)
+                )
+                for start in range(0, D, block)
+            ],
+            axis=1,
+        )
+
+    def mix_back():
+        second_grad = through(up_grad, 2, TILES[2])
+        hat = second_hat[...]
+        kept.gain_two_sum = jnp.sum(second_grad * hat, axis=0, keepdims=True)
+        kept.shift_two_sum = jnp.sum(second_grad, axis=0, keepdims=True)
+        gained = upstream + norm_back(second_grad * kept.gain_two, hat, second_inverse[...])
+        middle_grad[...] = gained
+        for half in range(2):
+            out_grad[half] = gained[:, half * half_width : (half + 1) * half_width].astype(BF16)
+        kept.out_grad_pair = hand_over(out_grad.at[1 - g], their_out)
+        mix_grad = through(out_grad, 1, third_rows)
+        share, shares = kept.share, kept.shares
+        near_lse_grad = share * (1.0 - share) * to_heads(kept.difference * mix_grad)
+        lse_grads[0] = near_lse_grad
+        near_grad[...] = (shares * mix_grad).astype(BF16)
+        pack_blocks(send_blocks.at[2], (1.0 - shares) * mix_grad, -near_lse_grad)
+        exchange(2)
+
+    def up_weights():
+        kept.second_in_pair.wait()
+        kept.up_grad_pair.wait()
+        weight_grad(2, second_in, their_second, up_grad, their_up, 0, D)
+
+    def out_weights():
+        kept.mixture_pair.wait()
+        kept.out_grad_pair.wait()
+        weight_grad(1, mixture, their_mixture, out_grad, their_out, 0, D)
+
+    def put_output():
+        result = kept.middle + kept.shift_down + jnp.concatenate(
+            [
+                dot(activated[...], weight(whole, 3, half, 0, FF, 0, third_rows))
                 for half in range(2)
-            )
-            for start in range(0, D, block)
-        ],
-        axis=1,
-    )
-    near_lse_grad = share * (1.0 - share) * to_heads(difference * mix_grad)
-    lse_grads[0] = near_lse_grad
-    near_grad[...] = (shares * mix_grad).astype(BF16)
-    pack_blocks(send_blocks.at[2], (1.0 - shares) * mix_grad, -near_lse_grad)
-    exchange(2)
-    pairs["second_in"].wait()
-    pairs["up_grad"].wait()
-    weight_grad(2, second_in, their_second, up_grad, their_up, 0, D)
-    reduce_first(2)
-    pairs["mixture"].wait()
-    pairs["out_grad"].wait()
-    weight_grad(1, mixture, their_mixture, out_grad, their_out, 0, D)
-    result = middle + shift_down + jnp.concatenate(
-        [dot(activated[...], weight(whole, 3, half, 0, FF, 0, third_rows)) for half in range(2)], axis=1
-    )
-    output[...] = in_order(result).astype(BF16)
-
-    attend_set_back(0, near_grad, {})
-    reduce_second(3)
-    exchanged(2)
-    far_grad[...] = unpack_values(recv_blocks.at[2]).astype(BF16)
-    lse_grads[1] = unpack_extra(recv_blocks.at[2])
-    attend_set_back(1, far_grad, {})
-    hand_over("qkv_grad", qkv_grad.at[1 - g], their_qkv)
-    reduce_second(2)
-    first_grad = jnp.concatenate(
-        [
-            sum(
-                dot_cols(qkv_grad[half], weight(whole, 0, half, start, block, 0, TILES[0]))
-                for half in range(2)
-            )
-            for start in range(0, D, block)
-        ],
-        axis=1,
-    )
-    pack_blocks(send_blocks.at[3], first_grad[rows:], None)
-    exchange(3)
-    pairs["normed"].wait()
-    pairs["qkv_grad"].wait()
-    weight_grad(0, normed, their_normed, qkv_grad, their_qkv, 0, D)
-    reduce_first(0)
-    reduce_third(3)
-    reduce_first(1)
-    reduce_relay(3)
-    reduce_third(2)
-    exchanged(3)
-    first_grad = first_grad[:rows] + unpack_values(recv_blocks.at[3])
-    hat = normed_hat[...]
-    gain_one_sum = jnp.sum(first_grad * hat, axis=0, keepdims=True)
-    shift_one_sum = jnp.sum(first_grad, axis=0, keepdims=True)
-    input_grad[...] = in_order(
-        middle_grad[...] + norm_back(first_grad * gain_one, hat, inverse[...])
-    )
-    down_sums = [
-        jnp.sum(down_grad[half].astype(F32), axis=0, keepdims=True) for half in range(2)
-    ]
-    up_sum = jnp.concatenate(up_sums, axis=1)
-    for half in range(2):
-        to = slice(half * half_width, (half + 1) * half_width)
-        listed = (
-            gain_one_sum[:, to], gain_two_sum[:, to], shift_one_sum[:, to], shift_two_sum[:, to],
-            down_sums[half], up_sum[:, half * FF // 2 : (half + 1) * FF // 2],
-        )
-        at = 0
-        for vector in listed:
-            count = vector.shape[1] // LANES
-            small_parts[half, at : at + count, :] = vector.reshape(count, LANES)
-            at += count
-        small_parts[half, at:, :] = jnp.zeros((SMALL_ROWS - at, LANES), F32)
-    hand_over("small", small_parts.at[1 - g], their_small)
-    pairs["small"].wait()
-    small_parts[g] = small_parts[g] + their_small[...]
-    pl.when(s != ways - 1)(lambda: small_home().start())
-    reduce_second(0)
-    reduce_relay(2)
-    reduce_second(1)
-    reduce_third(0)
-    reduce_relay(0)
-    reduce_end(1)
-    reduce_last()
+            ],
+            axis=1,
+        )
+        output[...] = in_order(result).astype(BF16)
+
+    def far_back():
+        exchanged(2)
+        far_grad[...] = unpack_values(recv_blocks.at[2]).astype(BF16)
+        lse_grads[1] = unpack_extra(recv_blocks.at[2])
+        attend_set_back(1, far_grad)
+        kept.qkv_grad_pair = hand_over(qkv_grad.at[1 - g], their_qkv)
+
+    def project_back():
+        kept.first_grad = through(qkv_grad, 0, TILES[0])
+        pack_blocks(send_blocks.at[3], kept.first_grad[rows:], None)
+        exchange(3)
+
+    def qkv_weights():
+        kept.normed_pair.wait()
+        kept.qkv_grad_pair.wait()
+        weight_grad(0, normed, their_normed, qkv_grad, their_qkv, 0, D)
+
+    def put_input_grad():
+        exchanged(3)
+        first_grad = kept.first_grad[:rows] + unpack_values(recv_blocks.at[3])
+        hat = normed_hat[...]
+        kept.gain_one_sum = jnp.sum(first_grad * hat, axis=0, keepdims=True)
+        kept.shift_one_sum = jnp.sum(first_grad, axis=0, keepdims=True)
+        input_grad[...] = in_order(
+            middle_grad[...] + norm_back(first_grad * kept.gain_one, hat, inverse[...])
+        )
+
+    def small_sums():
+        for half in range(2):
+            to = slice(half * half_width, (half + 1) * half_width)
+            down_sum = jnp.sum(down_grad[half].astype(F32), axis=0, keepdims=True)
+            sums = (kept.gain_one_sum, kept.gain_two_sum, kept.shift_one_sum, kept.shift_two_sum)
+            listed = [one[:, to] for one in sums] + [down_sum]
+            listed.append(kept.up_sum[:, half * FF // 2 : (half + 1) * FF // 2])
+            at = 0
+            for vector in listed:
+                count = vector.shape[1] // LANES
+                small_parts[half, at : at + count, :] = vector.reshape(count, LANES)
+                at += count
+            small_parts[half, at:, :] = jnp.zeros((SMALL_ROWS - at, LANES), F32)
+        kept.small_pair = hand_over(small_parts.at[1 - g], their_small)
+        kept.small_pair.wait()
+        small_parts[g] = small_parts[g] + their_small[...]
+        pl.when(s != ways - 1)(lambda: small_home().start())
+
+    early(order[0], late)
+    direct(order[0], late)
+    early(order[0], 1)
+    early(order[0], 0)
+    leave(1, False)
+    leave(0, False)
+    leave(1, True)
+    turn_piece(order[0], late)
+    direct(order[0], 0)
+    direct(order[0], 1)
+    turn_piece(order[0], 1)
+    enter_plane(order[1], 1)
+    turn_piece(order[0], 0)
+    early(order[1], 1)
+    enter_plane(order[2], 1)
+    enter_plane(order[1], 0)
+    early(order[1], 0)
+    finish(order[0], 1)
+    late_own()
+    turn_piece(order[1], 1)
+    direct(order[1], 1)
+    direct(order[1], 0)
+    norm()
+    enter_plane(order[2], 0)
+    turn_piece(order[1], 0)
+    finish(order[0], late)
+    early(order[2], 0)
+    direct(order[2], 1)
+    enter_plane(order[3], 1)
+    early(order[2], 1)
+    early(order[3], 1)
+    direct(order[3], 1)
+    late_on(order[1])
+    finish(order[1], 1)
+    finish(order[1], late)
+    finish(order[1], 0)
+    leave(0, True)
+    late_on(order[2])
+    turn_piece(order[3], 1)
+    turn_piece(order[2], 1)
+    finish(order[0], 0)
+    enter_plane(order[3], 0)
+    early(order[3], 0)
+    project()
+    turn_piece(order[2], 0)
+    direct(order[2], 0)
+    attend_far()
+    finish(order[2], late)
+    finish(order[3], 1)
+    finish(order[2], 1)
+    direct(order[3], 0)
+    attend_set(0)
+    turn_piece(order[3], 0)
+    late_on(order[3])
+    finish(order[3], late)
+    finish(order[2], 0)
+    mix()
+    finish(order[3], 0)
+    feed()
+    down_weights()
+    late_start(3)
+    out_ahead(3, 0)
+    feed_back()
+    out_ahead(3, 1)
+    out_keep(3, 1)
+    up_weights()
+    out_ahead(2, 0)
+    mix_back()
+    out_ahead(2, 1)
+    out_weights()
+    out_ahead(1, 0)
+    out_pass(3, 1)
+    out_keep(3, 0)
+    attend_set_back(0, near_grad)
+    out_keep(2, 0)
+    late_start(2)
+    out_pass(3, 0)
+    late_relay(3)
+    late_start(1)
+    out_pass(2, 0)
+    out_pass(2, 1)
+    out_keep(2, 1)
+    far_back()
+    late_relay(2)
+    qkv_weights()
+    late_relay(1)
+    out_ahead(0, 0)
+    out_keep(0, 0)
+    out_take(3, 0)
+    out_take(3, 1)
+    out_ahead(0, 1)
+    out_join(3, 1)
+    project_back()
+    out_join(3, 0)
+    put_output()
+    late_home(2)
+    late_start(0)
+    out_pass(0, 0)
+    out_relay(3, 1)
+    out_take(2, 0)
+    out_keep(0, 1)
+    out_take(2, 1)
+    out_join(2, 0)
+    out_take(0, 0)
+    out_pass(0, 1)
+    out_relay(3, 0)
+    out_join(2, 1)
+    out_ahead(1, 1)
+    late_home(1)
+    late_home(3)
+    out_keep(1, 0)
+    out_pass(1, 0)
+    out_join(0, 0)
+    out_keep(1, 1)
+    late_relay(0)
+    out_ahead(1, late)
+    out_take(0, 1)
+    out_relay(2, 1)
+    out_relay(2, 0)
+    out_relay(0, 0)
+    late_home(0)
+    out_keep(0, late)
+    out_keep(1, late)
+    out_join(0, 1)
+    out_ahead(2, late)
+    put_input_grad()
+    out_ahead(0, late)
+    out_relay(0, 1)
+    out_take(1, late)
+    out_take(1, 0)
+    out_pass(1, late)
+    out_keep(2, late)
+    out_pass(1, 1)
+    out_join(1, 0)
+    small_sums()
+    out_take(1, 1)
+    out_pass(0, late)
+    out_ahead(3, late)
+    out_relay(1, 0)
+    out_pass(2, late)
+    out_take(2, late)
+    out_keep(3, late)
+    out_take(0, late)
+    out_join(1, 1)
+    out_pass(3, late)
+    out_take(3, late)
+    out_join(3, late)
+    out_join(1, late)
+    out_join(0, late)
+    out_relay(1, 1)
+    out_join(2, late)
+    everything = [(part, piece) for piece in range(PIECES + 1) for part in range(2)]
+    out_last(everything[:1])
+    settle_first()
+    out_last(everything[1:])
     settle()
     pl.when(s != ways - 1)(lambda: small_home().wait_send())
     gather_sent()
     small_sent()
-    reduce_sent()
+    out_sent()
 
 
 def bounds_total():
@@ -1309,8 +1626,8 @@
 
 def run_step(tokens, cotangent, holes, lengths, flat, ways):
     rows = tokens.shape[0]
-    flat_rows = flat.shape[0]
     own = MAT_ROWS // ways
+    entries = (MAT_ROWS * LANES + bounds_total()) // ways
     half_own = own // 2
     planes = ways // 4
     vmem = pl.BlockSpec(memory_space=pltpu.VMEM)
@@ -1320,7 +1637,7 @@
         ((2, MAT_ROWS, LANES), BF16),
         ((MAT_ROWS, LANES), BF16),
         ((2, SMALL_ROWS, LANES), BF16),
-        ((own + 2 * SMALL_ROWS, LANES), F32),
+        ((SMALL_ROWS + 184, LANES), F32),
         ((own + SMALL_ROWS, LANES), F32),
         ((SMALL_ROWS, LANES), F32),
         ((D // LANES, rows, LANES), F32),
@@ -1357,9 +1674,10 @@
         ((rows, half), BF16),
         ((2, SMALL_ROWS, LANES), F32),
         ((SMALL_ROWS, LANES), F32),
-        ((planes, 2, 2, PIECES, half_own // PIECES, LANES), BF16),
-        ((planes, 2, PIECES, half_own // PIECES, LANES), BF16),
+        ((planes, 2, 2, PIECES + 1, half_own // PIECES, LANES), BF16),
+        ((planes, 2, PIECES + 1, half_own // PIECES, LANES), BF16),
         ((2, planes, 2, PIECES, half_own // PIECES, LANES), BF16),
+        ((2, planes, 2, 4, max(LATE_OUT), LANES), BF16),
         ((own, LANES), F32),
         ((own + 2 * SMALL_ROWS, LANES), F32),
         ((SMALL_ROWS, LANES), F32),
@@ -1370,7 +1688,7 @@
         out_shape=(
             jax.ShapeDtypeStruct((rows, D), BF16),
             jax.ShapeDtypeStruct((rows, D), F32),
-            jax.ShapeDtypeStruct((flat_rows, LANES), F32),
+            jax.ShapeDtypeStruct((-(-entries // (8 * LANES)) * 8, LANES), F32),
         ),
         in_specs=[
             vmem, vmem, vmem, pl.BlockSpec(memory_space=pltpu.SMEM), vmem,
@@ -1379,13 +1697,15 @@
         scratch_shapes=[pltpu.VMEM(*shape) for shape in shapes]
         + [
             dma((2,)),
-            dma((2, planes, 5)), dma((2, ways)),
-            dma((planes,)), dma((planes,)),
+            dma((2, planes, 5, PIECES + 1)), dma((2, ways, PIECES + 1)),
+            dma((2, planes, 2)), dma((planes, 2)),
+            dma((planes, 2, PIECES + 1)), dma((planes, 2, PIECES + 1)),
             dma((ways,)), dma((2,)),
             dma((4,)), dma((4,)), dma((9,)), dma((9,)),
-            dma((planes, 2, 2, PIECES)), dma((planes, 2, 2, PIECES)),
-            dma((planes, 2, PIECES)), dma((planes, 2, PIECES)),
+            dma((planes, 2, 2, PIECES + 1)), dma((planes, 2, 2, PIECES + 1)),
+            dma((planes, 2, PIECES + 1)), dma((planes, 2, PIECES + 1)),
             dma((planes, 2, PIECES)), dma((2, planes, 2, PIECES)),
+            dma((planes, 2)), dma((2, planes, 2)),
             dma((2,)), dma((2,)),
         ],
         compiler_params=pltpu.CompilerParams(
@@ -1409,11 +1729,11 @@
     flat[full : full + 1, :rest] = last[...]
 
 
-def to_rows(entries):
+def to_rows(entries, rows):
     size = entries.shape[1]
     return pl.pallas_call(
         rows_kernel,
-        out_shape=jax.ShapeDtypeStruct((-(-size // (8 * LANES)) * 8, LANES), F32),
+        out_shape=jax.ShapeDtypeStruct((rows, LANES), F32),
         in_specs=[pl.BlockSpec(memory_space=pl.ANY)],
         out_specs=pl.BlockSpec(memory_space=pltpu.VMEM),
         scratch_shapes=[pltpu.VMEM((1, size % LANES), F32), pltpu.SemaphoreType.DMA((2,))],
@@ -1422,13 +1742,14 @@
 
 
 def adam_kernel(
-    gradient, master, first_moment, second_moment, new_moment, new_second, new_master,
-    kept, last, load_sem, store_sem,
+    gradient, master, first_moment, second_moment, layer_output, layer_grad,
+    new_moment, new_second, new_master, output, input_grad, kept, last, kept_output, kept_grad,
+    load_sem, store_sem, pass_sem,
 ):
     size = master.shape[1]
     full, rest = divmod(size, LANES)
-    chunks = 4
-    chunk = -(-full // (8 * chunks)) * 8
+    chunks, step = 3, 56
+    chunk = -(-full // (step * chunks)) * step
     spans = [(c * chunk, min(chunk, full - c * chunk)) for c in range(chunks)]
     sources, targets = (first_moment, second_moment, master), (new_moment, new_second, new_master)
 
@@ -1437,6 +1758,11 @@
 
     def load(which, index):
         first, count = spans[index]
+        if which == 3:
+            span = pl.ds(first, -(-count // step) * step)
+            return pltpu.make_async_copy(
+                gradient.at[span], kept.at[3, span], load_sem.at[3, index]
+            )
         return pltpu.make_async_copy(
             piece(sources[which], first, count), kept.at[which, pl.ds(first, count)],
             load_sem.at[which, index],
@@ -1459,43 +1785,56 @@
             last.at[which], targets[which].at[:, pl.ds(full * LANES, rest)], store_sem.at[which, chunks]
         )
 
+    passed = tuple(
+        (
+            pltpu.make_async_copy(source, through, pass_sem.at[index]),
+            pltpu.make_async_copy(through, target, pass_sem.at[index]),
+        )
+        for index, (source, through, target) in enumerate(
+            ((layer_output, kept_output, output), (layer_grad, kept_grad, input_grad))
+        )
+    )
     for index in range(chunks):
-        for which in range(3):
+        for which in range(4):
             load(which, index).start()
     for which in range(3):
         load_last(which).start()
+    for copy, _ in passed:
+        copy.start()
     origin = lax.axis_index("seq") * size
 
-    def update(first, count, moment, second, weights):
+    def update(first, count, moment, second, weights, gradients):
         at = (
             origin
             + (first + lax.broadcasted_iota(jnp.int32, (count, LANES), 0)) * LANES
             + lax.broadcasted_iota(jnp.int32, (count, LANES), 1)
         )
-        return adam_update(weights, moment, second, gradient[pl.ds(first, count), :], at)
-
-    step = 8
+        return adam_update(weights, moment, second, gradients, at)
 
     for index, (first, count) in enumerate(spans):
-        for which in range(3):
+        for which in range(4):
             load(which, index).wait()
 
         def run(at, carry, first=first):
             where = pl.multiple_of(first + at * step, 8)
             span = pl.ds(where, step)
-            found = update(where, step, kept[0, span, :], kept[1, span, :], kept[2, span, :])
+            found = update(where, step, *(kept[which, span, :] for which in range(4)))
             for which in range(3):
                 kept[which, span, :] = found[which]
             return carry
 
-        lax.fori_loop(0, -(-count // step), run, 0, unroll=2)
+        lax.fori_loop(0, -(-count // step), run, 0)
         for which in range(3):
             store(which, index).start()
+        if index == 0:
+            for copy, onward in passed:
+                copy.wait()
+                onward.start()
     for which in range(3):
         load_last(which).wait()
     moment, second, weights = (last[which] for which in range(3))
     at = origin + full * LANES + lax.broadcasted_iota(jnp.int32, (1, rest), 1)
-    found = adam_update(weights, moment, second, gradient[full : full + 1, :rest], at)
+    found = adam_update(weights, moment, second, kept[3, full : full + 1, :rest], at)
     for which in range(3):
         last[which] = found[which]
         store_last(which).start()
@@ -1503,33 +1842,40 @@
         for index in range(chunks):
             store(which, index).wait()
         store_last(which).wait()
-
-
-def run_adam(gradient, master, first_moment, second_moment):
+    for _, copy in passed:
+        copy.wait()
+
+
+def run_adam(gradient, master, first_moment, second_moment, layer_output, layer_grad):
     size = master.shape[1]
     anywhere = pl.BlockSpec(memory_space=pl.ANY)
     return pl.pallas_call(
         adam_kernel,
-        out_shape=(jax.ShapeDtypeStruct((1, size), F32),) * 3,
-        in_specs=[pl.BlockSpec(memory_space=pltpu.VMEM), anywhere, anywhere, anywhere],
-        out_specs=(anywhere,) * 3,
+        out_shape=(jax.ShapeDtypeStruct((1, size), F32),) * 3
+        + tuple(jax.ShapeDtypeStruct(one.shape, one.dtype) for one in (layer_output, layer_grad)),
+        in_specs=[anywhere] * 6,
+        out_specs=(anywhere,) * 5,
         scratch_shapes=[
-            pltpu.VMEM((3,) + gradient.shape, F32),
+            pltpu.VMEM((4,) + gradient.shape, F32),
             pltpu.VMEM((3, 1, size % LANES), F32),
+            pltpu.VMEM(layer_output.shape, layer_output.dtype),
+            pltpu.VMEM(layer_grad.shape, layer_grad.dtype),
+            pltpu.SemaphoreType.DMA((4, 5)),
             pltpu.SemaphoreType.DMA((3, 5)),
-            pltpu.SemaphoreType.DMA((3, 5)),
+            pltpu.SemaphoreType.DMA((2,)),
         ],
         compiler_params=pltpu.CompilerParams(vmem_limit_bytes=VMEM_BYTES),
         name="run_adam",
-    )(gradient, master, first_moment, second_moment)
+    )(gradient, master, first_moment, second_moment, layer_output, layer_grad)
 
 
 def on_device(tokens, cotangent, holes, slide_lengths, master, first_moment, second_moment):
     ways = lax.axis_size("seq")
-    output, input_grad, gradient = run_step(
-        tokens[0], cotangent[0], holes, slide_lengths, to_rows(master), ways
-    )
-    new_moment, new_second, new_master = run_adam(gradient, master, first_moment, second_moment)
+    flat = to_rows(master, MAT_ROWS // ways + SMALL_ROWS)
+    output, input_grad, gradient = run_step(tokens[0], cotangent[0], holes, slide_lengths, flat, ways)
+    new_moment, new_second, new_master, output, input_grad = run_adam(
+        gradient, master, first_moment, second_moment, output, input_grad
+    )
     return (output[None], input_grad[None], new_moment, new_second, new_master)
 
 

time: 191 us -> 157 us (0.82)
  the two profiles are of different devices: /device:TPU:12 before, /device:TPU:8 now
where the time goes in v4:
time: 157 us
  Pallas kernels  156 us (99%)
    pallas_call x1, Pallas kernels, run_step(): pl.pallas_call(partial(step_kernel, ways), out_shape=(jax.ShapeDtypeStruc...  150 us
    pallas_call x1, Pallas kernels, run_adam(): pl.pallas_call(adam_kernel, out_shape=(jax.ShapeDtypeStruct((1, size), F3...  4.29 us

profile of v4, /device:TPU:8, one launch (start us, length us, event | category | flops | bytes accessed | tf_op | source)
XLA Modules:
  0.0 156.9 jit_solution(2658854212536684081)
XLA Ops:
  0.6 2.1 %to_rows.1.flat = f32[1760,128]{1,0:T(8,128)} custom-call(f32[1,221400]{1,0:T(1,128)} %master.1), custom_call_target="tpu_custom_call" | custom-call | tf_op jit(solution)/shard_map/to_rows/pallas_call | solution.py:1734
  2.8 149.7 %run_step.1 = (bf16[128,768]{1,0:T(8,128)(2,1)}, f32[128,768]{1,0:T(8,128)}, f32[1736,128]{1,0:T(8,128)}) custom-call(bf16[128,768]{1,0:T(8,128)(2,1)} %bitcast.4, bf16[128,768]{1,0:T(8,128)(2,1)} %bitcast.5, s32[1,128]{1,0:T(1,128)} %holes.1, s32[1,8]{1,0:T(1,128)} %lengths.1, f32[1760,128]{1,0:T(8,128)} %to_rows.1.flat), custom_call_target="tpu_custom_call" | custom-call | tf_op jit(solution)/shard_map/run_step/pallas_call | solution.py:1686
  152.4 4.3 %run_adam.1 = (f32[1,221400]{1,0:T(1,128)}, f32[1,221400]{1,0:T(1,128)}, f32[1,221400]{1,0:T(1,128)}, bf16[128,768]{1,0:T(8,128)(2,1)}, f32[128,768]{1,0:T(8,128)}) custom-call(f32[1736,128]{1,0:T(8,128)} %get-tuple-element.13.gradient, f32[1,221400]{1,0:T(1,128)} %master.1, f32[1,221400]{1,0:T(1,128)} %first_moment.1, f32[1,221400]{1,0:T(1,128)} %second_moment.1, ...), custom_call_target="tpu_custom_call" | custom-call | tf_op jit(solution)/shard_map/run_adam/pallas_call | solution.py:1852

commit v5 on v4

--- a/solution.py
+++ b/solution.py
@@ -387,7 +387,7 @@
 ORDERS = ((1, 2, 3), (0, 2, 3), (0, 3, 1), (0, 2, 1))
 PIECES = 2
 LATE_ROWS = 160
-LATE_OUT = (64, 128, 192, 192)
+LATE_OUT = (128, 160, 192, 192)
 
 
 def matrix_starts():
@@ -559,17 +559,25 @@
     return result
 
 
+def lay_group(tiled, laid, first, group, count, turn=None):
+    for tile in range(count):
+        block = tiled[pl.ds(pl.multiple_of(first + 16 * (group * count + tile), 16), 16), :]
+        if turn is not None:
+            block = pltpu.roll(block, turn, 1)
+        laid[pl.ds(first + group * 16 * count + tile, 16, stride=count), :] = block
+
+
 def step_kernel(
-    ways, tokens, cotangent, holes, lengths, flat,
-    output, input_grad, flat_grad,
-    whole, grads, small, extended, aligned, tail,
+    ways, tokens, cotangent, holes, lengths, master,
+    output, input_grad, total, after_rows,
+    whole, grads, small, entries_here, entries_end, extended, aligned, tail,
     turning, send_blocks, recv_blocks, masks, normed, normed_hat, inverse, projected, attended, lses,
     mixture, second_in, activated, slope, second_hat, second_inverse, middle_grad,
     qkv_grad, out_grad, up_grad, down_grad, near_grad, far_grad, lse_grads,
     their_normed, their_mixture, their_second, their_activated,
     their_qkv, their_out, their_up, their_down, small_parts, their_small,
-    by_x, by_y, by_z, by_late, total, laid, follow_rows, small_all,
-    tail_sem, slot_send, slot_recv, late_send, late_recv, core_send, core_recv, small_send, small_recv,
+    by_x, by_y, by_z, by_late, laid, follow_rows, small_all,
+    load_sem, tail_sem, slot_send, slot_recv, late_send, late_recv, core_send, core_recv, small_send, small_recv,
     block_send, block_recv, pair_send, pair_recv,
     x_send, x_recv, y_send, y_recv, z_send, z_recv, late_out_send, late_out_recv, end_sem, sum_sem,
 ):
@@ -597,6 +605,26 @@
 
     last_row, last_lanes = divmod(own * LANES + entries, LANES)
     step_rows = 176
+    full = last_row * LANES
+    loads = (
+        pltpu.make_async_copy(
+            master.at[:, pl.ds(0, full)], entries_here.at[:, pl.ds(0, full)], load_sem.at[0]
+        ),
+        pltpu.make_async_copy(master.at[:, pl.ds(full, last_lanes)], entries_end, load_sem.at[1]),
+    )
+
+    def loaded():
+        for load in loads:
+            load.wait()
+        entries_here[:, full:] = jnp.zeros((1, entries_here.shape[1] - full), F32)
+        entries_here[:, full : full + last_lanes] = entries_end[...]
+
+    def flat_rows(first, count):
+        if not isinstance(first, int):
+            first = pl.multiple_of(first * LANES, LANES)
+        else:
+            first = first * LANES
+        return entries_here[:, pl.ds(first, count * LANES)].reshape(count, LANES)
 
     def follow_copy():
         return remote(
@@ -604,49 +632,50 @@
             (lax.rem(s + 1, ways), g),
         )
 
-    def send_tail():
+    def make_tail():
         lanes = lax.broadcasted_iota(jnp.int32, (SMALL_ROWS, LANES), 1)
         gap = LANES - last_lanes
-        older = pltpu.roll(flat[last_row - SMALL_ROWS : last_row, :], gap, 1)
-        newer = pltpu.roll(flat[last_row - SMALL_ROWS + 1 : last_row + 1, :], gap, 1)
+        older = pltpu.roll(flat_rows(last_row - SMALL_ROWS, SMALL_ROWS), gap, 1)
+        newer = pltpu.roll(flat_rows(last_row - SMALL_ROWS + 1, SMALL_ROWS), gap, 1)
         tail[...] = jnp.where(lanes < gap, older, newer)
-        follow_copy().start()
-
-    def align_own():
+
+    def align(here, before, to):
         lanes = lax.broadcasted_iota(jnp.int32, (step_rows, LANES), 1)
-
-        def align(source, start, to):
-            here = source[pl.ds(start - row_shift, step_rows), :]
-            before = source[pl.ds(start - row_shift - 1, step_rows), :]
-            aligned[pl.ds(pl.multiple_of(to, 8), step_rows), :] = jnp.where(
-                lanes >= lane_shift,
-                pltpu.roll(here, lane_shift, 1),
-                pltpu.roll(before, lane_shift, 1),
-            )
-
+        aligned[pl.ds(pl.multiple_of(to, 8), step_rows), :] = jnp.where(
+            lanes >= lane_shift, pltpu.roll(here, lane_shift, 1), pltpu.roll(before, lane_shift, 1)
+        )
+
+    def fill(unit):
+        first = unit * UNIT
+
+        def tiled(count):
+            for group in range(UNIT // (16 * count)):
+                for tile in range(count):
+                    block = aligned[pl.ds(first + group * 16 * count + tile, 16, stride=count), :]
+                    at = s * own + first + 16 * (group * count + tile)
+                    whole[g, pl.ds(pl.multiple_of(at, 16), 16), :] = block.astype(BF16)
+
+        unit_tiles(s * (own // UNIT) + unit, tiled)
+
+    def fill_most():
         def align_step(step, carry):
-            align(flat, step * step_rows, step * step_rows)
+            first = step * step_rows - row_shift
+            align(flat_rows(first, step_rows), flat_rows(first - 1, step_rows), step * step_rows)
             return carry
 
-        def fill(unit, carry):
-            first = unit * UNIT
-
-            def tiled(count):
-                for group in range(UNIT // (16 * count)):
-                    for tile in range(count):
-                        block = aligned[pl.ds(first + group * 16 * count + tile, 16, stride=count), :]
-                        at = s * own + first + 16 * (group * count + tile)
-                        whole[g, pl.ds(pl.multiple_of(at, 16), 16), :] = block.astype(BF16)
-
-            unit_tiles(s * (own // UNIT) + unit, tiled)
+        def fill_unit(unit, carry):
+            fill(unit)
             return carry
 
-        extended[SMALL_ROWS:, :] = flat[: extended.shape[0] - SMALL_ROWS, :]
+        extended[SMALL_ROWS:, :] = flat_rows(0, extended.shape[0] - SMALL_ROWS)
         lax.fori_loop(1, (own + SMALL_ROWS) // step_rows, align_step, 0)
-        lax.fori_loop(1, own // UNIT, fill, 0)
+        lax.fori_loop(1, own // UNIT, fill_unit, 0)
+
+    def fill_first():
         follow_copy().wait()
-        align(extended, SMALL_ROWS, 0)
-        fill(0, 0)
+        first = SMALL_ROWS - row_shift
+        align(extended[pl.ds(first, step_rows), :], extended[pl.ds(first - 1, step_rows), :], 0)
+        fill(0)
 
     order = [z]
     for step in range(1, planes):
@@ -1060,11 +1089,6 @@
             small_parts.at[g], small_all.at[s], sum_sem.at[0], sum_sem.at[1], (ways - 1, g)
         )
 
-    def lay_group(first, group, count):
-        for tile in range(count):
-            block = total[pl.ds(pl.multiple_of(first + 16 * (group * count + tile), 16), 16), :]
-            laid[pl.ds(first + group * 16 * count + tile, 16, stride=count), :] = block
-
     def follow_back():
         return remote(
             laid.at[pl.ds(0, SMALL_ROWS)], follow_rows, end_sem.at[0], end_sem.at[1],
@@ -1072,23 +1096,15 @@
         )
 
     def settle_first():
-        unit_tiles(s * (own // UNIT), lambda count: lay_group(0, 0, count))
+        unit_tiles(s * (own // UNIT), lambda count: lay_group(total, laid, 0, 0, count))
         follow_back().start()
 
     def settle():
-        def lay(unit, carry):
-            def tiled(count):
-                for group in range(1, UNIT // (16 * count)):
-                    lay_group(unit * UNIT, group, count)
-
-            def first_group(count):
-                lay_group(unit * UNIT, 0, count)
-
-            unit_tiles(s * (own // UNIT) + unit, tiled)
-            pl.when(unit > 0)(lambda: unit_tiles(s * (own // UNIT) + unit, first_group))
-            return carry
-
-        lax.fori_loop(0, own // UNIT, lay, 0)
+        follow_back().wait()
+
+        @pl.when(s != ways - 1)
+        def _():
+            after_rows[...] = follow_rows[...]
 
         @pl.when(s == ways - 1)
         def _():
@@ -1097,29 +1113,7 @@
                 sum_sem.at[0], sum_sem.at[1], (0, g),
             ).wait_recv()
             small_all[ways - 1] = small_parts[g]
-            laid[own : own + SMALL_ROWS, :] = jnp.sum(small_all[...], axis=0)
-
-        laid[own + SMALL_ROWS :, :] = jnp.zeros((laid.shape[0] - own - SMALL_ROWS, LANES), F32)
-        follow_back().wait()
-
-        @pl.when(s != ways - 1)
-        def _():
-            laid[own : own + SMALL_ROWS, :] = follow_rows[...]
-
-        back = lax.rem(LANES - lane_shift, LANES)
-        step_rows = 56
-        lanes = lax.broadcasted_iota(jnp.int32, (step_rows, LANES), 1)
-
-        def align(step, carry):
-            start = step * step_rows
-            here = laid[pl.ds(start + row_shift, step_rows), :]
-            after = laid[pl.ds(start + row_shift + 1, step_rows), :]
-            flat_grad[pl.ds(pl.multiple_of(start, 8), step_rows), :] = jnp.where(
-                lanes < LANES - lane_shift, pltpu.roll(here, back, 1), pltpu.roll(after, back, 1)
-            )
-            return carry
-
-        lax.fori_loop(0, flat_grad.shape[0] // step_rows, align, 0)
+            after_rows[...] = jnp.sum(small_all[...], axis=0)
 
 
     widths = (half_width + LANES,) * 3 + (half_width,)
@@ -1246,6 +1240,8 @@
 
     kept = SimpleNamespace()
     barrier = greet_all(ways)
+    for load in loads:
+        load.start()
     inputs = by_residue(tokens[...].astype(F32))
     lane = lax.broadcasted_iota(jnp.int32, (rows, rows), 1)
     row = lax.broadcasted_iota(jnp.int32, (rows, rows), 0)
@@ -1257,17 +1253,23 @@
     turned_row_at = ways * lax.rem(lane, across) + lane // across
     turned_row = jnp.sum((turned_row_at == row).astype(F32) * own_column, axis=0, keepdims=True)
     pack_blocks(send_blocks.at[0], inputs, jnp.broadcast_to(turned_column, (rows, HEADS)) * 1.0)
+    loaded()
+    make_tail()
+    fill_most()
     pl.semaphore_wait(barrier, ways)
-    send_tail()
+    follow_copy().start()
+    early(order[0], late)
+    direct(order[0], late)
     exchange(0)
-    align_own()
     small_out()
-    upstream = by_residue(cotangent[...].astype(F32))
-    for half in range(2):
-        down_grad[half] = upstream[:, half * half_width : (half + 1) * half_width].astype(BF16)
-    kept.down_grad_pair = hand_over(down_grad.at[1 - g], their_down)
+    fill_first()
 
     def norm():
+        kept.upstream = by_residue(cotangent[...].astype(F32))
+        for half in range(2):
+            to = slice(half * half_width, (half + 1) * half_width)
+            down_grad[half] = kept.upstream[:, to].astype(BF16)
+        kept.down_grad_pair = hand_over(down_grad.at[1 - g], their_down)
         exchanged(0)
         far_inputs = unpack_values(recv_blocks.at[0])
         far_column = unpack_extra(recv_blocks.at[0])[:, :1]
@@ -1380,7 +1382,7 @@
         hat = second_hat[...]
         kept.gain_two_sum = jnp.sum(second_grad * hat, axis=0, keepdims=True)
         kept.shift_two_sum = jnp.sum(second_grad, axis=0, keepdims=True)
-        gained = upstream + norm_back(second_grad * kept.gain_two, hat, second_inverse[...])
+        gained = kept.upstream + norm_back(second_grad * kept.gain_two, hat, second_inverse[...])
         middle_grad[...] = gained
         for half in range(2):
             out_grad[half] = gained[:, half * half_width : (half + 1) * half_width].astype(BF16)
@@ -1458,157 +1460,155 @@
         small_parts[g] = small_parts[g] + their_small[...]
         pl.when(s != ways - 1)(lambda: small_home().start())
 
-    early(order[0], late)
-    direct(order[0], late)
+    leave(1, False)
     early(order[0], 1)
     early(order[0], 0)
-    leave(1, False)
+    leave(1, True)
     leave(0, False)
-    leave(1, True)
     turn_piece(order[0], late)
+    turn_piece(order[0], 1)
+    direct(order[0], 1)
     direct(order[0], 0)
-    direct(order[0], 1)
-    turn_piece(order[0], 1)
     enter_plane(order[1], 1)
+    early(order[1], 1)
     turn_piece(order[0], 0)
-    early(order[1], 1)
     enter_plane(order[2], 1)
     enter_plane(order[1], 0)
     early(order[1], 0)
+    early(order[2], 1)
+    late_own()
+    direct(order[1], 1)
+    finish(order[0], late)
+    turn_piece(order[1], 1)
+    norm()
+    direct(order[1], 0)
+    enter_plane(order[2], 0)
+    early(order[2], 0)
+    turn_piece(order[1], 0)
+    finish(order[0], 0)
+    enter_plane(order[3], 1)
+    early(order[3], 1)
+    direct(order[2], 0)
+    turn_piece(order[2], 1)
+    direct(order[2], 1)
     finish(order[0], 1)
-    late_own()
-    turn_piece(order[1], 1)
-    direct(order[1], 1)
-    direct(order[1], 0)
-    norm()
-    enter_plane(order[2], 0)
-    turn_piece(order[1], 0)
-    finish(order[0], late)
-    early(order[2], 0)
-    direct(order[2], 1)
-    enter_plane(order[3], 1)
-    early(order[2], 1)
-    early(order[3], 1)
-    direct(order[3], 1)
     late_on(order[1])
     finish(order[1], 1)
+    leave(0, True)
+    late_on(order[2])
+    turn_piece(order[2], 0)
     finish(order[1], late)
     finish(order[1], 0)
-    leave(0, True)
-    late_on(order[2])
-    turn_piece(order[3], 1)
-    turn_piece(order[2], 1)
-    finish(order[0], 0)
     enter_plane(order[3], 0)
     early(order[3], 0)
+    turn_piece(order[3], 1)
+    direct(order[3], 1)
     project()
-    turn_piece(order[2], 0)
-    direct(order[2], 0)
     attend_far()
     finish(order[2], late)
-    finish(order[3], 1)
     finish(order[2], 1)
+    attend_set(0)
+    finish(order[2], 0)
     direct(order[3], 0)
-    attend_set(0)
     turn_piece(order[3], 0)
     late_on(order[3])
+    finish(order[3], 1)
     finish(order[3], late)
-    finish(order[2], 0)
     mix()
     finish(order[3], 0)
     feed()
     down_weights()
     late_start(3)
+    out_keep(3, 0)
     out_ahead(3, 0)
+    out_ahead(3, 1)
     feed_back()
-    out_ahead(3, 1)
+    mix_back()
+    up_weights()
+    out_ahead(2, 1)
+    late_start(2)
+    out_ahead(2, 0)
+    out_pass(3, 0)
+    attend_set_back(0, near_grad)
+    out_take(3, 0)
+    out_weights()
     out_keep(3, 1)
-    up_weights()
-    out_ahead(2, 0)
-    mix_back()
-    out_ahead(2, 1)
-    out_weights()
     out_ahead(1, 0)
+    late_start(1)
+    out_keep(2, 1)
+    late_relay(3)
     out_pass(3, 1)
-    out_keep(3, 0)
-    attend_set_back(0, near_grad)
     out_keep(2, 0)
-    late_start(2)
-    out_pass(3, 0)
-    late_relay(3)
-    late_start(1)
     out_pass(2, 0)
     out_pass(2, 1)
-    out_keep(2, 1)
     far_back()
     late_relay(2)
+    out_take(3, 1)
+    late_relay(1)
     qkv_weights()
-    late_relay(1)
+    late_start(0)
+    out_ahead(0, 1)
+    late_home(3)
+    out_join(3, 0)
+    out_join(3, 1)
+    out_take(2, 0)
+    out_take(2, 1)
     out_ahead(0, 0)
     out_keep(0, 0)
-    out_take(3, 0)
-    out_take(3, 1)
-    out_ahead(0, 1)
-    out_join(3, 1)
     project_back()
-    out_join(3, 0)
+    out_join(2, 0)
+    out_pass(0, 0)
+    out_keep(0, 1)
+    out_relay(3, 0)
     put_output()
+    out_take(0, 0)
     late_home(2)
-    late_start(0)
-    out_pass(0, 0)
+    out_pass(0, 1)
     out_relay(3, 1)
-    out_take(2, 0)
-    out_keep(0, 1)
-    out_take(2, 1)
-    out_join(2, 0)
-    out_take(0, 0)
-    out_pass(0, 1)
-    out_relay(3, 0)
+    late_home(1)
+    out_relay(2, 0)
+    late_relay(0)
     out_join(2, 1)
+    out_ahead(2, late)
+    out_ahead(1, late)
+    out_keep(1, 0)
+    out_join(0, 0)
+    put_input_grad()
     out_ahead(1, 1)
-    late_home(1)
-    late_home(3)
-    out_keep(1, 0)
-    out_pass(1, 0)
-    out_join(0, 0)
-    out_keep(1, 1)
-    late_relay(0)
-    out_ahead(1, late)
+    out_relay(0, 0)
+    out_pass(1, late)
     out_take(0, 1)
     out_relay(2, 1)
-    out_relay(2, 0)
-    out_relay(0, 0)
+    out_keep(2, late)
+    out_join(0, 1)
+    out_keep(1, late)
+    out_pass(1, 0)
+    out_take(1, 0)
+    out_relay(0, 1)
+    out_keep(1, 1)
+    out_pass(1, 1)
+    small_sums()
+    out_take(1, late)
+    out_ahead(3, late)
     late_home(0)
+    out_join(1, 0)
     out_keep(0, late)
-    out_keep(1, late)
-    out_join(0, 1)
-    out_ahead(2, late)
-    put_input_grad()
+    out_keep(3, late)
     out_ahead(0, late)
-    out_relay(0, 1)
-    out_take(1, late)
-    out_take(1, 0)
-    out_pass(1, late)
-    out_keep(2, late)
-    out_pass(1, 1)
-    out_join(1, 0)
-    small_sums()
+    out_pass(2, late)
+    out_relay(1, 0)
     out_take(1, 1)
+    out_join(1, 1)
+    out_relay(1, 1)
+    out_take(2, late)
+    out_pass(3, late)
+    out_join(2, late)
     out_pass(0, late)
-    out_ahead(3, late)
-    out_relay(1, 0)
-    out_pass(2, late)
-    out_take(2, late)
-    out_keep(3, late)
+    out_join(1, late)
     out_take(0, late)
-    out_join(1, 1)
-    out_pass(3, late)
     out_take(3, late)
     out_join(3, late)
-    out_join(1, late)
     out_join(0, late)
-    out_relay(1, 1)
-    out_join(2, late)
     everything = [(part, piece) for piece in range(PIECES + 1) for part in range(2)]
     out_last(everything[:1])
     settle_first()
@@ -1624,7 +1624,7 @@
     return 5 * D // 2 + FF // 2
 
 
-def run_step(tokens, cotangent, holes, lengths, flat, ways):
+def run_step(tokens, cotangent, holes, lengths, master, ways):
     rows = tokens.shape[0]
     own = MAT_ROWS // ways
     entries = (MAT_ROWS * LANES + bounds_total()) // ways
@@ -1637,6 +1637,8 @@
         ((2, MAT_ROWS, LANES), BF16),
         ((MAT_ROWS, LANES), BF16),
         ((2, SMALL_ROWS, LANES), BF16),
+        ((1, (own + SMALL_ROWS) * LANES), F32),
+        ((1, entries % LANES), F32),
         ((SMALL_ROWS + 184, LANES), F32),
         ((own + SMALL_ROWS, LANES), F32),
         ((SMALL_ROWS, LANES), F32),
@@ -1678,8 +1680,7 @@
         ((planes, 2, PIECES + 1, half_own // PIECES, LANES), BF16),
         ((2, planes, 2, PIECES, half_own // PIECES, LANES), BF16),
         ((2, planes, 2, 4, max(LATE_OUT), LANES), BF16),
-        ((own, LANES), F32),
-        ((own + 2 * SMALL_ROWS, LANES), F32),
+        ((16 * max(TILES), LANES), F32),
         ((SMALL_ROWS, LANES), F32),
         ((ways, SMALL_ROWS, LANES), F32),
     ]
@@ -1688,15 +1689,16 @@
         out_shape=(
             jax.ShapeDtypeStruct((rows, D), BF16),
             jax.ShapeDtypeStruct((rows, D), F32),
-            jax.ShapeDtypeStruct((-(-entries // (8 * LANES)) * 8, LANES), F32),
+            jax.ShapeDtypeStruct((own, LANES), F32),
+            jax.ShapeDtypeStruct((SMALL_ROWS, LANES), F32),
         ),
         in_specs=[
-            vmem, vmem, vmem, pl.BlockSpec(memory_space=pltpu.SMEM), vmem,
+            vmem, vmem, vmem, pl.BlockSpec(memory_space=pltpu.SMEM), pl.BlockSpec(memory_space=pl.ANY),
         ],
-        out_specs=(vmem,) * 3,
+        out_specs=(vmem,) * 4,
         scratch_shapes=[pltpu.VMEM(*shape) for shape in shapes]
         + [
-            dma((2,)),
+            dma((2,)), dma((2,)),
             dma((2, planes, 5, PIECES + 1)), dma((2, ways, PIECES + 1)),
             dma((2, planes, 2)), dma((planes, 2)),
             dma((planes, 2, PIECES + 1)), dma((planes, 2, PIECES + 1)),
@@ -1712,45 +1714,32 @@
             collective_id=1, has_side_effects=True, vmem_limit_bytes=VMEM_BYTES
         ),
         name="run_step",
-    )(tokens, cotangent, holes, lengths, flat)
-
-
-def rows_kernel(entries, flat, last, sems):
-    full, rest = divmod(entries.shape[1], LANES)
-    bulk = pltpu.make_async_copy(
-        entries.at[:, pl.ds(0, full * LANES)].reshape(full, LANES), flat.at[pl.ds(0, full)], sems.at[0]
-    )
-    end = pltpu.make_async_copy(entries.at[:, pl.ds(full * LANES, rest)], last, sems.at[1])
-    bulk.start()
-    end.start()
-    bulk.wait()
-    end.wait()
-    flat[full:, :] = jnp.zeros((flat.shape[0] - full, LANES), F32)
-    flat[full : full + 1, :rest] = last[...]
-
-
-def to_rows(entries, rows):
-    size = entries.shape[1]
-    return pl.pallas_call(
-        rows_kernel,
-        out_shape=jax.ShapeDtypeStruct((rows, LANES), F32),
-        in_specs=[pl.BlockSpec(memory_space=pl.ANY)],
-        out_specs=pl.BlockSpec(memory_space=pltpu.VMEM),
-        scratch_shapes=[pltpu.VMEM((1, size % LANES), F32), pltpu.SemaphoreType.DMA((2,))],
-        name="to_rows",
-    )(entries)
+    )(tokens, cotangent, holes, lengths, master)
+
+
+def rates_at(at):
+    values = (
+        0.7 * (2.0 / D) ** 0.5, 0.7 * (24.0 / D) ** 0.5, 0.7 * (1.0 / D) ** 0.5, 0.7 * (1.0 / FF) ** 0.5,
+        0.15, 0.2,
+    )
+    rates = values[5]
+    for edge, value in reversed(list(zip(bounds(), values))):
+        rates = jnp.where(at < edge, jnp.float32(value), rates)
+    return rates, jnp.where(at < bounds()[3], jnp.float32(0.1), jnp.float32(0.0))
 
 
 def adam_kernel(
-    gradient, master, first_moment, second_moment, layer_output, layer_grad,
+    tiled, after_rows, master, first_moment, second_moment, layer_output, layer_grad,
     new_moment, new_second, new_master, output, input_grad, kept, last, kept_output, kept_grad,
-    load_sem, store_sem, pass_sem,
+    kept_tiled, laid, load_sem, store_sem, pass_sem, grad_sem,
 ):
     size = master.shape[1]
     full, rest = divmod(size, LANES)
-    chunks, step = 3, 56
-    chunk = -(-full // (step * chunks)) * step
-    spans = [(c * chunk, min(chunk, full - c * chunk)) for c in range(chunks)]
+    own, step = tiled.shape[0], 56
+    chunks = own // UNIT
+    edges = [(UNIT * c - SMALL_ROWS) // step * step for c in range(1, chunks)]
+    edges = [0] + edges + [full]
+    spans = [(first, end - first) for first, end in zip(edges, edges[1:])]
     sources, targets = (first_moment, second_moment, master), (new_moment, new_second, new_master)
 
     def piece(array, first, count):
@@ -1758,11 +1747,6 @@
 
     def load(which, index):
         first, count = spans[index]
-        if which == 3:
-            span = pl.ds(first, -(-count // step) * step)
-            return pltpu.make_async_copy(
-                gradient.at[span], kept.at[3, span], load_sem.at[3, index]
-            )
         return pltpu.make_async_copy(
             piece(sources[which], first, count), kept.at[which, pl.ds(first, count)],
             load_sem.at[which, index],
@@ -1794,33 +1778,84 @@
             ((layer_output, kept_output, output), (layer_grad, kept_grad, input_grad))
         )
     )
+    after = pltpu.make_async_copy(
+        after_rows, laid.at[pl.ds(own, SMALL_ROWS)], grad_sem.at[chunks]
+    )
+
+    def unit_in(unit):
+        span = pl.ds(unit * UNIT, UNIT)
+        return pltpu.make_async_copy(tiled.at[span], kept_tiled.at[span], grad_sem.at[unit])
+
     for index in range(chunks):
-        for which in range(4):
+        unit_in(index).start()
+        for which in range(3):
             load(which, index).start()
+    after.start()
     for which in range(3):
         load_last(which).start()
     for copy, _ in passed:
         copy.start()
-    origin = lax.axis_index("seq") * size
-
-    def update(first, count, moment, second, weights, gradients):
-        at = (
-            origin
-            + (first + lax.broadcasted_iota(jnp.int32, (count, LANES), 0)) * LANES
-            + lax.broadcasted_iota(jnp.int32, (count, LANES), 1)
-        )
-        return adam_update(weights, moment, second, gradients, at)
+    s = lax.axis_index("seq")
+    origin = s * size
+    shift = s * (size - own * LANES)
+    row_shift, lane_shift = shift // LANES, lax.rem(shift, LANES)
+    back = lax.rem(LANES - lane_shift, LANES)
+
+    def gradients(first, count):
+        here = laid[pl.ds(first + row_shift, count), :]
+        after = laid[pl.ds(first + row_shift + 1, count), :]
+        lanes = lax.broadcasted_iota(jnp.int32, (count, LANES), 1)
+        return jnp.where(lanes < LANES - lane_shift, here, after)
+
+
+    def update(at, moment, second, weights, gradient):
+        rates, decays = rates_at(at)
+        moment = BETA_ONE * moment + (1.0 - BETA_ONE) * gradient
+        second = BETA_TWO * second + (1.0 - BETA_TWO) * gradient * gradient
+        scaled = moment * (1.0 / (1.0 - BETA_ONE**STEP))
+        change = scaled / (jnp.sqrt(second * (1.0 / (1.0 - BETA_TWO**STEP))) + EPS_ADAM)
+        return moment, second, weights - rates * (change + decays * weights)
+
+    laid[own + SMALL_ROWS :, :] = jnp.zeros((laid.shape[0] - own - SMALL_ROWS, LANES), F32)
+
+    def lay(unit):
+        def groups(count):
+            for group in range(UNIT // (16 * count)):
+                lay_group(kept_tiled, laid, unit * UNIT, group, count, back)
+
+        unit_tiles(s * (own // UNIT) + unit, groups)
 
     for index, (first, count) in enumerate(spans):
-        for which in range(4):
+        unit_in(index).wait()
+        lay(index)
+        if index == chunks - 1:
+            after.wait()
+            laid[own : own + SMALL_ROWS, :] = pltpu.roll(laid[own : own + SMALL_ROWS, :], back, 1)
+        for which in range(3):
             load(which, index).wait()
 
-        def run(at, carry, first=first):
-            where = pl.multiple_of(first + at * step, 8)
+        def run(index, carry, first=first):
+            where = pl.multiple_of(first + index * step, 8)
             span = pl.ds(where, step)
-            found = update(where, step, *(kept[which, span, :] for which in range(4)))
-            for which in range(3):
-                kept[which, span, :] = found[which]
+            start = origin + where * LANES
+            end = start + step * LANES - 1
+            edge_list = bounds()
+            cut = (start < edge_list[0]) & (end >= edge_list[0])
+            for edge in edge_list[1:]:
+                cut = cut | ((start < edge) & (end >= edge))
+
+            def put(at):
+                found = update(at, *(kept[which, span, :] for which in range(3)), gradients(where, step))
+                for which in range(3):
+                    kept[which, span, :] = found[which]
+
+            pl.when(jnp.logical_not(cut))(lambda: put(start))
+
+            @pl.when(cut)
+            def _():
+                row = lax.broadcasted_iota(jnp.int32, (step, LANES), 0)
+                put(start + row * LANES + lax.broadcasted_iota(jnp.int32, (step, LANES), 1))
+
             return carry
 
         lax.fori_loop(0, -(-count // step), run, 0)
@@ -1834,7 +1869,7 @@
         load_last(which).wait()
     moment, second, weights = (last[which] for which in range(3))
     at = origin + full * LANES + lax.broadcasted_iota(jnp.int32, (1, rest), 1)
-    found = adam_update(weights, moment, second, kept[3, full : full + 1, :rest], at)
+    found = update(at, moment, second, weights, gradients(full, 8)[:1, :rest])
     for which in range(3):
         last[which] = found[which]
         store_last(which).start()
@@ -1846,35 +1881,39 @@
         copy.wait()
 
 
-def run_adam(gradient, master, first_moment, second_moment, layer_output, layer_grad):
+def run_adam(tiled, after_rows, master, first_moment, second_moment, layer_output, layer_grad):
     size = master.shape[1]
     anywhere = pl.BlockSpec(memory_space=pl.ANY)
     return pl.pallas_call(
         adam_kernel,
         out_shape=(jax.ShapeDtypeStruct((1, size), F32),) * 3
         + tuple(jax.ShapeDtypeStruct(one.shape, one.dtype) for one in (layer_output, layer_grad)),
-        in_specs=[anywhere] * 6,
+        in_specs=[anywhere] * 7,
         out_specs=(anywhere,) * 5,
         scratch_shapes=[
-            pltpu.VMEM((4,) + gradient.shape, F32),
+            pltpu.VMEM((3, -(-size // (8 * LANES)) * 8, LANES), F32),
             pltpu.VMEM((3, 1, size % LANES), F32),
             pltpu.VMEM(layer_output.shape, layer_output.dtype),
             pltpu.VMEM(layer_grad.shape, layer_grad.dtype),
-            pltpu.SemaphoreType.DMA((4, 5)),
-            pltpu.SemaphoreType.DMA((3, 5)),
+            pltpu.VMEM(tiled.shape, F32),
+            pltpu.VMEM((tiled.shape[0] + 2 * SMALL_ROWS, LANES), F32),
+            pltpu.SemaphoreType.DMA((3, tiled.shape[0] // UNIT + 1)),
+            pltpu.SemaphoreType.DMA((3, tiled.shape[0] // UNIT + 1)),
             pltpu.SemaphoreType.DMA((2,)),
+            pltpu.SemaphoreType.DMA((tiled.shape[0] // UNIT + 1,)),
         ],
         compiler_params=pltpu.CompilerParams(vmem_limit_bytes=VMEM_BYTES),
         name="run_adam",
-    )(gradient, master, first_moment, second_moment, layer_output, layer_grad)
+    )(tiled, after_rows, master, first_moment, second_moment, layer_output, layer_grad)
 
 
 def on_device(tokens, cotangent, holes, slide_lengths, master, first_moment, second_moment):
     ways = lax.axis_size("seq")
-    flat = to_rows(master, MAT_ROWS // ways + SMALL_ROWS)
-    output, input_grad, gradient = run_step(tokens[0], cotangent[0], holes, slide_lengths, flat, ways)
+    output, input_grad, tiled, after_rows = run_step(
+        tokens[0], cotangent[0], holes, slide_lengths, master, ways
+    )
     new_moment, new_second, new_master, output, input_grad = run_adam(
-        gradient, master, first_moment, second_moment, output, input_grad
+        tiled, after_rows, master, first_moment, second_moment, output, input_grad
     )
     return (output[None], input_grad[None], new_moment, new_second, new_master)
 

time: 157 us -> 150 us (0.955)
  the two profiles are of different devices: /device:TPU:8 before, /device:TPU:0 now
where the time goes in v5:
time: 150 us
  Pallas kernels  149 us (99%)
    pallas_call x1, Pallas kernels, run_step(): pl.pallas_call(partial(step_kernel, ways), out_shape=(jax.ShapeDtypeStruc...  144 us
    pallas_call x1, Pallas kernels, run_adam(): pl.pallas_call(adam_kernel, out_shape=(jax.ShapeDtypeStruct((1, size), F3...  5.08 us

profile of v5, /device:TPU:0, one launch (start us, length us, event | category | flops | bytes accessed | tf_op | source)
XLA Modules:
  0.0 150.2 jit_solution(3453346761398741145)
XLA Ops:
  0.6 144.3 %run_step.1 = (bf16[128,768]{1,0:T(8,128)(2,1)}, f32[128,768]{1,0:T(8,128)}, f32[1728,128]{1,0:T(8,128)}, f32[32,128]{1,0:T(8,128)}) custom-call(bf16[128,768]{1,0:T(8,128)(2,1)} %bitcast.4, bf16[128,768]{1,0:T(8,128)(2,1)} %bitcast.5, s32[1,128]{1,0:T(1,128)} %holes.1, s32[1,8]{1,0:T(1,128)} %lengths.1, f32[1,221400]{1,0:T(1,128)} %master.3), custom_call_target="tpu_custom_call" | custom-call | tf_op jit(solution)/shard_map/run_step/pallas_call | solution.py:1687
  144.9 5.1 %run_adam.1 = (f32[1,221400]{1,0:T(1,128)}, f32[1,221400]{1,0:T(1,128)}, f32[1,221400]{1,0:T(1,128)}, bf16[128,768]{1,0:T(8,128)(2,1)}, f32[128,768]{1,0:T(8,128)}) custom-call(f32[1728,128]{1,0:T(8,128)} %get-tuple-element.14.tiled, f32[32,128]{1,0:T(8,128)} %get-tuple-element.15.after_rows, f32[1,221400]{1,0:T(1,128)} %master.3, f32[1,221400]{1,0:T(1,128)} %first_moment.1, ...), custom_call_target="tpu_custom_call" | custom-call | tf_op jit(solution)/shard_map/run_adam/pallas_call | solution.py:1887

commit v6 on v5

--- a/solution.py
+++ b/solution.py
@@ -573,6 +573,7 @@
     whole, grads, small, entries_here, entries_end, extended, aligned, tail,
     turning, send_blocks, recv_blocks, masks, normed, normed_hat, inverse, projected, attended, lses,
     mixture, second_in, activated, slope, second_hat, second_inverse, middle_grad,
+    normed_t, mixture_t, second_t, activated_t,
     qkv_grad, out_grad, up_grad, down_grad, near_grad, far_grad, lse_grads,
     their_normed, their_mixture, their_second, their_activated,
     their_qkv, their_out, their_up, their_down, small_parts, their_small,
@@ -1190,21 +1191,24 @@
         found = jnp.where(masks[which] > 0.5, dot_cols(query, key) * temper, NEG)
         return query, key, value, found
 
-    def attend_set(which):
+    def attend_set(which, part):
+        first = part * HEADS // 2
         results, totals = [], []
-        for head in range(HEADS):
+        for head in range(first, first + HEADS // 2):
             _, _, value, found = scores(which, head)
             top = jnp.max(found, axis=1, keepdims=True)
             weights = jnp.exp(found - top)
             summed = jnp.sum(weights, axis=1, keepdims=True)
             results.append(dot(weights.astype(BF16), value) * (1.0 / summed))
             totals.append(top + jnp.log(summed))
-        attended[which] = jnp.concatenate(results, axis=1)
-        lses[which] = jnp.concatenate(totals, axis=1)
-
-    def attend_set_back(which, out_grads):
+        to = slice(part * half_width, (part + 1) * half_width)
+        attended[which, :, to] = jnp.concatenate(results, axis=1)
+        lses[which, :, first : first + HEADS // 2] = jnp.concatenate(totals, axis=1)
+
+    def attend_set_back(which, out_grads, part):
+        first = part * HEADS // 2
         lists = ([], [], [])
-        for head in range(HEADS):
+        for head in range(first, first + HEADS // 2):
             query, key, value, found = scores(which, head)
             weights = jnp.exp(found - lses[which, :, head : head + 1])
             pulled = out_grads[:, head * HEAD : (head + 1) * HEAD]
@@ -1216,22 +1220,20 @@
             lists[1].append(dot_rows(score_grad, query) * temper)
             lists[2].append(dot_rows(weights.astype(BF16), pulled))
         at = slice(which * rows, (which + 1) * rows)
-        query_grad, key_grad, value_grad = (jnp.concatenate(one, axis=1).astype(BF16) for one in lists)
-        qkv_grad[0, at, :D] = query_grad
-        qkv_grad[0, at, D:] = key_grad[:, :half_width]
-        qkv_grad[1, at, :half_width] = key_grad[:, half_width:]
-        qkv_grad[1, at, half_width:] = value_grad
+        for index, one in enumerate(lists):
+            half, start = divmod(index * D + part * half_width, 3 * half_width)
+            qkv_grad[half, at, start : start + half_width] = jnp.concatenate(one, axis=1).astype(BF16)
 
     def weight_grad(index, mine, theirs, grad, their_grad, first, count):
         left = jnp.concatenate(
-            [mine[:, first : first + count], theirs[:, first : first + count]], axis=0
+            [mine[first : first + count, :], theirs[first : first + count, :]], axis=1
         )
         view, base = tile_view(grads, index)
         at = base + first // 16
         for tile, width in tile_groups(index):
             to = slice(tile * LANES, (tile + width) * LANES)
             right = jnp.concatenate([grad[g, :, to], their_grad[:, to]], axis=0)
-            found = dot_rows(left, right).astype(BF16)
+            found = dot(left, right).astype(BF16)
             for t in range(width):
                 view[at : at + count // 16, 16 * (tile + t) : 16 * (tile + t) + 16, :] = found[
                     :, t * LANES : (t + 1) * LANES
@@ -1284,10 +1286,12 @@
         kept.shift_one, kept.shift_two = small_row(2 * count, count), small_row(3 * count, count)
         kept.shift_down = small_row(4 * count, count)
         kept.bias_up = small_row(5 * count, FF // 2 // LANES)
-        normed[...] = (hat * kept.gain_one + kept.shift_one).astype(BF16)
+        both = hat * kept.gain_one + kept.shift_one
+        normed[...] = both.astype(BF16)
+        normed_t[...] = both.T.astype(BF16)
         normed_hat[...] = hat[:rows]
         inverse[...] = scale[:rows]
-        kept.normed_pair = hand_over(normed, their_normed)
+        kept.normed_pair = hand_over(normed_t, their_normed)
 
     def project():
         arrived(0)
@@ -1299,7 +1303,8 @@
                 ).astype(BF16)
 
     def attend_far():
-        attend_set(1)
+        attend_set(1, 0)
+        attend_set(1, 1)
         pack_blocks(send_blocks.at[1], attended[1], lses[1])
         exchange(1)
 
@@ -1310,8 +1315,10 @@
         kept.share = jax.nn.sigmoid(lses[0] - unpack_extra(recv_blocks.at[1]))
         kept.shares = to_columns(kept.share)
         kept.difference = near_out - far_out
-        mixture[...] = (kept.shares * near_out + (1.0 - kept.shares) * far_out).astype(BF16)
-        kept.mixture_pair = hand_over(mixture, their_mixture)
+        mixed = kept.shares * near_out + (1.0 - kept.shares) * far_out
+        mixture[...] = mixed.astype(BF16)
+        mixture_t[...] = mixed.T.astype(BF16)
+        kept.mixture_pair = hand_over(mixture_t, their_mixture)
 
     def feed():
         arrived(1)
@@ -1323,9 +1330,10 @@
         hat, scale = normalize(kept.middle)
         second_hat[...] = hat
         second_inverse[...] = scale
-        second_in[...] = (hat * kept.gain_two + kept.shift_two).astype(BF16)
-        kept.second_in_pair = hand_over(second_in, their_second)
+        second = hat * kept.gain_two + kept.shift_two
+        second_in[...] = second.astype(BF16)
         root = (2.0 / 3.141592653589793) ** 0.5
+        kept.activated_pairs = []
         for half in range(2):
             for tile, width in tile_groups(2):
                 at = half * FF // 2 + tile * LANES
@@ -1334,11 +1342,19 @@
                 v = v + kept.bias_up[:, to]
                 square = v * v
                 t = jnp.tanh(root * (v + 0.044715 * v * square))
-                activated[:, to] = (0.5 * v * (1.0 + t)).astype(BF16)
+                active = 0.5 * v * (1.0 + t)
+                activated[:, to] = active.astype(BF16)
+                activated_t[to, :] = active.T.astype(BF16)
                 slope[:, to] = 0.5 * (1.0 + t) + 0.5 * v * (1.0 - t * t) * (
                     root * (1.0 + 3 * 0.044715 * square)
                 )
-        kept.activated_pair = hand_over(activated, their_activated)
+                if (at + width * LANES) % D == 0:
+                    span = pl.ds(at + width * LANES - D, D)
+                    kept.activated_pairs.append(
+                        hand_over(activated_t.at[span], their_activated.at[span])
+                    )
+        second_t[...] = second.T.astype(BF16)
+        kept.second_in_pair = hand_over(second_t, their_second)
 
     block = 256
 
@@ -1361,9 +1377,9 @@
 
     def down_weights():
         kept.down_grad_pair.wait()
-        kept.activated_pair.wait()
         for first in range(0, FF, D):
-            weight_grad(3, activated, their_activated, down_grad, their_down, first, D)
+            kept.activated_pairs[first // D].wait()
+            weight_grad(3, activated_t, their_activated, down_grad, their_down, first, D)
 
     def through(left, index, tiles_to):
         return jnp.concatenate(
@@ -1398,12 +1414,12 @@
     def up_weights():
         kept.second_in_pair.wait()
         kept.up_grad_pair.wait()
-        weight_grad(2, second_in, their_second, up_grad, their_up, 0, D)
+        weight_grad(2, second_t, their_second, up_grad, their_up, 0, D)
 
     def out_weights():
         kept.mixture_pair.wait()
         kept.out_grad_pair.wait()
-        weight_grad(1, mixture, their_mixture, out_grad, their_out, 0, D)
+        weight_grad(1, mixture_t, their_mixture, out_grad, their_out, 0, D)
 
     def put_output():
         result = kept.middle + kept.shift_down + jnp.concatenate(
@@ -1415,12 +1431,20 @@
         )
         output[...] = in_order(result).astype(BF16)
 
-    def far_back():
+    def far_back_start():
+        kept.qkv_near_pair = hand_over(
+            qkv_grad.at[1 - g, pl.ds(0, rows)], their_qkv.at[pl.ds(0, rows)]
+        )
         exchanged(2)
         far_grad[...] = unpack_values(recv_blocks.at[2]).astype(BF16)
         lse_grads[1] = unpack_extra(recv_blocks.at[2])
-        attend_set_back(1, far_grad)
-        kept.qkv_grad_pair = hand_over(qkv_grad.at[1 - g], their_qkv)
+        attend_set_back(1, far_grad, 0)
+
+    def far_back():
+        attend_set_back(1, far_grad, 1)
+        kept.qkv_far_pair = hand_over(
+            qkv_grad.at[1 - g, pl.ds(rows, rows)], their_qkv.at[pl.ds(rows, rows)]
+        )
 
     def project_back():
         kept.first_grad = through(qkv_grad, 0, TILES[0])
@@ -1429,8 +1453,9 @@
 
     def qkv_weights():
         kept.normed_pair.wait()
-        kept.qkv_grad_pair.wait()
-        weight_grad(0, normed, their_normed, qkv_grad, their_qkv, 0, D)
+        kept.qkv_near_pair.wait()
+        kept.qkv_far_pair.wait()
+        weight_grad(0, normed_t, their_normed, qkv_grad, their_qkv, 0, D)
 
     def put_input_grad():
         exchanged(3)
@@ -1460,6 +1485,7 @@
         small_parts[g] = small_parts[g] + their_small[...]
         pl.when(s != ways - 1)(lambda: small_home().start())
 
+    everything = [(part, piece) for piece in range(PIECES + 1) for part in range(2)]
     leave(1, False)
     early(order[0], 1)
     early(order[0], 0)
@@ -1507,7 +1533,8 @@
     attend_far()
     finish(order[2], late)
     finish(order[2], 1)
-    attend_set(0)
+    attend_set(0, 0)
+    attend_set(0, 1)
     finish(order[2], 0)
     direct(order[3], 0)
     turn_piece(order[3], 0)
@@ -1529,7 +1556,8 @@
     late_start(2)
     out_ahead(2, 0)
     out_pass(3, 0)
-    attend_set_back(0, near_grad)
+    attend_set_back(0, near_grad, 0)
+    attend_set_back(0, near_grad, 1)
     out_take(3, 0)
     out_weights()
     out_keep(3, 1)
@@ -1541,6 +1569,7 @@
     out_keep(2, 0)
     out_pass(2, 0)
     out_pass(2, 1)
+    far_back_start()
     far_back()
     late_relay(2)
     out_take(3, 1)
@@ -1573,7 +1602,6 @@
     out_ahead(1, late)
     out_keep(1, 0)
     out_join(0, 0)
-    put_input_grad()
     out_ahead(1, 1)
     out_relay(0, 0)
     out_pass(1, late)
@@ -1585,6 +1613,7 @@
     out_pass(1, 0)
     out_take(1, 0)
     out_relay(0, 1)
+    put_input_grad()
     out_keep(1, 1)
     out_pass(1, 1)
     small_sums()
@@ -1597,6 +1626,8 @@
     out_ahead(0, late)
     out_pass(2, late)
     out_relay(1, 0)
+    out_last(everything[:1])
+    settle_first()
     out_take(1, 1)
     out_join(1, 1)
     out_relay(1, 1)
@@ -1609,9 +1640,6 @@
     out_take(3, late)
     out_join(3, late)
     out_join(0, late)
-    everything = [(part, piece) for piece in range(PIECES + 1) for part in range(2)]
-    out_last(everything[:1])
-    settle_first()
     out_last(everything[1:])
     settle()
     pl.when(s != ways - 1)(lambda: small_home().wait_send())
@@ -1633,6 +1661,7 @@
     vmem = pl.BlockSpec(memory_space=pltpu.VMEM)
     dma = pltpu.SemaphoreType.DMA
     half = D // 2
+    most = max((half_own - min(LATE_OUT)) // PIECES, max(LATE_OUT))
     shapes = [
         ((2, MAT_ROWS, LANES), BF16),
         ((MAT_ROWS, LANES), BF16),
@@ -1659,6 +1688,10 @@
         ((rows, D), F32),
         ((rows, 1), F32),
         ((rows, D), F32),
+        ((D, 2 * rows), BF16),
+        ((D, rows), BF16),
+        ((D, rows), BF16),
+        ((FF, rows), BF16),
         ((2, 2 * rows, 3 * half), BF16),
         ((2, rows, half), BF16),
         ((2, rows, FF // 2), BF16),
@@ -1666,19 +1699,19 @@
         ((rows, D), BF16),
         ((rows, D), BF16),
         ((2, rows, HEADS), F32),
-        ((2 * rows, D), BF16),
-        ((rows, D), BF16),
-        ((rows, D), BF16),
-        ((rows, FF), BF16),
+        ((D, 2 * rows), BF16),
+        ((D, rows), BF16),
+        ((D, rows), BF16),
+        ((FF, rows), BF16),
         ((2 * rows, 3 * half), BF16),
         ((rows, half), BF16),
         ((rows, FF // 2), BF16),
         ((rows, half), BF16),
         ((2, SMALL_ROWS, LANES), F32),
         ((SMALL_ROWS, LANES), F32),
-        ((planes, 2, 2, PIECES + 1, half_own // PIECES, LANES), BF16),
-        ((planes, 2, PIECES + 1, half_own // PIECES, LANES), BF16),
-        ((2, planes, 2, PIECES, half_own // PIECES, LANES), BF16),
+        ((planes, 2, 2, PIECES + 1, most, LANES), BF16),
+        ((planes, 2, PIECES + 1, most, LANES), BF16),
+        ((2, planes, 2, PIECES, most, LANES), BF16),
         ((2, planes, 2, 4, max(LATE_OUT), LANES), BF16),
         ((16 * max(TILES), LANES), F32),
         ((SMALL_ROWS, LANES), F32),
@@ -1703,7 +1736,7 @@
             dma((2, planes, 2)), dma((planes, 2)),
             dma((planes, 2, PIECES + 1)), dma((planes, 2, PIECES + 1)),
             dma((ways,)), dma((2,)),
-            dma((4,)), dma((4,)), dma((9,)), dma((9,)),
+            dma((4,)), dma((4,)), dma((13,)), dma((13,)),
             dma((planes, 2, 2, PIECES + 1)), dma((planes, 2, 2, PIECES + 1)),
             dma((planes, 2, PIECES + 1)), dma((planes, 2, PIECES + 1)),
             dma((planes, 2, PIECES)), dma((2, planes, 2, PIECES)),

time: 150 us -> 148 us (0.987); the launches traced: 150 us -> 146 us
  Pallas kernels: 149 us -> 146 us
    pallas_call x1, Pallas kernels: 144 us -> 140 us  [run_step(): pl.pallas_call(partial(step_kernel, ways), out_shape=(jax.ShapeDtypeStruc...]
where the time goes in v6:
time: 148 us; the launch traced here: 146 us
  Pallas kernels  146 us (99%)
    pallas_call x1, Pallas kernels, run_step(): pl.pallas_call(partial(step_kernel, ways), out_shape=(jax.ShapeDtypeStruc...  140 us
    pallas_call x1, Pallas kernels, run_adam(): pl.pallas_call(adam_kernel, out_shape=(jax.ShapeDtypeStruct((1, size), F3...  5.08 us

profile of v6, /device:TPU:0, one launch (start us, length us, event | category | flops | bytes accessed | tf_op | source)
XLA Modules:
  0.0 146.4 jit_solution(13306526595234604669)
XLA Ops:
  0.6 140.5 %run_step.1 = (bf16[128,768]{1,0:T(8,128)(2,1)}, f32[128,768]{1,0:T(8,128)}, f32[1728,128]{1,0:T(8,128)}, f32[32,128]{1,0:T(8,128)}) custom-call(bf16[128,768]{1,0:T(8,128)(2,1)} %bitcast.4, bf16[128,768]{1,0:T(8,128)(2,1)} %bitcast.5, s32[1,128]{1,0:T(1,128)} %holes.1, s32[1,8]{1,0:T(1,128)} %lengths.1, f32[1,221400]{1,0:T(1,128)} %master.3), custom_call_target="tpu_custom_call" | custom-call | tf_op jit(solution)/shard_map/run_step/pallas_call | solution.py:1720
  141.1 5.1 %run_adam.1 = (f32[1,221400]{1,0:T(1,128)}, f32[1,221400]{1,0:T(1,128)}, f32[1,221400]{1,0:T(1,128)}, bf16[128,768]{1,0:T(8,128)(2,1)}, f32[128,768]{1,0:T(8,128)}) custom-call(f32[1728,128]{1,0:T(8,128)} %get-tuple-element.14.tiled, f32[32,128]{1,0:T(8,128)} %get-tuple-element.15.after_rows, f32[1,221400]{1,0:T(1,128)} %master.3, f32[1,221400]{1,0:T(1,128)} %first_moment.1, ...), custom_call_target="tpu_custom_call" | custom-call | tf_op jit(solution)/shard_map/run_adam/pallas_call | solution.py:1920

commit v7 on v6

--- a/solution.py
+++ b/solution.py
@@ -1123,7 +1123,8 @@
         width = widths[index]
 
         def start(step, carry):
-            to = lax.rem(s + step, ways)
+            apart = ways // 2 + (step // 2) * (1 - 2 * lax.rem(step, 2))
+            to = lax.rem(s + apart, ways)
             remote(
                 send_blocks.at[index, to, :, pl.ds(0, width)],
                 recv_blocks.at[index, s, :, pl.ds(0, width)],

time: 148 us -> 148 us (level)
  no operation moved by 1% of the time
where the time goes in v7:
time: 148 us; the launch traced here: 147 us
  Pallas kernels  146 us (99%)
    pallas_call x1, Pallas kernels, run_step(): pl.pallas_call(partial(step_kernel, ways), out_shape=(jax.ShapeDtypeStruc...  141 us
    pallas_call x1, Pallas kernels, run_adam(): pl.pallas_call(adam_kernel, out_shape=(jax.ShapeDtypeStruct((1, size), F3...  5.08 us

profile of v7, /device:TPU:0, one launch (start us, length us, event | category | flops | bytes accessed | tf_op | source)
XLA Modules:
  0.0 146.8 jit_solution(8977766205060824596)
XLA Ops:
  0.6 140.9 %run_step.1 = (bf16[128,768]{1,0:T(8,128)(2,1)}, f32[128,768]{1,0:T(8,128)}, f32[1728,128]{1,0:T(8,128)}, f32[32,128]{1,0:T(8,128)}) custom-call(bf16[128,768]{1,0:T(8,128)(2,1)} %bitcast.4, bf16[128,768]{1,0:T(8,128)(2,1)} %bitcast.5, s32[1,128]{1,0:T(1,128)} %holes.1, s32[1,8]{1,0:T(1,128)} %lengths.1, f32[1,221400]{1,0:T(1,128)} %master.3), custom_call_target="tpu_custom_call" | custom-call | tf_op jit(solution)/shard_map/run_step/pallas_call | solution.py:1721
  141.5 5.1 %run_adam.1 = (f32[1,221400]{1,0:T(1,128)}, f32[1,221400]{1,0:T(1,128)}, f32[1,221400]{1,0:T(1,128)}, bf16[128,768]{1,0:T(8,128)(2,1)}, f32[128,768]{1,0:T(8,128)}) custom-call(f32[1728,128]{1,0:T(8,128)} %get-tuple-element.14.tiled, f32[32,128]{1,0:T(8,128)} %get-tuple-element.15.after_rows, f32[1,221400]{1,0:T(1,128)} %master.3, f32[1,221400]{1,0:T(1,128)} %first_moment.1, ...), custom_call_target="tpu_custom_call" | custom-call | tf_op jit(solution)/shard_map/run_adam/pallas_call | solution.py:1921
